TPU v7x, 128 devices: a whole 4x4x4 slice. The times are simulated.
128 devices in a mesh: ctx: 16 (over x_lo, z, core), exp: 8 (over y, x_hi).
Axes of the slice: x: 4 (x_hi: 2, x_lo: 2; x = x_hi * 2 + x_lo), y: 4, z: 4, core: 2. Of those that a mesh axis runs over, the one named last changes fastest.
Arguments:
- stream: bfloat16 [16384, 2048], P(('ctx', 'exp')), may hold values from -4 to 4
- queries: bfloat16 [16384, 2048], P('ctx', 'exp'), may hold values from -108 to 108
- keys: bfloat16 [16384, 512], P('ctx'), may hold values from -4.5 to 4.5
- values: bfloat16 [16384, 512], P('ctx'), may hold values from -5 to 5
- out_proj: bfloat16 [2048, 2048], P('exp'), may hold values from -0.59765625 to 0.59765625
- norm_gain: bfloat16 [2048], replicated, may hold values from 0.099609375 to 1.8984375
- gate_proj: bfloat16 [128, 2048, 768], P(('ctx', 'exp')), may hold values from -0.125 to 0.125
- up_proj: bfloat16 [128, 2048, 768], P(('ctx', 'exp')), may hold values from -0.125 to 0.125
- down_proj: bfloat16 [128, 768, 2048], P(('ctx', 'exp')), may hold values from -0.21875 to 0.21875
- expert_ids: int32 [16384, 8], P(('ctx', 'exp')), may hold values from 0 to 127, all different within a row; in each aligned block of 128 rows (0 to 127, 128 to 255, ...) at most 9 rows name the same one
- route_weights: float32 [16384, 8], P(('ctx', 'exp')), may hold values from 0.02 to 1
- segment_lengths: int32 [17], replicated, may hold values from 1 to 8192, 16384 in all
Outputs:
- mixed: bfloat16 [16384, 2048], P(('ctx', 'exp'))
Inputs may be any that keep to these rules, and one draw needn't show every extreme that they name: `expert_ids`: each position names 8 different experts; among the 128 positions of one device no expert is named more than 9 times, a bound that some block reaches. `segment_lengths`: they sum to 16384.
All inputs are finite; a program needn't handle non-finite values.
Results may differ from a plain program's by a relative error of at most 0.023.
Values may be sent and summed in bfloat16 or wider, within the bound.
No kernel may reach another device: no remote copies, remote signals or barrier semaphores. Data moves between devices by JAX's collectives and lax.ppermute only.
A program may use at most 128 MiB of HBM per device.

v0:
```python
import math

import jax
import jax.numpy as jnp
from jax import lax
from jax.sharding import PartitionSpec as P

HD = 128
KVH = 4
HQ = 16


def segment_of(positions, ends):
    return jnp.sum((positions[:, None] >= ends[None, :]).astype(jnp.int32), axis=1)


def expert_rows(rows, weight_gate, weight_up, weight_down):
    gate = jnp.dot(rows, weight_gate, preferred_element_type=jnp.float32)
    upper = jnp.dot(rows, weight_up, preferred_element_type=jnp.float32)
    hidden = (jax.nn.silu(gate) * upper).astype(jnp.bfloat16)
    return jnp.dot(hidden, weight_down, preferred_element_type=jnp.float32).astype(jnp.bfloat16)


def on_device(
    stream,
    queries,
    keys,
    values,
    out_proj,
    norm_gain,
    gate_proj,
    up_proj,
    down_proj,
    expert_ids,
    route_weights,
    segment_lengths,
):
    ctx_count = lax.axis_size("ctx")
    exp_count = lax.axis_size("exp")
    ctx_index = lax.axis_index("ctx")
    exp_index = lax.axis_index("exp")
    rows_ctx = queries.shape[0]
    heads_here = queries.shape[1] // HD
    group = HQ // KVH
    scale = 1.0 / math.sqrt(HD)
    kv_start = exp_index * heads_here // group * HD
    key_own = lax.dynamic_slice_in_dim(keys, kv_start, HD, 1)
    value_own = lax.dynamic_slice_in_dim(values, kv_start, HD, 1)
    ends = jnp.cumsum(segment_lengths)
    query_pos = ctx_index * rows_ctx + jnp.arange(rows_ctx, dtype=jnp.int32)
    query_seg = segment_of(query_pos, ends)
    query_heads = queries.reshape(rows_ctx, heads_here, HD)

    def absorb(carry, key_block, value_block, first):
        width = key_block.shape[0]
        key_pos = first + jnp.arange(width, dtype=jnp.int32)
        key_seg = segment_of(key_pos, ends)
        visible = (key_pos[None, :] <= query_pos[:, None]) & (
            (key_seg[None, :] == 0) | (key_seg[None, :] == query_seg[:, None])
        )
        run_max, run_sum, run_out = carry
        scores = (
            jnp.einsum("qhd,kd->hqk", query_heads, key_block, preferred_element_type=jnp.float32)
            * scale
        )
        masked = jnp.where(visible[None], scores, -1e30)
        new_max = jnp.maximum(run_max, jnp.max(masked, axis=2))
        factor = jnp.exp(run_max - new_max)
        weights = jnp.where(visible[None], jnp.exp(scores - new_max[:, :, None]), 0.0)
        new_sum = run_sum * factor + jnp.sum(weights, axis=2)
        mixed_part = jnp.einsum(
            "hqk,kd->hqd",
            weights.astype(jnp.bfloat16),
            value_block,
            preferred_element_type=jnp.float32,
        )
        return (new_max, new_sum, run_out * factor[:, :, None] + mixed_part)

    initial = (
        jnp.full((heads_here, rows_ctx), -1e30, jnp.float32),
        jnp.zeros((heads_here, rows_ctx), jnp.float32),
        jnp.zeros((heads_here, rows_ctx, HD), jnp.float32),
    )
    key_piece = lax.all_gather(key_own, "ctx", axis=0, tiled=True)
    value_piece = lax.all_gather(value_own, "ctx", axis=0, tiled=True)
    width = key_piece.shape[0]
    step_rows = math.gcd(width, 1024)

    def one_block(number, state):
        offset = number * step_rows
        key_block = lax.dynamic_slice_in_dim(key_piece, offset, step_rows, 0)
        value_block = lax.dynamic_slice_in_dim(value_piece, offset, step_rows, 0)
        return absorb(state, key_block, value_block, offset)

    run_max, run_sum, run_out = lax.fori_loop(0, width // step_rows, one_block, initial)
    attended = (
        jnp.transpose(run_out / run_sum[:, :, None], (1, 0, 2))
        .reshape(rows_ctx, heads_here * HD)
        .astype(jnp.bfloat16)
    )
    tok_rows = stream.shape[0]
    projected = lax.psum_scatter(
        jnp.dot(attended, out_proj, preferred_element_type=jnp.float32).astype(jnp.bfloat16),
        "exp",
        scatter_dimension=0,
        tiled=True,
    ).astype(jnp.float32)
    residual = stream.astype(jnp.float32) + projected
    normed = (
        residual
        * lax.rsqrt(jnp.mean(residual * residual, axis=1, keepdims=True) + 1e-06)
        * norm_gain.astype(jnp.float32)
    ).astype(jnp.bfloat16)
    shares = route_weights / jnp.sum(route_weights, axis=1, keepdims=True)
    top_count = expert_ids.shape[1]
    expert_count = ctx_count * exp_count
    capacity = max(2, tok_rows * top_count * 9 // (expert_count * 8))
    model_width = normed.shape[1]
    flat_ids = expert_ids.reshape(-1)
    onehot = (flat_ids[:, None] == jnp.arange(expert_count, dtype=jnp.int32)[None, :]).astype(
        jnp.int32
    )
    slots = jnp.sum(onehot * jnp.cumsum(onehot, axis=0), axis=1) - 1
    sources = jnp.arange(flat_ids.shape[0], dtype=jnp.int32) // top_count
    outgoing = (
        jnp.zeros((expert_count, capacity, model_width), jnp.bfloat16)
        .at[flat_ids, slots]
        .set(normed[sources])
    )
    arrived = lax.all_to_all(outgoing, ("ctx", "exp"), split_axis=0, concat_axis=0, tiled=True)
    senders = arrived.shape[0]
    count = arrived.shape[1]
    results = expert_rows(
        arrived.reshape(senders * count, model_width), gate_proj[0], up_proj[0], down_proj[0]
    )
    returned = lax.all_to_all(
        results.reshape(senders, count, model_width),
        ("ctx", "exp"),
        split_axis=0,
        concat_axis=0,
        tiled=True,
    )
    picked = returned[flat_ids, slots].reshape(tok_rows, top_count, model_width)
    total = residual
    for rank_index in range(top_count):
        total = total + shares[:, rank_index, None] * picked[:, rank_index].astype(jnp.float32)
    return total.astype(jnp.bfloat16)


def solution(mesh):
    placed = (
        P(("ctx", "exp"), None),
        P("ctx", "exp"),
        P("ctx", None),
        P("ctx", None),
        P("exp", None),
        P(),
        P(("ctx", "exp"), None, None),
        P(("ctx", "exp"), None, None),
        P(("ctx", "exp"), None, None),
        P(("ctx", "exp"), None),
        P(("ctx", "exp"), None),
        P(),
    )
    return jax.shard_map(
        on_device, mesh=mesh, in_specs=placed, out_specs=P(("ctx", "exp"), None), check_vma=False
    )
```

profile of v0, /device:TPU:0, one launch (start us, length us, event | category | flops | bytes accessed | tf_op | source)
XLA Modules:
  0.0 847.5 jit_solution(7232164266113110464)
XLA Ops:
  15.3 33.7 %all-gather.3.cloned.1.call-done = bf16[16384,128]{1,0:T(8,128)(2,1)} async-done(((bf16[1024,128]{1,0:T(8,128)(2,1)}), bf16[16384,128]{1,0:T(8,128)(2,1)}) %all-gather.3.cloned.1.call-update) | async-done | bytes 4194320 | tf_op jit(solution)/shard_map/all_gather | solution.py:84
  49.0 39.2 %all-gather.5.cloned.1.call-done = bf16[16384,128]{1,0:T(8,128)(2,1)} async-done(((bf16[1024,128]{1,0:T(8,128)(2,1)}), bf16[16384,128]{1,0:T(8,128)(2,1)}) %all-gather.5.cloned.1.call-update) | async-done | bytes 4194320 | tf_op jit(solution)/shard_map/all_gather | solution.py:85
  88.2 316.2 %while.18 = (s32[]{:T(128)}, f32[2,1024]{1,0:T(2,128)S(1)}, f32[2,1024]{1,0:T(2,128)S(1)}, f32[2,1024,128]{2,1,0:T(8,128)}, s32[17]{0:T(128)S(1)}, /*index=5*/s3...) while((s32[]{:T(128)}, f32[2,1024]{1,0:T(2,128)S(1)}, ...), condition=%wide.region_6.7_spmd.clone, body=%wide.region_2.6_spmd.clone.sunk | while | flops 1101855744 | bytes 70424904 | solution.py:95
  90.5 6.5 fusion.63
  97.0 4.8 fusion.65
  110.1 6.5 fusion.63
  116.6 4.8 fusion.65
  122.9 4.6 fusion.67
  129.9 6.5 fusion.63
  136.4 4.8 fusion.65
  142.7 4.6 fusion.67
  149.6 6.5 fusion.63
  156.1 4.8 fusion.65
  162.5 4.6 fusion.67
  169.4 6.5 fusion.63
  175.9 4.8 fusion.65
  182.3 4.6 fusion.67
  189.2 6.5 fusion.63
  195.7 4.8 fusion.65
  202.0 4.6 fusion.67
  209.0 6.5 fusion.63
  215.5 4.8 fusion.65
  221.8 4.6 fusion.67
  228.7 6.5 fusion.63
  235.2 4.8 fusion.65
  241.6 4.6 fusion.67
  248.5 6.5 fusion.63
  255.0 4.8 fusion.65
  261.4 4.6 fusion.67
  268.3 6.5 fusion.63
  274.8 4.8 fusion.65
  281.1 4.6 fusion.67
  288.1 6.5 fusion.63
  294.6 4.8 fusion.65
  300.9 4.6 fusion.67
  307.8 6.5 fusion.63
  314.3 4.8 fusion.65
  320.7 4.6 fusion.67
  327.6 6.5 fusion.63
  334.1 4.8 fusion.65
  340.5 4.6 fusion.67
  347.4 6.5 fusion.63
  353.9 4.8 fusion.65
  360.2 4.6 fusion.67
  367.1 6.5 fusion.63
  373.6 4.8 fusion.65
  380.0 4.6 fusion.67
  386.9 6.5 fusion.63
  393.4 4.8 fusion.65
  399.8 4.6 fusion.67
  416.4 81.0 %reduce-scatter.2.cloned.1.call-done = bf16[128,2048]{1,0:T(8,128)(2,1)} async-done(((bf16[1024,2048]{1,0:T(8,128)(2,1)}), bf16[128,2048]{1,0:T(8,128)(2,1)}) %reduce-scatter.2.cloned.1.call-update) | async-done | bytes 524304 | tf_op jit(solution)/shard_map/reduce_scatter | solution.py:102
  501.0 23.4 %scatter_custom_fusion = bf16[1152,2048]{1,0:T(8,128)(2,1)} fusion(s32[1024]{0:T(1024)S(1)} %get-tuple-element.301, bf16[128,2048]{1,0:T(8,128)(2,1)} %multiply_convert_fusion, s32[1024]{0:T(1024)S(1)} %get-tuple-element.300, bf16[]{:T(256)} %constant.124.clone.1), kind=kCustom, calls=%fused_computation.35 | custom fusion | bytes 4719104
  524.4 5.4 copy.85
  529.8 105.1 %all_to_all.10 = bf16[128,9,2048]{2,1,0:T(8,128)(2,1)} all-to-all(bf16[128,9,2048]{2,1,0:T(8,128)(2,1)S(1)} %copy.85), channel_id=1, replica_groups=mesh['ctx'=16,'exp'=8] {'ctx','exp'}, dimensions={0} | all-to-all | bytes 9437184 | tf_op jit(solution)/shard_map/all_to_all | solution.py:130
  635.0 8.4 reshape.274
  643.4 6.8 fusion.29
  654.4 5.5 convolution_convert_fusion
  659.9 8.1 reshape.275
  668.0 7.3 all-to-all-start.1
  675.4 104.7 %all-to-all-done.1 = bf16[128,9,2048]{2,1,0:T(8,128)(2,1)} async-done(((bf16[128,9,2048]{2,1,0:T(8,128)(2,1)}), bf16[128,9,2048]{2,1,0:T(8,128)(2,1)}, u32[]{:S(2)}, u32[]{:S(2)}) %all-to-all-start.1) | async-done | bytes 4718624 | tf_op jit(solution)/shard_map/all_to_all | solution.py:136
  780.1 8.4 copy.86
  788.5 25.4 %gather_fusion = bf16[1024,2048]{1,0:T(8,128)(2,1)} fusion(bf16[128,9,2048]{2,0,1:T(8,128)(2,1)} %copy.86, s32[1024]{0:T(1024)S(1)} %bitcast.128), kind=kCustom, calls=%fused_computation.1 | custom fusion | bytes 8396800 | tf_op jit(solution)/shard_map/gather | solution.py:143
  813.8 21.1 %fusion.45 = (bf16[128,1,2048]{2,1,0:T(2,128)(2,1)S(1)}, bf16[128,1,2048]{2,1,0:T(2,128)(2,1)S(1)}, bf16[128,1,2048]{2,1,0:T(2,128)(2,1)S(1)}, bf16[128,1,2048]{...) fusion(bf16[128,8,2048]{2,1,0:T(8,128)(2,1)} %bitcast.129), kind=kLoop, calls=%fused_computation.112 | loop fusion | bytes 8388608 | tf_op jit(solution)/shard_map/slice | solution.py:146
  835.0 5.5 fusion.33
  (246 shorter events, 95.1 us)
Async XLA Ops:
  6.5 647.8 %copy-start = (bf16[1,768,2048]{2,1,0:T(8,128)(2,1)S(1)}, bf16[1,768,2048]{2,1,0:T(8,128)(2,1)}, u32[]{:S(2)}) copy-start(bf16[1,768,2048]{2,1,0:T(8,128)(2,1)} %param.22) | copy-start | bytes 9437188
  6.5 42.5 %all-gather.3.cloned.1.call-start = ((), (), s32[]{:S(2)}) async-start(), calls=%async_computation.3 | async-start | bytes 4456448 | tf_op jit(solution)/shard_map/all_gather | solution.py:84
  8.4 79.8 %all-gather.5.cloned.1.call-start = ((), (), s32[]{:S(2)}) async-start(), calls=%async_computation.4 | async-start | bytes 4456448 | tf_op jit(solution)/shard_map/all_gather | solution.py:85
  10.2 487.2 %reduce-scatter.2.cloned.1.call-start = ((), (), s32[]{:S(2)}) async-start(), calls=%async_computation.5 | async-start | bytes 4718592 | tf_op jit(solution)/shard_map/reduce_scatter | solution.py:102
  97.0 6.1 copy-start.1
  97.0 6.4 copy-start.2
  116.6 6.1 copy-start.1
  116.6 6.4 copy-start.2
  136.3 6.1 copy-start.1
  136.4 6.4 copy-start.2
  156.1 6.1 copy-start.1
  156.1 6.4 copy-start.2
  175.9 6.1 copy-start.1
  175.9 6.4 copy-start.2
  195.7 6.1 copy-start.1
  195.7 6.4 copy-start.2
  215.4 6.1 copy-start.1
  215.4 6.4 copy-start.2
  235.2 6.1 copy-start.1
  235.2 6.4 copy-start.2
  255.0 6.1 copy-start.1
  255.0 6.4 copy-start.2
  274.8 6.1 copy-start.1
  274.8 6.4 copy-start.2
  294.5 6.1 copy-start.1
  294.5 6.4 copy-start.2
  314.3 6.1 copy-start.1
  314.3 6.4 copy-start.2
  334.1 6.1 copy-start.1
  334.1 6.4 copy-start.2
  353.9 6.1 copy-start.1
  353.9 6.4 copy-start.2
  373.6 6.1 copy-start.1
  373.6 6.4 copy-start.2
  393.4 6.1 copy-start.1
  393.4 6.4 copy-start.2
  408.2 4.5 copy-start.8
  412.7 0.7 copy-start.9
  412.7 3.4 copy-start.11
  412.7 3.5 copy-start.10
  413.7 0.8 copy-start.6
  643.4 6.8 copy-start.3
  643.4 6.8 copy-start.12
  668.0 7.3 copy-start.7
  668.0 112.0 %all-to-all-start.1 = ((bf16[128,9,2048]{2,1,0:T(8,128)(2,1)}), bf16[128,9,2048]{2,1,0:T(8,128)(2,1)}, u32[]{:S(2)}, u32[]{:S(2)}) async-start(bf16[128,9,2048]{2,1,0:T(8,128)(2,1)} %reshape.275), calls=%async_computation.2 | async-start | bytes 16777216 | tf_op jit(solution)/shard_map/all_to_all | solution.py:136
  813.8 21.1 %copy-start.4 = (bf16[128,2048]{1,0:T(8,128)(2,1)S(1)}, bf16[128,2048]{1,0:T(8,128)(2,1)}, u32[]{:S(2)}) copy-start(bf16[128,2048]{1,0:T(8,128)(2,1)} %param.14) | copy-start | bytes 1572868
  813.8 21.1 %copy-start.5 = (bf16[128,2048]{1,0:T(8,128)(2,1)S(1)}, bf16[128,2048]{1,0:T(8,128)(2,1)}, u32[]{:S(2)}) copy-start(bf16[128,2048]{1,0:T(8,128)(2,1)} %reduce-scatter.2.cloned.1.call-done) | copy-start | bytes 1572868
Sparse Core Ops, SparseCore 0:
  9.1 39.8 all-gather.2
  50.7 37.4 all-gather.4
  412.9 84.4 reduce-scatter.1
where the time goes:
time: 858 us; the launch traced here: 848 us
  waiting for transfers between devices  259 us (30%)
  matrix products  198 us (23%)
  local copies, waits for them, and re-layouts  138 us (16%)
  other arithmetic  127 us (15%)
  blocking collectives  105 us (12%)
  between operations  13.9 us (2%)
    all_to_all x1, blocking collectives, on_device(): lax.all_to_all(outgoing, ('ctx', 'exp'), split_axis=0, concat_axis=0, til...  105 us
    all_to_all x1, waiting for transfers between devices, on_device(): lax.all_to_all(results.reshape(senders, count, model_width), ('ctx', 'exp...  105 us
    dot_general x16, matrix products, absorb(): jnp.einsum('qhd,kd->hqk', query_heads, key_block, preferred_element_type=...  104 us
    reduce_scatter x1, waiting for transfers between devices, on_device(): lax.psum_scatter(jnp.dot(attended, out_proj, preferred_element_type=jnp.f...  81 us
    reduce_sum x16, other arithmetic, absorb(): new_sum = run_sum * factor + jnp.sum(weights, axis=2)  76.5 us
    dot_general x16, matrix products, absorb(): jnp.einsum('hqk,kd->hqd', weights.astype(jnp.bfloat16), value_block, pref...  73.4 us
    all_gather x1, waiting for transfers between devices, on_device(): value_piece = lax.all_gather(value_own, 'ctx', axis=0, tiled=True)  39.2 us
    and x16, other arithmetic, absorb(): (key_pos[None, :] <= query_pos[:, None]) & ((key_seg[None, :] == 0) | (ke...  35.3 us
  transfers between devices with their start and end apart: 4, of which 4 were waited for; matrix products, arithmetic and copies ran while one was open for 1% of the time, Pallas kernels for 0%

commit v1 on v0

v1 whole, which is shorter than its diff:
```python
import functools, math
import jax
import jax.numpy as jnp
from jax import lax
from jax.experimental import pallas as pl
from jax.experimental.pallas import tpu as pltpu
from jax.sharding import PartitionSpec as P

HD = 128
KVH = 4
HQ = 16
RESP1 = 17

def attend_kernel(TQ, TK, RC, place_ref, lengths_ref, q_ref, kv_ref, out_ref, q_s, m_s, acc_s, v_s):
    rows = q_ref.shape[0]
    M = 2 * TQ
    base = place_ref[0]
    prompt = lengths_ref[0]
    scale = 1.0 / math.sqrt(HD)
    v_s[:, HD:] = jnp.ones((TK, HD), jnp.bfloat16)

    def tile(number, _):
        at = pl.multiple_of(number * TQ, TQ)
        first = base + at
        begin = jnp.int32(0); begin_last = jnp.int32(0); end = jnp.int32(0)
        for s in range(RESP1):
            end = end + lengths_ref[s]
            begin = jnp.where(first >= end, end, begin)
            begin_last = jnp.where(first + TQ - 1 >= end, end, begin_last)
        q_s[:TQ] = q_ref[pl.ds(at, TQ), :HD]
        q_s[TQ:] = q_ref[pl.ds(at, TQ), HD:]
        m_s[...] = jnp.full_like(m_s, -1e30)
        acc_s[...] = jnp.zeros_like(acc_s)
        last = (first + TQ - 1) // TK
        shared = jnp.minimum((prompt + TK - 1) // TK, last + 1)
        own = jnp.maximum(begin // TK, shared)
        count = shared + last + 1 - own

        def block(lo, masked):
            k = kv_ref[pl.ds(lo, TK), :HD]
            v_s[:, :HD] = kv_ref[pl.ds(lo, TK), HD:]
            v = v_s[...]
            for r in range(M // RC):
                rs = pl.ds(r * RC, RC)
                s = lax.dot_general(q_s[rs], k, (((1,), (1,)), ((), ())), preferred_element_type=jnp.float32) * scale
                if masked:
                    pos = first + (r * RC) % TQ + lax.broadcasted_iota(jnp.int32, (min(RC, TQ), 1), 0)
                    starts = jnp.zeros_like(pos)
                    end = jnp.int32(0)
                    for i in range(RESP1):
                        end = end + lengths_ref[i]
                        starts = jnp.where(pos >= end, end, starts)
                    if RC > TQ:
                        pos = jnp.concatenate([pos] * (RC // TQ), axis=0)
                        starts = jnp.concatenate([starts] * (RC // TQ), axis=0)
                    kpos = lo + lax.broadcasted_iota(jnp.int32, (1, TK), 1)
                    seen = (kpos <= pos) & ((kpos < prompt) | (kpos >= starts))
                    s = jnp.where(seen, s, -1e30)
                old = m_s[rs]
                new = jnp.maximum(old, jnp.max(s, axis=1, keepdims=True))
                p = jnp.exp(s - new[:, :1]).astype(jnp.bfloat16)
                pv = jnp.dot(p, v, preferred_element_type=jnp.float32)
                alpha = jnp.exp(old - new)
                acc_s[rs, :HD] = acc_s[rs, :HD] * alpha + pv[:, :HD]
                acc_s[rs, HD:] = acc_s[rs, HD:] * alpha + pv[:, HD:]
                m_s[rs] = new

        def step(i, _):
            j = jnp.where(i < shared, i, own + i - shared)
            lo = pl.multiple_of(j * TK, TK)
            hi = lo + TK
            whole = (hi <= first + 1) & ((hi <= prompt) | (lo >= begin_last))
            pl.when(whole)(lambda: block(lo, False))
            pl.when(jnp.logical_not(whole))(lambda: block(lo, True))
            return 0

        lax.fori_loop(0, count, step, 0)
        o = (acc_s[:, :HD] / acc_s[:, HD:]).astype(jnp.bfloat16)
        out_ref[pl.ds(at, TQ), :HD] = o[:TQ]
        out_ref[pl.ds(at, TQ), HD:] = o[TQ:]
        return 0

    lax.fori_loop(0, rows // TQ, tile, 0)

def attend(place, lengths, q, kv, TQ=512, TK=1024, RC=128):
    return pl.pallas_call(
        functools.partial(attend_kernel, TQ, TK, RC),
        out_shape=jax.ShapeDtypeStruct(q.shape, jnp.bfloat16),
        in_specs=[pl.BlockSpec(memory_space=pltpu.SMEM)]*2 + [pl.BlockSpec(memory_space=pltpu.VMEM)]*2,
        out_specs=pl.BlockSpec(memory_space=pltpu.VMEM),
        scratch_shapes=[pltpu.VMEM((2*TQ, HD), jnp.bfloat16), pltpu.VMEM((2*TQ, HD), jnp.float32),
            pltpu.VMEM((2*TQ, 2*HD), jnp.float32), pltpu.VMEM((TK, 2*HD), jnp.bfloat16)],
        compiler_params=pltpu.CompilerParams(vmem_limit_bytes=48 << 20),
        name="attend",
    )(place, lengths, q, kv)

LANES = 128
VM = pl.BlockSpec(memory_space=pltpu.VMEM)
SM = pl.BlockSpec(memory_space=pltpu.SMEM)

def slots_kernel(capacity, ids_ref, weights_ref, place_ref, shares_ref):
    rows, top = ids_ref.shape
    experts = 128
    ids = ids_ref[...]
    lane = lax.broadcasted_iota(jnp.int32, (rows, experts), 1)
    named = [(ids[:, k : k + 1] == lane).astype(jnp.float32) for k in range(top)]
    chosen = functools.reduce(jnp.add, named).astype(jnp.bfloat16)
    before = (
        lax.broadcasted_iota(jnp.int32, (rows, rows), 1)
        < lax.broadcasted_iota(jnp.int32, (rows, rows), 0)
    ).astype(jnp.bfloat16)
    rank = jnp.dot(before, chosen, preferred_element_type=jnp.float32)
    slot = [jnp.sum(one * rank, axis=1, keepdims=True) for one in named]
    place_ref[...] = ids * capacity + jnp.concatenate(slot, axis=1).astype(jnp.int32)
    weights = weights_ref[...]
    shares_ref[...] = weights / jnp.sum(weights, axis=1, keepdims=True)

def slots(ids, weights, capacity):
    return pl.pallas_call(
        functools.partial(slots_kernel, capacity),
        out_shape=(jax.ShapeDtypeStruct(ids.shape, jnp.int32), jax.ShapeDtypeStruct(weights.shape, jnp.float32)),
        in_specs=[VM, VM], out_specs=(VM, VM), name="slots",
    )(ids, weights)

def pack_kernel(place_ref, projected_ref, stream_ref, gain_ref, residual_ref, out_ref, rows32):
    rows, width = stream_ref.shape
    parts = width // LANES
    residual = stream_ref[...].astype(jnp.float32) + projected_ref[...].astype(jnp.float32)
    spread = lax.rsqrt(jnp.mean(residual * residual, axis=1, keepdims=True) + 1e-06)
    normed = residual * spread * gain_ref[...].astype(jnp.float32)
    for part in range(parts):
        residual_ref[:, part, :] = residual[:, part * LANES : (part + 1) * LANES]
        rows32[:, part, :] = normed[:, part * LANES : (part + 1) * LANES]
    out_ref[...] = jnp.zeros_like(out_ref)

    def one(t, _):
        row = rows32[t].astype(jnp.bfloat16)
        for k in range(8):
            out_ref[place_ref[t * 8 + k]] = row
        return 0
    lax.fori_loop(0, rows, one, 0, unroll=4)

def pack(place, projected, stream, gain, slots_count):
    rows, width = stream.shape
    parts = width // LANES
    return pl.pallas_call(
        pack_kernel,
        out_shape=(jax.ShapeDtypeStruct((rows, parts, LANES), jnp.float32),
                   jax.ShapeDtypeStruct((slots_count, parts, LANES), jnp.bfloat16)),
        in_specs=[SM, VM, VM, VM], out_specs=(VM, VM),
        scratch_shapes=[pltpu.VMEM((rows, parts, LANES), jnp.float32)],
        compiler_params=pltpu.CompilerParams(vmem_limit_bytes=48 << 20),
        name="pack",
    )(place, projected, stream, gain)

TR = 384

def experts_kernel(x_ref, gate_ref, up_ref, down_ref, out_ref, rows32, rows16, back32):
    parts = x_ref.shape[1]
    rows32[...] = x_ref[...].astype(jnp.float32)
    for part in range(parts):
        rows16[:, part * LANES : (part + 1) * LANES] = rows32[:, part, :].astype(jnp.bfloat16)
    rows = rows16[...]
    gate = jnp.dot(rows, gate_ref[0], preferred_element_type=jnp.float32)
    upper = jnp.dot(rows, up_ref[0], preferred_element_type=jnp.float32)
    hidden = (gate / (1.0 + jnp.exp(-gate)) * upper).astype(jnp.bfloat16)
    result = jnp.dot(hidden, down_ref[0], preferred_element_type=jnp.float32)
    for part in range(parts):
        back32[:, part, :] = result[:, part * LANES : (part + 1) * LANES]
    out_ref[...] = back32[...].astype(jnp.bfloat16)

def experts(x, gate, up, down):
    count, parts, lanes = x.shape
    width = parts * lanes
    hidden = gate.shape[2]
    return pl.pallas_call(
        experts_kernel,
        out_shape=jax.ShapeDtypeStruct(x.shape, jnp.bfloat16),
        grid=(count // TR,),
        in_specs=[pl.BlockSpec((TR, parts, lanes), lambda i: (i, 0, 0)),
                  pl.BlockSpec(gate.shape, lambda i: (0, 0, 0)),
                  pl.BlockSpec(up.shape, lambda i: (0, 0, 0)),
                  pl.BlockSpec(down.shape, lambda i: (0, 0, 0))],
        out_specs=pl.BlockSpec((TR, parts, lanes), lambda i: (i, 0, 0)),
        scratch_shapes=[pltpu.VMEM((TR, parts, lanes), jnp.float32), pltpu.VMEM((TR, width), jnp.bfloat16),
                        pltpu.VMEM((TR, parts, lanes), jnp.float32)],
        compiler_params=pltpu.CompilerParams(vmem_limit_bytes=56 << 20),
        name="experts",
    )(x, gate, up, down)

def combine_kernel(place_ref, shares_ref, residual_ref, back_ref, out_ref, total):
    rows, parts, lanes = residual_ref.shape
    def one(t, _):
        acc = residual_ref[t]
        for k in range(8):
            acc = acc + shares_ref[t * 8 + k] * back_ref[place_ref[t * 8 + k]].astype(jnp.float32)
        total[t] = acc
        return 0
    lax.fori_loop(0, rows, one, 0, unroll=2)
    for part in range(parts):
        out_ref[:, part * LANES : (part + 1) * LANES] = total[:, part, :].astype(jnp.bfloat16)

def combine(place, shares, residual, back):
    rows, parts, lanes = residual.shape
    return pl.pallas_call(
        combine_kernel,
        out_shape=jax.ShapeDtypeStruct((rows, parts * lanes), jnp.bfloat16),
        in_specs=[SM, SM, VM, VM], out_specs=VM,
        scratch_shapes=[pltpu.VMEM((rows, parts, lanes), jnp.float32)],
        compiler_params=pltpu.CompilerParams(vmem_limit_bytes=48 << 20),
        name="combine",
    )(place, shares, residual, back)


def on_device(
    stream,
    queries,
    keys,
    values,
    out_proj,
    norm_gain,
    gate_proj,
    up_proj,
    down_proj,
    expert_ids,
    route_weights,
    segment_lengths,
):
    ctx_count = lax.axis_size("ctx")
    exp_count = lax.axis_size("exp")
    ctx_index = lax.axis_index("ctx")
    exp_index = lax.axis_index("exp")
    rows_ctx = queries.shape[0]
    heads_here = queries.shape[1] // HD
    group = HQ // KVH
    expert_count = ctx_count * exp_count
    tok_rows, top_count = expert_ids.shape
    capacity = max(2, tok_rows * top_count * 9 // (expert_count * 8))
    kv_start = exp_index * heads_here // group * HD
    own = jnp.concatenate(
        [
            lax.dynamic_slice_in_dim(keys, kv_start, HD, 1),
            lax.dynamic_slice_in_dim(values, kv_start, HD, 1),
        ],
        axis=1,
    )
    place, shares = slots(expert_ids, route_weights, capacity)
    place = place.reshape(-1)
    shares = shares.reshape(-1)
    gathered = lax.all_gather(own, "ctx", axis=0, tiled=True)
    first = (ctx_index * rows_ctx).astype(jnp.int32).reshape(1)
    attended = attend(first, segment_lengths, queries, gathered)
    projected = lax.psum_scatter(
        jnp.dot(attended, out_proj, preferred_element_type=jnp.float32).astype(jnp.bfloat16),
        "exp",
        scatter_dimension=0,
        tiled=True,
    )
    residual, outgoing = pack(
        place, projected, stream, norm_gain.reshape(1, -1), expert_count * capacity
    )
    shape = (expert_count, capacity) + outgoing.shape[1:]
    arrived = lax.all_to_all(
        outgoing.reshape(shape), ("ctx", "exp"), split_axis=0, concat_axis=0, tiled=True
    )
    results = experts(arrived.reshape(outgoing.shape), gate_proj, up_proj, down_proj)
    returned = lax.all_to_all(
        results.reshape(shape), ("ctx", "exp"), split_axis=0, concat_axis=0, tiled=True
    )
    return combine(place, shares, residual, returned.reshape(outgoing.shape))


def solution(mesh):
    placed = (
        P(("ctx", "exp"), None),
        P("ctx", "exp"),
        P("ctx", None),
        P("ctx", None),
        P("exp", None),
        P(),
        P(("ctx", "exp"), None, None),
        P(("ctx", "exp"), None, None),
        P(("ctx", "exp"), None, None),
        P(("ctx", "exp"), None),
        P(("ctx", "exp"), None),
        P(),
    )
    return jax.shard_map(
        on_device, mesh=mesh, in_specs=placed, out_specs=P(("ctx", "exp"), None), check_vma=False
    )
```

time: 858 us -> 378 us (0.44); the launches traced: 848 us -> 379 us
  matrix products: 198 us -> 3.22 us
  local copies, waits for them, and re-layouts: 138 us -> 6.41 us
  other arithmetic: 127 us -> 0.85 us
  Pallas kernels: 0 us -> 53.7 us
  blocking collectives: 105 us -> 65.9 us
  waiting for transfers between devices: 259 us -> 229 us
    dot_general x35 -> x0, matrix products: 193 us -> none  [the longest x16 104 us: absorb(): jnp.einsum('qhd,kd->hqk', query_heads, key_block, preferred_element_type=...]
    reduce_sum x36 -> x0, other arithmetic: 79.9 us -> none  [the longest x16 76.5 us: absorb(): new_sum = run_sum * factor + jnp.sum(weights, axis=2)]
    pallas_call x0 -> x5, Pallas kernels: none -> 53.7 us  [the longest x1 30.1 us: experts(): pl.pallas_call(experts_kernel, out_shape=jax.ShapeDtypeStruct(x.shape, jn...]
    all_to_all x1, waiting for transfers between devices: 105 us -> 58.2 us  [on_device(): lax.all_to_all(results.reshape(shape), ('ctx', 'exp'), split_axis=0, conc...]
    all_to_all x1, blocking collectives: 105 us -> 65.9 us  [on_device(): lax.all_to_all(outgoing.reshape(shape), ('ctx', 'exp'), split_axis=0, con...]
    and x16 -> x0, other arithmetic: 35.3 us -> none  [absorb(): (key_pos[None, :] <= query_pos[:, None]) & ((key_seg[None, :] == 0) | (ke...]
    reduce_scatter x1, waiting for transfers between devices: 81 us -> 116 us  [on_device(): lax.psum_scatter(jnp.dot(attended, out_proj, preferred_element_type=jnp.f...]
    while x81 -> x0, local copies, waits for them, and re-layouts: 27.2 us -> none
  transfers between devices with their start and end apart: 4 -> 3, of which waited for: 4 -> 3; matrix products, arithmetic and copies ran while one was open for 1% -> 1% of each run, Pallas kernels for 0% -> 1%
where the time goes in v1:
time: 378 us; the launch traced here: 379 us
  waiting for transfers between devices  229 us (61%)
  blocking collectives  65.9 us (17%)
  Pallas kernels  53.7 us (14%)
  between operations  13.5 us (4%)
  local copies, waits for them, and re-layouts  6.41 us (2%)
  starting transfers between devices  5.96 us (2%)
    reduce_scatter x1, waiting for transfers between devices, on_device(): lax.psum_scatter(jnp.dot(attended, out_proj, preferred_element_type=jnp.f...  116 us
    all_to_all x1, blocking collectives, on_device(): lax.all_to_all(outgoing.reshape(shape), ('ctx', 'exp'), split_axis=0, con...  65.9 us
    all_to_all x1, waiting for transfers between devices, on_device(): lax.all_to_all(results.reshape(shape), ('ctx', 'exp'), split_axis=0, conc...  58.2 us
    all_gather x1, waiting for transfers between devices, on_device(): gathered = lax.all_gather(own, 'ctx', axis=0, tiled=True)  55.1 us
    pallas_call x1, Pallas kernels, experts(): pl.pallas_call(experts_kernel, out_shape=jax.ShapeDtypeStruct(x.shape, jn...  30.1 us
    pallas_call x1, Pallas kernels, attend(): pl.pallas_call(functools.partial(attend_kernel, TQ, TK, RC), out_shape=ja...  9.11 us
  transfers between devices with their start and end apart: 3, of which 3 were waited for; matrix products, arithmetic and copies ran while one was open for 1% of the time, Pallas kernels for 1%

profile of v1, /device:TPU:0, one launch (start us, length us, event | category | flops | bytes accessed | tf_op | source)
XLA Modules:
  0.0 378.5 jit_solution(17793220549330143214)
XLA Ops:
  6.5 0.0 copy-start
  6.5 0.0 all-gather.2.cloned.1.call-start
  6.5 1.2 constant_dynamic-slice_fusion
  7.7 0.9 pad_maximum_fusion
  8.6 0.0 all-gather.2.cloned.1.call-update
  8.6 0.0 reduce-scatter.2.cloned.1.call-start
  8.6 55.1 %all-gather.2.cloned.1.call-done.kv_ref = bf16[16384,256]{1,0:T(8,128)(2,1)} async-done(((bf16[1024,256]{1,0:T(8,128)(2,1)}), bf16[16384,256]{1,0:T(8,128)(2,1)}) %all-gather.2.cloned.1.call-update) | async-done | bytes 8388624 | tf_op jit(solution)/shard_map/all_gather | solution.py:250
  63.7 0.0 copy-start.1
  63.7 1.0 copy-done.1
  64.8 0.0 copy-start.4
  64.8 0.7 copy-done.4
  65.4 9.1 %attend.1 = bf16[1024,256]{1,0:T(8,128)(2,1)S(1)} custom-call(s32[1]{0:T(128)} %bitcast.place_ref, s32[17]{0:T(128)S(1)} %copy-done.4, bf16[1024,256]{1,0:T(8,128)(2,1)S(1)} %copy-done.1, bf16[16384,256]{1,0:T(8,128)(2,1)} %all-gather.2.cloned.1.call-done.kv_ref), custom_call_target="tpu_custom_call" | custom-call | tf_op jit(solution)/shard_map/attend/pallas_call | solution.py:86
  74.5 0.0 copy-done
  74.6 0.0 copy-start.6
  74.6 0.0 copy-start.7
  74.6 0.0 copy-start.8
  74.6 0.0 copy-start.2
  74.6 3.2 convolution_convert_fusion
  77.8 0.0 reduce-scatter.2.cloned.1.call-update
  77.8 0.0 copy-done.6
  77.9 0.0 copy-done.7
  77.9 0.7 copy.15.ids_ref
  78.6 0.0 copy-done.8
  78.6 0.7 copy.16.weights_ref
  79.3 2.1 slots.1
  81.4 0.9 reshape.24.place_ref
  82.3 115.6 %reduce-scatter.2.cloned.1.call-done.projected_ref = bf16[128,2048]{1,0:T(8,128)(2,1)} async-done(((bf16[1024,2048]{1,0:T(8,128)(2,1)}), bf16[128,2048]{1,0:T(8,128)(2,1)}) %reduce-scatter.2.cloned.1.call-update) | async-done | bytes 524304 | tf_op jit(solution)/shard_map/reduce_scatter | solution.py:253
  198.0 0.0 copy-done.2
  198.0 0.0 copy-start.3
  198.0 1.0 copy-done.3
  199.0 6.3 %pack.1 = (f32[128,16,128]{2,1,0:T(8,128)S(1)}, bf16[1152,16,128]{2,1,0:T(8,128)(2,1)}) custom-call(s32[1024]{0:T(1024)S(1)} %reshape.24.place_ref, bf16[128,2048]{1,0:T(8,128)(2,1)S(1)} %copy-done.3, bf16[128,2048]{1,0:T(8,128)(2,1)S(1)} %copy-done.2, bf16[1,2048]{1,0:T(2,128)(2,1)S(1)} %reshape.27.gain_ref), custom_call_target="tpu_custom_call" | custom-call | tf_op jit(solution)/shard_map/pack/pallas_call | solution.py:146
  205.4 65.9 %all_to_all.10 = bf16[128,9,16,128]{3,2,1,0:T(8,128)(2,1)} all-to-all(bf16[128,9,16,128]{3,2,1,0:T(8,128)(2,1)} %bitcast.9), channel_id=1, replica_groups=mesh['ctx'=16,'exp'=8] {'ctx','exp'}, dimensions={0} | all-to-all | bytes 9437184 | tf_op jit(solution)/shard_map/all_to_all | solution.py:263
  271.3 30.1 %experts.1 = bf16[1152,16,128]{2,1,0:T(8,128)(2,1)} custom-call(bf16[1152,16,128]{2,1,0:T(8,128)(2,1)} %bitcast.8, bf16[1,2048,768]{2,1,0:T(8,128)(2,1)} %gate_ref.1, bf16[1,2048,768]{2,1,0:T(8,128)(2,1)} %up_ref.1, bf16[1,768,2048]{2,1,0:T(8,128)(2,1)} %down_ref.1), custom_call_target="tpu_custom_call" | custom-call | tf_op jit(solution)/shard_map/experts/pallas_call | solution.py:176
  301.4 0.0 copy-start.5
  301.4 5.9 %all-to-all-start.1 = ((bf16[128,9,16,128]{3,2,1,0:T(8,128)(2,1)}), bf16[128,9,16,128]{3,2,1,0:T(8,128)(2,1)}, u32[]{:S(2)}, u32[]{:S(2)}) async-start(bf16[128,9,16,128]{3,2,1,0:T(8,128)(2,1)} %bitcast.7), calls=%async_computation.2 | async-start | bytes 9437184 | tf_op jit(solution)/shard_map/all_to_all | solution.py:267
  307.4 0.0 copy-done.5
  307.4 0.1 reshape.25.shares_ref
  307.5 58.2 %all-to-all-done.1 = bf16[128,9,16,128]{3,2,1,0:T(8,128)(2,1)} async-done(((bf16[128,9,16,128]{3,2,1,0:T(8,128)(2,1)}), bf16[128,9,16,128]{3,2,1,0:T(8,128)(2,1)}, u32[]{:S(2)}, u32[]{:S(2)}) %all-to-all-start.1) | async-done | bytes 4718624 | tf_op jit(solution)/shard_map/all_to_all | solution.py:267
  365.6 6.0 %combine.1 = bf16[128,2048]{1,0:T(8,128)(2,1)} custom-call(s32[1024]{0:T(1024)S(1)} %reshape.24.place_ref, f32[1024]{0:T(1024)S(1)} %reshape.25.shares_ref, f32[128,16,128]{2,1,0:T(8,128)S(1)} %get-tuple-element.11.residual_ref, bf16[1152,16,128]{2,1,0:T(8,128)(2,1)} %bitcast.4.back_ref), custom_call_target="tpu_custom_call" | custom-call | tf_op jit(solution)/shard_map/combine/pallas_call | solution.py:205
  (1 shorter events, 0.0 us)
Async XLA Ops:
  6.5 68.0 %copy-start = (bf16[256,2048]{1,0:T(8,128)(2,1)S(1)}, bf16[256,2048]{1,0:T(8,128)(2,1)}, u32[]{:S(2)}) copy-start(bf16[256,2048]{1,0:T(8,128)(2,1)} %param.16) | copy-start | bytes 3145732
  6.5 57.2 %all-gather.2.cloned.1.call-start = ((), (), s32[]{:S(2)}) async-start(), calls=%async_computation.3 | async-start | bytes 8912896 | tf_op jit(solution)/shard_map/all_gather | solution.py:250
  8.6 189.4 %reduce-scatter.2.cloned.1.call-start = ((), (), s32[]{:S(2)}) async-start(), calls=%async_computation.4 | async-start | bytes 4718592 | tf_op jit(solution)/shard_map/reduce_scatter | solution.py:253
  63.7 1.0 copy-start.1
  64.8 0.7 copy-start.4
  74.6 3.3 copy-start.6
  74.6 3.3 copy-start.7
  74.6 4.0 %copy-start.8 = (f32[128,8]{0,1:T(8,128)S(1)}, f32[128,8]{0,1:T(8,128)}, u32[]{:S(2)}) copy-start(f32[128,8]{0,1:T(8,128)} %param.22) | copy-start | bytes 12292
  74.6 123.4 %copy-start.2 = (bf16[128,2048]{1,0:T(8,128)(2,1)S(1)}, bf16[128,2048]{1,0:T(8,128)(2,1)}, u32[]{:S(2)}) copy-start(bf16[128,2048]{1,0:T(8,128)(2,1)} %stream_ref.1) | copy-start | bytes 1572868
  198.0 1.0 copy-start.3
  301.4 5.9 %copy-start.5 = (f32[128,8]{1,0:T(8,128)S(1)}, f32[128,8]{1,0:T(8,128)}, u32[]{:S(2)}) copy-start(f32[128,8]{1,0:T(8,128)} %get-tuple-element.10) | copy-start | bytes 12292
  301.4 64.2 %all-to-all-start.1 = ((bf16[128,9,16,128]{3,2,1,0:T(8,128)(2,1)}), bf16[128,9,16,128]{3,2,1,0:T(8,128)(2,1)}, u32[]{:S(2)}, u32[]{:S(2)}) async-start(bf16[128,9,16,128]{3,2,1,0:T(8,128)(2,1)} %bitcast.7), calls=%async_computation.2 | async-start | bytes 9437184 | tf_op jit(solution)/shard_map/all_to_all | solution.py:267
Sparse Core Ops, SparseCore 0:
  9.1 54.6 all-gather.1
  78.0 119.9 reduce-scatter.1

commit v2 on v1

v2 whole, which is shorter than its diff:
```python
import functools
import math

import jax
import jax.numpy as jnp
from jax import lax
from jax.experimental import pallas as pl
from jax.experimental.pallas import tpu as pltpu
from jax.sharding import PartitionSpec as P

HD = 128
KVH = 4
HQ = 16
LANES = 128
SEGMENTS = 17
SHARD = 1024
HALF = 8
TQ = 1024
RC = 256
NEVER = -1e30
VM = pl.BlockSpec(memory_space=pltpu.VMEM)
SM = pl.BlockSpec(memory_space=pltpu.SMEM)
HBM = pl.BlockSpec(memory_space=pl.ANY)


def attend_part(final, meta_ref, lengths_ref, *refs):
    pieces = refs[:10]
    if final:
        q_ref, out_ref, lse_ref, kv_s, q_s, m_s, acc_s, v_s, sems = refs[10:]
    else:
        q_refs, out_refs = refs[10:12], refs[12:14]
        kv_s, q_s, m_s, acc_s, v_s, sems = refs[14:]
    base, low, active, z, core = (meta_ref[i] for i in range(5))
    prompt = lengths_ref[0]
    scale = math.log2(math.e) / math.sqrt(HD)

    first = base
    begin = jnp.int32(0)
    begin_last = jnp.int32(0)
    end = jnp.int32(0)
    for s in range(SEGMENTS):
        end = end + lengths_ref[s]
        begin = jnp.where(first >= end, end, begin)
        begin_last = jnp.where(first + TQ - 1 >= end, end, begin_last)
    last = (first + TQ - 1) // SHARD
    shared = jnp.minimum((prompt + SHARD - 1) // SHARD, last + 1)
    own = jnp.maximum(begin // SHARD, shared)
    one_from, one_to = low, jnp.minimum(shared, low + HALF)
    two_from, two_to = jnp.maximum(own, low), jnp.minimum(last + 1, low + HALF)
    one_count = jnp.maximum(one_to - one_from, 0)
    count = one_count + jnp.maximum(two_to - two_from, 0)

    copies = []
    for other in range(2):
        side = core if other == 0 else 1 - core
        for n, (dz, begin_row) in enumerate(((0, 0), (3, 0), (1, 0), (2, 0), (2, SHARD // 2))):
            piece = pieces[other * 5 + n]
            shard = ((z + dz) & 3) * 2 + side
            target = kv_s.at[shard, pl.ds(begin_row, piece.shape[0])]
            number = low + shard
            used = (number < one_to) | ((number >= two_from) & (number < two_to))
            copies.append(
                ((active > 0) & used, pltpu.make_async_copy(piece, target, sems.at[other * 5 + n]))
            )

    for used, copy in copies:
        pl.when(used)(copy.start)

    @pl.when(active > 0)
    def _():
        v_s[:, HD:] = jnp.ones((SHARD, HD), jnp.bfloat16)
        for head in range(2):
            hs = slice(head * HD, (head + 1) * HD)
            if final:
                q = q_ref[:, hs].astype(jnp.float32) * scale
            else:
                q = jnp.concatenate([ref[:, hs] for ref in q_refs], axis=0).astype(jnp.float32) * scale
            rounded = q.astype(jnp.bfloat16)
            q_s[head * TQ : (head + 1) * TQ, :HD] = rounded
            q_s[head * TQ : (head + 1) * TQ, HD:] = (q - rounded.astype(jnp.float32)).astype(jnp.bfloat16)
        m_s[...] = jnp.full_like(m_s, NEVER)
        acc_s[...] = jnp.zeros_like(acc_s)

    for used, copy in copies:
        pl.when(used)(copy.wait)

    @pl.when(active > 0)
    def _():
        def block(number, masked):
            lo = number * SHARD
            k = kv_s[number - low, :, :HD]
            k = jnp.concatenate([k, k], axis=1)
            v_s[:, :HD] = kv_s[number - low, :, HD:]
            v = v_s[...]

            def score(r):
                return lax.dot_general(
                    q_s[pl.ds(r * RC, RC)], k, (((1,), (1,)), ((), ())), preferred_element_type=jnp.float32
                )

            ahead = score(0)
            for r in range(2 * TQ // RC):
                rs = pl.ds(r * RC, RC)
                s = ahead
                if r + 1 < 2 * TQ // RC:
                    ahead = score(r + 1)
                if masked:
                    pos = first + (r * RC) % TQ + lax.broadcasted_iota(jnp.int32, (RC, 1), 0)
                    starts = jnp.zeros_like(pos)
                    end = jnp.int32(0)
                    for i in range(SEGMENTS):
                        end = end + lengths_ref[i]
                        starts = jnp.where(pos >= end, end, starts)
                    kpos = lo + lax.broadcasted_iota(jnp.int32, (1, SHARD), 1)
                    seen = jnp.where(kpos < prompt, SHARD * 2 * HALF, kpos) >= starts
                    if final:
                        seen = seen & (kpos <= pos)
                    s = jnp.where(seen, s, NEVER)
                old = m_s[rs]
                new = jnp.maximum(old, jnp.max(s, axis=1, keepdims=True))
                p = jnp.exp2(s - new[:, :1]).astype(jnp.bfloat16)
                m_s[rs] = new
                alpha = jnp.exp2(old - new)
                pv = jnp.dot(p, v, preferred_element_type=jnp.float32)
                acc_s[rs, :HD] = acc_s[rs, :HD] * alpha + pv[:, :HD]
                acc_s[rs, HD:] = acc_s[rs, HD:] * alpha + pv[:, HD:]

        def step(i, _):
            number = jnp.where(i < one_count, one_from + i, two_from + i - one_count)
            lo = number * SHARD
            hi = lo + SHARD
            whole = (hi <= first + 1) & ((hi <= prompt) | (lo >= begin_last))
            pl.when(whole)(lambda: block(number, False))
            pl.when(jnp.logical_not(whole))(lambda: block(number, True))
            return 0

        lax.fori_loop(0, count, step, 0)
        for head in range(2):
            hs = pl.ds(head * TQ, TQ)
            total = acc_s[hs, HD:]
            o = acc_s[hs, :HD] / total
            lse = m_s[hs] + jnp.log2(total)
            if final:
                out_ref[:, head * HD : (head + 1) * HD] = o
                lse_ref[:, head * HD : (head + 1) * HD] = lse
            else:
                a = lse.astype(jnp.bfloat16).astype(jnp.float32)
                b = (lse - a).astype(jnp.bfloat16).astype(jnp.float32)
                c = lse - a - b
                lane = lax.broadcasted_iota(jnp.int32, (TQ, LANES), 1)
                parts = jnp.where(lane == 0, a, jnp.where(lane == 1, b, c)).astype(jnp.bfloat16)
                o = o.astype(jnp.bfloat16)
                half = TQ // 2
                for n in range(2):
                    out_refs[n][:, head * HD : (head + 1) * HD] = o[n * half : (n + 1) * half]
                    out_refs[n][:, (2 + head) * HD : (3 + head) * HD] = parts[n * half : (n + 1) * half]


def attend(final, meta, lengths, q, pieces, blocks):
    if final:
        shapes = tuple(jax.ShapeDtypeStruct((SHARD, 2 * HD), jnp.float32) for _ in range(2))
    else:
        shapes = tuple(jax.ShapeDtypeStruct((TQ // 2, 4 * HD), jnp.bfloat16) for _ in range(2))
    return pl.pallas_call(
        functools.partial(attend_part, final),
        out_shape=shapes,
        in_specs=[SM, SM] + [HBM] * 10 + [VM] * len(q),
        out_specs=(VM, VM),
        scratch_shapes=[
            pltpu.VMEM((HALF, SHARD, 2 * HD), jnp.bfloat16),
            pltpu.VMEM((2 * TQ, 2 * HD), jnp.bfloat16),
            pltpu.VMEM((2 * TQ, HD), jnp.float32),
            pltpu.VMEM((2 * TQ, 2 * HD), jnp.float32),
            pltpu.VMEM((SHARD, 2 * HD), jnp.bfloat16),
            pltpu.SemaphoreType.DMA((10,)),
        ],
        compiler_params=pltpu.CompilerParams(vmem_limit_bytes=60 << 20),
        cost_estimate=pl.CostEstimate(
            flops=blocks * 32 * HD * SHARD * SHARD, bytes_accessed=8 << 20, transcendentals=blocks * 2 * SHARD * SHARD
        ),
        name="attend_own" if final else "attend_sent",
    )(meta, lengths, *pieces, *q)


def merge_kernel(meta_ref, first_ref, second_ref, own_ref, lse_ref, out_ref):
    high = meta_ref[0] > 0
    half = first_ref.shape[0]
    for n, sent_ref in enumerate((first_ref, second_ref)):
        rs = pl.ds(n * half, half)
        for head in range(2):
            hs = pl.ds(head * HD, HD)
            parts = sent_ref[:, (2 + head) * HD : (3 + head) * HD].astype(jnp.float32)
            sent = parts[:, 0:1] + parts[:, 1:2] + parts[:, 2:3]
            sent = jnp.where(high, sent, NEVER)
            here = lse_ref[rs, hs]
            top = jnp.maximum(sent, here)
            w_sent = jnp.exp2(sent - top)
            w_here = jnp.exp2(here - top)
            o = w_sent * sent_ref[:, hs].astype(jnp.float32) + w_here * own_ref[rs, hs]
            out_ref[rs, hs] = (o / (w_sent + w_here)).astype(jnp.bfloat16)


def merge(meta, first, second, own, lse):
    return pl.pallas_call(
        merge_kernel,
        out_shape=jax.ShapeDtypeStruct(own.shape, jnp.bfloat16),
        in_specs=[SM, VM, VM, VM, VM],
        out_specs=VM,
        compiler_params=pltpu.CompilerParams(vmem_limit_bytes=32 << 20),
        name="merge",
    )(meta, first, second, own, lse)


def slots_kernel(capacity, ids_ref, weights_ref, place_ref, shares_ref):
    rows, top = ids_ref.shape
    experts = 128
    ids = ids_ref[...]
    lane = lax.broadcasted_iota(jnp.int32, (rows, experts), 1)
    named = [(ids[:, k : k + 1] == lane).astype(jnp.float32) for k in range(top)]
    chosen = functools.reduce(jnp.add, named).astype(jnp.bfloat16)
    before = (
        lax.broadcasted_iota(jnp.int32, (rows, rows), 1)
        < lax.broadcasted_iota(jnp.int32, (rows, rows), 0)
    ).astype(jnp.bfloat16)
    rank = jnp.dot(before, chosen, preferred_element_type=jnp.float32)
    slot = [jnp.sum(one * rank, axis=1, keepdims=True) for one in named]
    place_ref[...] = ids * capacity + jnp.concatenate(slot, axis=1).astype(jnp.int32)
    weights = weights_ref[...]
    shares_ref[...] = weights / jnp.sum(weights, axis=1, keepdims=True)

def slots(ids, weights, capacity):
    return pl.pallas_call(
        functools.partial(slots_kernel, capacity),
        out_shape=(jax.ShapeDtypeStruct(ids.shape, jnp.int32), jax.ShapeDtypeStruct(weights.shape, jnp.float32)),
        in_specs=[VM, VM], out_specs=(VM, VM), name="slots",
    )(ids, weights)

def pack_kernel(
    meta_ref, place_ref, attended_ref, near_ref, far_ref, stream_ref, gain_ref, residual_ref, out_ref, rows32
):
    rows, width = stream_ref.shape
    parts = width // LANES
    upper = meta_ref[0] > 0
    near, far = [], []
    for e in range(attended_ref.shape[0]):
        a, b = attended_ref[e, :, :LANES], attended_ref[e, :, LANES:]
        near.append(jnp.where(upper, b, a))
        far.append(jnp.where(upper, a, b))
    projected = jnp.dot(
        jnp.concatenate(near, axis=1), near_ref[...], preferred_element_type=jnp.float32
    ) + jnp.dot(jnp.concatenate(far, axis=1), far_ref[...], preferred_element_type=jnp.float32)
    residual = stream_ref[...].astype(jnp.float32) + projected
    spread = lax.rsqrt(jnp.mean(residual * residual, axis=1, keepdims=True) + 1e-06)
    normed = residual * spread * gain_ref[...].astype(jnp.float32)
    residual_ref[...] = residual.reshape(rows, parts, LANES)
    rows32[...] = normed.astype(jnp.bfloat16).reshape(rows, parts, LANES)
    out_ref[...] = jnp.zeros_like(out_ref)

    def one(t, _):
        row = rows32[t]
        for k in range(8):
            out_ref[place_ref[t * 8 + k]] = row
        return 0
    lax.fori_loop(0, rows, one, 0, unroll=4)

def pack(meta, place, attended, near, far, stream, gain, slots_count):
    rows, width = stream.shape
    parts = width // LANES
    return pl.pallas_call(
        pack_kernel,
        out_shape=(
            jax.ShapeDtypeStruct((rows, parts, LANES), jnp.float32),
            jax.ShapeDtypeStruct((slots_count, parts, LANES), jnp.bfloat16),
        ),
        in_specs=[SM, SM] + [VM] * 5,
        out_specs=(VM, VM),
        scratch_shapes=[pltpu.VMEM((rows, parts, LANES), jnp.bfloat16)],
        compiler_params=pltpu.CompilerParams(vmem_limit_bytes=32 << 20),
        name="pack",
    )(meta, place, attended, near, far, stream, gain)


TR = 384


def experts_kernel(x_ref, gate_ref, up_ref, down_ref, out_ref):
    rows, parts, lanes = x_ref.shape
    x = x_ref[...].reshape(rows, parts * lanes)
    gate = jnp.dot(x, gate_ref[0], preferred_element_type=jnp.float32)
    upper = jnp.dot(x, up_ref[0], preferred_element_type=jnp.float32)
    hidden = (gate / (1.0 + jnp.exp(-gate)) * upper).astype(jnp.bfloat16)
    result = jnp.dot(hidden, down_ref[0], preferred_element_type=jnp.float32)
    out_ref[...] = result.astype(jnp.bfloat16).reshape(rows, parts, lanes)


def experts(x, gate, up, down):
    count, parts, lanes = x.shape
    return pl.pallas_call(
        experts_kernel,
        out_shape=jax.ShapeDtypeStruct(x.shape, jnp.bfloat16),
        grid=(count // TR,),
        in_specs=[
            pl.BlockSpec((TR, parts, lanes), lambda i: (i, 0, 0)),
            VM,
            VM,
            VM,
        ],
        out_specs=pl.BlockSpec((TR, parts, lanes), lambda i: (i, 0, 0)),
        compiler_params=pltpu.CompilerParams(vmem_limit_bytes=36 << 20),
        name="experts",
    )(x, gate, up, down)


def combine_kernel(place_ref, shares_ref, residual_ref, back_ref, out_ref, total):
    rows, parts, lanes = residual_ref.shape
    def one(t, _):
        acc = residual_ref[t]
        for k in range(8):
            acc = acc + shares_ref[t * 8 + k] * back_ref[place_ref[t * 8 + k]].astype(jnp.float32)
        total[t] = acc.astype(jnp.bfloat16)
        return 0
    lax.fori_loop(0, rows, one, 0, unroll=2)
    out_ref[...] = total[...].reshape(rows, parts * lanes)

def combine(place, shares, residual, back):
    rows, parts, lanes = residual.shape
    return pl.pallas_call(
        combine_kernel,
        out_shape=jax.ShapeDtypeStruct((rows, parts * lanes), jnp.bfloat16),
        in_specs=[SM, SM, VM, VM], out_specs=VM,
        scratch_shapes=[pltpu.VMEM((rows, parts, lanes), jnp.bfloat16)],
        compiler_params=pltpu.CompilerParams(vmem_limit_bytes=48 << 20),
        name="combine",
    )(place, shares, residual, back)


def permute(x, move):
    pairs = []
    for n in range(128):
        ctx, exp = divmod(n, 8)
        x_lo, z, core = ctx // 8, ctx // 2 % 4, ctx % 2
        y, x_hi = exp // 2, exp % 2
        target = move(x_hi * 2 + x_lo, y, z, core)
        if target is None:
            continue
        tx, ty, tz, tc = target
        tx, ty, tz = tx % 4, ty % 4, tz % 4
        pairs.append((n, ((tx % 2) * 8 + tz * 2 + tc) * 8 + ty * 2 + tx // 2))
    return lax.ppermute(x, ("ctx", "exp"), pairs)


def along_z(a, step):
    return permute(a, lambda x, y, z, c: (x, y, z + step, c))


def along_y(a, step):
    return permute(a, lambda x, y, z, c: (x, y + step, z, c))


def other_core(a):
    return permute(a, lambda x, y, z, c: (x, y, z, 1 - c))


def down_x(a, step):
    return permute(a, lambda x, y, z, c: (x + step, y, z, c) if x % 2 == 1 else None)


def back_x(a, step):
    return permute(a, lambda x, y, z, c: (x + step, y, z, c) if x % 2 == 0 else None)


def on_device(
    stream,
    queries,
    keys,
    values,
    out_proj,
    norm_gain,
    gate_proj,
    up_proj,
    down_proj,
    expert_ids,
    route_weights,
    segment_lengths,
):
    ctx_count = lax.axis_size("ctx")
    exp_count = lax.axis_size("exp")
    ctx_index = lax.axis_index("ctx").astype(jnp.int32)
    exp_index = lax.axis_index("exp").astype(jnp.int32)
    rows_ctx = queries.shape[0]
    expert_count = ctx_count * exp_count
    tok_rows, top_count = expert_ids.shape
    capacity = max(2, tok_rows * top_count * 9 // (expert_count * 8))
    x_lo, z, core = ctx_index // 8, ctx_index // 2 % 4, ctx_index % 2
    y = exp_index // 2
    own = jnp.concatenate(
        [lax.dynamic_slice_in_dim(keys, y * HD, HD, 1), lax.dynamic_slice_in_dim(values, y * HD, HD, 1)],
        axis=1,
    )
    middle = rows_ctx // 2
    up, down = along_z(own, 1), along_z(own, -1)
    q_sent = (down_x(queries[:middle], -1), down_x(queries[middle:], 1))
    far_a, far_b = along_z(up[:middle], 1), along_z(down[middle:], -1)
    near = (own, up, down, far_a, far_b)
    pieces = near + tuple(other_core(piece) for piece in near)

    mine = lax.dynamic_slice_in_dim(out_proj, core * LANES, LANES, 0)
    w_near = lax.all_gather(mine, "exp", axis=0, tiled=True)

    place, shares = slots(expert_ids, route_weights, capacity)
    place = place.reshape(-1)
    shares = shares.reshape(-1)

    low = x_lo * HALF
    one = jnp.int32(1)
    meta_sent = jnp.stack([(ctx_index + HALF) * rows_ctx, low, one - x_lo, z, core])
    meta_own = jnp.stack([ctx_index * rows_ctx, low, one, z, core])
    sent = attend(False, meta_sent, segment_lengths, q_sent, pieces, 4)
    meta_own, first, second = lax.optimization_barrier((meta_own, *sent))
    first, second = back_x(first, 1), back_x(second, -1)
    partial, lse = attend(True, meta_own, segment_lengths, (queries,), pieces, 5)
    attended = merge(x_lo.reshape(1), first, second, partial, lse)
    w_near, attended = lax.optimization_barrier((w_near, attended))
    w_far = other_core(w_near)
    spread = lax.all_to_all(
        attended.reshape(exp_count, tok_rows, 2 * HD), "exp", split_axis=0, concat_axis=0, tiled=True
    )
    residual, outgoing = pack(
        core.reshape(1),
        place,
        spread,
        w_near,
        w_far,
        stream,
        norm_gain.reshape(1, -1),
        expert_count * capacity,
    )
    shape = (expert_count, capacity) + outgoing.shape[1:]
    arrived = lax.all_to_all(
        outgoing.reshape(shape), ("ctx", "exp"), split_axis=0, concat_axis=0, tiled=True
    )
    results = experts(arrived.reshape(outgoing.shape), gate_proj, up_proj, down_proj)
    returned = lax.all_to_all(
        results.reshape(shape), ("ctx", "exp"), split_axis=0, concat_axis=0, tiled=True
    )
    return combine(place, shares, residual, returned.reshape(outgoing.shape))


def solution(mesh):
    placed = (
        P(("ctx", "exp"), None),
        P("ctx", "exp"),
        P("ctx", None),
        P("ctx", None),
        P("exp", None),
        P(),
        P(("ctx", "exp"), None, None),
        P(("ctx", "exp"), None, None),
        P(("ctx", "exp"), None, None),
        P(("ctx", "exp"), None),
        P(("ctx", "exp"), None),
        P(),
    )
    return jax.shard_map(
        on_device, mesh=mesh, in_specs=placed, out_specs=P(("ctx", "exp"), None), check_vma=False
    )
```

time: 378 us -> 276 us (0.73)
  waiting for transfers between devices: 229 us -> 107 us
  starting transfers between devices: 5.96 us -> 23.1 us
  local copies, waits for them, and re-layouts: 6.41 us -> 14.8 us
    reduce_scatter x1 -> x0, waiting for transfers between devices: 116 us -> none  [on_device(): lax.psum_scatter(jnp.dot(attended, out_proj, preferred_element_type=jnp.f...]
    all_gather x1, waiting for transfers between devices: 55.1 us -> 8.32 us  [on_device(): w_near = lax.all_gather(mine, 'exp', axis=0, tiled=True)]
    ppermute x0 -> x14, waiting for transfers between devices: none -> 32.4 us  [permute(): return lax.ppermute(x, ('ctx', 'exp'), pairs)]
    pallas_call x1 -> x3, Pallas kernels: 9.11 us -> 27.8 us  [the longest x2 26.1 us: attend(): pl.pallas_call(functools.partial(attend_part, final), out_shape=shapes, i...]
    pallas_call x1, Pallas kernels: 30.1 us -> 12.9 us  [experts(): pl.pallas_call(experts_kernel, out_shape=jax.ShapeDtypeStruct(x.shape, jn...]
    ppermute x0 -> x14, starting transfers between devices: none -> 13.4 us  [permute(): return lax.ppermute(x, ('ctx', 'exp'), pairs)]
    all_to_all x0 -> x1, waiting for transfers between devices: none -> 7.78 us  [on_device(): lax.all_to_all(attended.reshape(exp_count, tok_rows, 2 * HD), 'exp', spli...]
    unnamed x20 -> x40, local copies, waits for them, and re-layouts: 4.22 us -> 9.52 us
  transfers between devices with their start and end apart: 3 -> 17, of which waited for: 3 -> 10; matrix products, arithmetic and copies ran while one was open for 1% -> 2% of each run, Pallas kernels for 1% -> 11%
where the time goes in v2:
time: 276 us
  waiting for transfers between devices  107 us (39%)
  blocking collectives  64.2 us (23%)
  Pallas kernels  53.9 us (20%)
  starting transfers between devices  23.1 us (8%)
  local copies, waits for them, and re-layouts  14.8 us (5%)
  between operations  13.7 us (5%)
    all_to_all x1, blocking collectives, on_device(): lax.all_to_all(outgoing.reshape(shape), ('ctx', 'exp'), split_axis=0, con...  64.2 us
    all_to_all x1, waiting for transfers between devices, on_device(): lax.all_to_all(results.reshape(shape), ('ctx', 'exp'), split_axis=0, conc...  58.2 us
    ppermute x14, waiting for transfers between devices, permute(): return lax.ppermute(x, ('ctx', 'exp'), pairs)  32.4 us
    pallas_call x2, Pallas kernels, attend(): pl.pallas_call(functools.partial(attend_part, final), out_shape=shapes, i...  26.1 us
    ppermute x14, starting transfers between devices, permute(): return lax.ppermute(x, ('ctx', 'exp'), pairs)  13.4 us
    pallas_call x1, Pallas kernels, experts(): pl.pallas_call(experts_kernel, out_shape=jax.ShapeDtypeStruct(x.shape, jn...  12.9 us
    unnamed x40, local copies, waits for them, and re-layouts  9.52 us
    all_gather x1, waiting for transfers between devices, on_device(): w_near = lax.all_gather(mine, 'exp', axis=0, tiled=True)  8.32 us
  transfers between devices with their start and end apart: 17, of which 10 were waited for; matrix products, arithmetic and copies ran while one was open for 2% of the time, Pallas kernels for 11%

profile of v2, /device:TPU:0, one launch (start us, length us, event | category | flops | bytes accessed | tf_op | source)
XLA Modules:
  0.0 276.5 jit_solution(17238361626385160189)
XLA Ops:
  6.5 1.2 copy-done
  7.8 0.8 constant_dynamic-slice_fusion.2
  8.6 0.0 all-gather.2.cloned.1.call-update
  8.6 1.1 constant_dynamic-slice_fusion
  9.7 0.1 pad_maximum_fusion.refs_0_
  9.8 0.0 copy-start.9
  9.8 4.2 %collective-permute-start.1 = (bf16[1024,256]{1,0:T(8,128)(2,1)S(1)}, bf16[1024,256]{1,0:T(8,128)(2,1)S(1)}, u32[]{:S(2)}, u32[]{:S(2)}) collective-permute-start(bf16[1024,256]{1,0:T(8,128)(2,1)S(1)} %pad_maximum_fusion.refs_0_), channel_id=1, source_target_pairs={{0,48},{1,49},{2,50},{3,51},{4,52},{5,53},{6,54},{7,55},{8,56},{9,... | collective-permute-start | bytes 1572872 | tf_op jit(solution)/shard_map/ppermute | solution.py:349
  14.0 0.0 collective-permute-start
  14.0 1.1 fusion
  15.1 1.3 collective-permute-start.10
  16.4 1.3 collective-permute-start.9
  17.7 0.1 collective-permute-start.4
  17.7 7.4 %collective-permute-done.1.refs_2_ = bf16[1024,256]{1,0:T(8,128)(2,1)S(1)} collective-permute-done((bf16[1024,256]{1,0:T(8,128)(2,1)S(1)}, bf16[1024,256]{1,0:T(8,128)(2,1)S(1)}, u32[]{:S(2)}, u32[]{:S(2)}) %collective-permute-start.1) | collective-permute-done | bytes 524320 | tf_op jit(solution)/shard_map/ppermute | solution.py:349
  25.2 3.8 %collective-permute-start.3 = (bf16[512,256]{1,0:T(8,128)(2,1)S(1)}, bf16[512,256]{1,0:T(8,128)(2,1)S(1)}, u32[]{:S(2)}, u32[]{:S(2)}) collective-permute-start(bf16[512,256]{1,0:T(8,128)(2,1)S(1)} %slice.17), channel_id=1, source_target_pairs={{0,48},{1,49},{2,50},{3,51},{4,52},{5,53},{6,54},{7,55},{8,56},{9,... | collective-permute-start | bytes 786440 | tf_op jit(solution)/shard_map/ppermute | solution.py:349
  29.0 0.0 collective-permute-done.refs_1_
  29.0 0.1 collective-permute-start.2
  29.1 0.0 collective-permute-done.10.refs_11_
  29.1 0.1 collective-permute-start.6
  29.2 1.2 collective-permute-done.9.refs_10_
  30.4 0.0 collective-permute-start.5
  30.4 3.3 %collective-permute-done.3.refs_4_ = bf16[512,256]{1,0:T(8,128)(2,1)S(1)} collective-permute-done((bf16[512,256]{1,0:T(8,128)(2,1)S(1)}, bf16[512,256]{1,0:T(8,128)(2,1)S(1)}, u32[]{:S(2)}, u32[]{:S(2)}) %collective-permute-start.3) | collective-permute-done | bytes 262176 | tf_op jit(solution)/shard_map/ppermute | solution.py:349
  33.6 0.0 collective-permute-start.8
  33.7 3.6 %collective-permute-done.2.refs_3_ = bf16[512,256]{1,0:T(8,128)(2,1)} collective-permute-done((bf16[512,256]{1,0:T(8,128)(2,1)S(1)}, bf16[512,256]{1,0:T(8,128)(2,1)}, u32[]{:S(2)}, u32[]{:S(2)}) %collective-permute-start.2) | collective-permute-done | bytes 262176 | tf_op jit(solution)/shard_map/ppermute | solution.py:349
  37.3 0.0 collective-permute-start.7
  37.3 0.6 stack.31.meta_ref
  37.9 0.7 stack.28.meta_ref
  38.6 0.0 collective-permute-done.4.refs_5_
  38.6 0.0 collective-permute-done.8.refs_9_
  38.6 0.0 collective-permute-done.6.refs_7_
  38.6 0.6 collective-permute-done.7.refs_8_
  39.2 17.7 %attend_sent.1 = (bf16[512,512]{1,0:T(8,128)(2,1)}, bf16[512,512]{1,0:T(8,128)(2,1)}) custom-call(s32[5]{0:T(128)} %stack.31.meta_ref, s32[17]{0:T(128)} %lengths_ref.3, bf16[1024,256]{1,0:T(8,128)(2,1)} %copy-done.9, bf16[1024,256]{1,0:T(8,128)(2,1)} %copy-done.11, bf16[1024,256]{1,0:T(8,128)(2,1)} %copy-done.10, ...), custom_call_target="tpu_custom_call" | custom-call | flops 17179869184 | bytes 8388608 | tf_op jit(solution)/shard_map/attend_sent/pallas_call | solution.py:164
  56.9 1.3 collective-permute-start.11
  58.3 1.3 collective-permute-start.12
  59.6 0.0 copy-start.14
  59.6 0.0 copy-start.15
  59.6 0.0 copy-start.8
  59.6 8.4 %attend_own.1 = (f32[1024,256]{1,0:T(8,128)}, f32[1024,256]{1,0:T(8,128)}) custom-call(s32[5]{0:T(128)} %stack.28.meta_ref, s32[17]{0:T(128)} %lengths_ref.3, bf16[1024,256]{1,0:T(8,128)(2,1)} %copy-done.9, bf16[1024,256]{1,0:T(8,128)(2,1)} %copy-done.11, bf16[1024,256]{1,0:T(8,128)(2,1)} %copy-done.10, bf16[512,256]{1,0:T(8,128)(2,1)} %collective-permute-done.2.refs_3_, ...), custom_call_target="tpu_custom_call" | custom-call | flops 21474836480 | bytes 8388608 | tf_op jit(solution)/shard_map/attend_own/pallas_call | solution.py:164
  68.0 0.0 copy-start.13
  68.0 13.8 %collective-permute-done.11.first_ref = bf16[512,512]{1,0:T(8,128)(2,1)S(1)} collective-permute-done((bf16[512,512]{1,0:T(8,128)(2,1)}, bf16[512,512]{1,0:T(8,128)(2,1)S(1)}, u32[]{:S(2)}, u32[]{:S(2)}) %collective-permute-start.11) | collective-permute-done | bytes 524320 | tf_op jit(solution)/shard_map/ppermute | solution.py:349
  81.9 2.5 collective-permute-done.12.second_ref
  84.4 1.2 copy-done.6
  85.6 1.2 copy-done.7
  86.8 1.7 merge.1
  88.5 8.3 %all-gather.2.cloned.1.call-done.near_ref = bf16[1024,2048]{1,0:T(8,128)(2,1)} async-done(((bf16[128,2048]{1,0:T(8,128)(2,1)}), bf16[1024,2048]{1,0:T(8,128)(2,1)}) %all-gather.2.cloned.1.call-update) | async-done | bytes 4194320 | tf_op jit(solution)/shard_map/all_gather | solution.py:408
  96.8 0.0 collective-permute-start.13
  96.8 3.7 %all-to-all-start = ((bf16[8,128,256]{2,1,0:T(8,128)(2,1)}), bf16[8,128,256]{2,1,0:T(8,128)(2,1)S(1)}, u32[]{:S(2)}, u32[]{:S(2)}) async-start(bf16[8,128,256]{2,1,0:T(8,128)(2,1)} %bitcast.7), calls=%async_computation | async-start | bytes 1048576 | tf_op jit(solution)/shard_map/all_to_all | solution.py:425
  100.6 0.7 copy.15.ids_ref
  101.3 0.7 copy.16.weights_ref
  102.0 2.1 slots.1
  104.1 0.9 reshape.30.place_ref
  105.0 7.8 %all-to-all-done.attended_ref = bf16[8,128,256]{2,1,0:T(8,128)(2,1)S(1)} async-done(((bf16[8,128,256]{2,1,0:T(8,128)(2,1)}), bf16[8,128,256]{2,1,0:T(8,128)(2,1)S(1)}, u32[]{:S(2)}, u32[]{:S(2)}) %all-to-all-start) | async-done | bytes 524320 | tf_op jit(solution)/shard_map/all_to_all | solution.py:425
  112.8 0.0 collective-permute-done.13.far_ref
  112.8 2.2 copy-done.2
  115.0 5.9 %pack.1 = (f32[128,16,128]{2,1,0:T(8,128)S(1)}, bf16[1152,16,128]{2,1,0:T(8,128)(2,1)S(1)}) custom-call(s32[1]{0:T(128)} %bitcast.meta_ref, s32[1024]{0:T(1024)S(1)} %reshape.30.place_ref, bf16[8,128,256]{2,1,0:T(8,128)(2,1)S(1)} %all-to-all-done.attended_ref, bf16[1024,2048]{1,0:T(8,128)(2,1)S(1)} %copy-done.2, ...), custom_call_target="tpu_custom_call" | custom-call | tf_op jit(solution)/shard_map/pack/pallas_call | solution.py:269
  120.9 0.0 copy-start.3
  120.9 0.0 copy-start.4
  120.9 0.0 copy-start.5
  120.9 64.2 %all_to_all.15 = bf16[128,9,16,128]{3,2,1,0:T(8,128)(2,1)} all-to-all(bf16[128,9,16,128]{3,2,1,0:T(8,128)(2,1)S(1)} %bitcast.13), channel_id=1, replica_groups=mesh['ctx'=16,'exp'=8] {'ctx','exp'}, dimensions={0} | all-to-all | bytes 9437184 | tf_op jit(solution)/shard_map/all_to_all | solution.py:439
  185.1 12.9 %experts.1 = bf16[1152,16,128]{2,1,0:T(8,128)(2,1)S(1)} custom-call(bf16[1152,16,128]{2,1,0:T(8,128)(2,1)} %bitcast.14, bf16[1,2048,768]{2,1,0:T(8,128)(2,1)S(1)} %copy-done.3, bf16[1,2048,768]{2,1,0:T(8,128)(2,1)S(1)} %copy-done.4, bf16[1,768,2048]{2,1,0:T(8,128)(2,1)S(1)} %copy-done.5), custom_call_target="tpu_custom_call" | custom-call | tf_op jit(solution)/shard_map/experts/pallas_call | solution.py:298
  198.1 2.2 copy-done.1
  200.2 5.9 %all-to-all-start.2 = ((bf16[128,9,16,128]{3,2,1,0:T(8,128)(2,1)}), bf16[128,9,16,128]{3,2,1,0:T(8,128)(2,1)}, u32[]{:S(2)}, u32[]{:S(2)}) async-start(bf16[128,9,16,128]{3,2,1,0:T(8,128)(2,1)} %bitcast.12), calls=%async_computation.2 | async-start | bytes 9437184 | tf_op jit(solution)/shard_map/all_to_all | solution.py:443
  206.1 0.1 reshape.31.shares_ref
  206.2 58.2 %all-to-all-done.2 = bf16[128,9,16,128]{3,2,1,0:T(8,128)(2,1)} async-done(((bf16[128,9,16,128]{3,2,1,0:T(8,128)(2,1)}), bf16[128,9,16,128]{3,2,1,0:T(8,128)(2,1)}, u32[]{:S(2)}, u32[]{:S(2)}) %all-to-all-start.2) | async-done | bytes 4718624 | tf_op jit(solution)/shard_map/all_to_all | solution.py:443
  264.4 5.2 %combine.1 = bf16[128,2048]{1,0:T(8,128)(2,1)} custom-call(s32[1024]{0:T(1024)S(1)} %reshape.30.place_ref, f32[1024]{0:T(1024)S(1)} %reshape.31.shares_ref, f32[128,16,128]{2,1,0:T(8,128)S(1)} %get-tuple-element.29.residual_ref, bf16[1152,16,128]{2,1,0:T(8,128)(2,1)} %bitcast.11.back_ref), custom_call_target="tpu_custom_call" | custom-call | tf_op jit(solution)/shard_map/combine/pallas_call | solution.py:327
  (30 shorter events, 0.1 us)
Async XLA Ops:
  6.5 1.2 copy-start
  6.5 90.3 %all-gather.2.cloned.1.call-start = ((), (), s32[]{:S(2)}) async-start(), calls=%async_computation.3 | async-start | bytes 4718592 | tf_op jit(solution)/shard_map/all_gather | solution.py:408
  9.8 29.4 %copy-start.9 = (bf16[1024,256]{1,0:T(8,128)(2,1)}, bf16[1024,256]{1,0:T(8,128)(2,1)S(1)}, u32[]{:S(2)}) copy-start(bf16[1024,256]{1,0:T(8,128)(2,1)S(1)} %pad_maximum_fusion.refs_0_) | copy-start | bytes 1572868
  9.8 15.4 %collective-permute-start.1 = (bf16[1024,256]{1,0:T(8,128)(2,1)S(1)}, bf16[1024,256]{1,0:T(8,128)(2,1)S(1)}, u32[]{:S(2)}, u32[]{:S(2)}) collective-permute-start(bf16[1024,256]{1,0:T(8,128)(2,1)S(1)} %pad_maximum_fusion.refs_0_), channel_id=1, source_target_pairs={{0,48},{1,49},{2,50},{3,51},{4,52},{5,53},{6,54},{7,55},{8,56},{9,... | collective-permute-start | bytes 1572872 | tf_op jit(solution)/shard_map/ppermute | solution.py:349
  14.0 15.0 %collective-permute-start = (bf16[1024,256]{1,0:T(8,128)(2,1)S(1)}, bf16[1024,256]{1,0:T(8,128)(2,1)S(1)}, u32[]{:S(2)}, u32[]{:S(2)}) collective-permute-start(bf16[1024,256]{1,0:T(8,128)(2,1)S(1)} %pad_maximum_fusion.refs_0_), channel_id=1, source_target_pairs={{0,16},{1,17},{2,18},{3,19},{4,20},{5,21},{6,22},{7,23},{8,24},{9,... | collective-permute-start | bytes 1572872 | tf_op jit(solution)/shard_map/ppermute | solution.py:349
  15.1 14.0 %collective-permute-start.10 = (bf16[512,256]{1,0:T(8,128)(2,1)S(1)}, bf16[512,256]{1,0:T(8,128)(2,1)S(1)}, u32[]{:S(2)}, u32[]{:S(2)}) collective-permute-start(bf16[512,256]{1,0:T(8,128)(2,1)S(1)} %get-tuple-element.31), channel_id=1, source_target_pairs={{64,1},{65,0},{66,3},{67,2},{68,5},{69,4},{70,7},{71,6},{72,9},{73... | collective-permute-start | bytes 786440 | tf_op jit(solution)/shard_map/ppermute | solution.py:349
  16.4 14.0 %collective-permute-start.9 = (bf16[512,256]{1,0:T(8,128)(2,1)S(1)}, bf16[512,256]{1,0:T(8,128)(2,1)S(1)}, u32[]{:S(2)}, u32[]{:S(2)}) collective-permute-start(bf16[512,256]{1,0:T(8,128)(2,1)S(1)} %get-tuple-element.32), channel_id=1, source_target_pairs={{64,0},{65,1},{66,2},{67,3},{68,4},{69,5},{70,6},{71,7},{72,8},{73... | collective-permute-start | bytes 786440 | tf_op jit(solution)/shard_map/ppermute | solution.py:349
  17.7 20.9 %collective-permute-start.4 = (bf16[1024,256]{1,0:T(8,128)(2,1)S(1)}, bf16[1024,256]{1,0:T(8,128)(2,1)}, u32[]{:S(2)}, u32[]{:S(2)}) collective-permute-start(bf16[1024,256]{1,0:T(8,128)(2,1)S(1)} %pad_maximum_fusion.refs_0_), channel_id=1, source_target_pairs={{0,8},{1,9},{2,10},{3,11},{4,12},{5,13},{6,14},{7,15},{8,0},{9,1},... | collective-permute-start | bytes 1572872 | tf_op jit(solution)/shard_map/ppermute | solution.py:349
  25.2 14.0 %copy-start.10 = (bf16[1024,256]{1,0:T(8,128)(2,1)}, bf16[1024,256]{1,0:T(8,128)(2,1)S(1)}, u32[]{:S(2)}) copy-start(bf16[1024,256]{1,0:T(8,128)(2,1)S(1)} %collective-permute-done.1.refs_2_) | copy-start | bytes 1572868
  25.2 8.5 %collective-permute-start.3 = (bf16[512,256]{1,0:T(8,128)(2,1)S(1)}, bf16[512,256]{1,0:T(8,128)(2,1)S(1)}, u32[]{:S(2)}, u32[]{:S(2)}) collective-permute-start(bf16[512,256]{1,0:T(8,128)(2,1)S(1)} %slice.17), channel_id=1, source_target_pairs={{0,48},{1,49},{2,50},{3,51},{4,52},{5,53},{6,54},{7,55},{8,56},{9,... | collective-permute-start | bytes 786440 | tf_op jit(solution)/shard_map/ppermute | solution.py:349
  29.0 10.2 %copy-start.11 = (bf16[1024,256]{1,0:T(8,128)(2,1)}, bf16[1024,256]{1,0:T(8,128)(2,1)S(1)}, u32[]{:S(2)}) copy-start(bf16[1024,256]{1,0:T(8,128)(2,1)S(1)} %collective-permute-done.refs_1_) | copy-start | bytes 1572868
  29.0 8.3 %collective-permute-start.2 = (bf16[512,256]{1,0:T(8,128)(2,1)S(1)}, bf16[512,256]{1,0:T(8,128)(2,1)}, u32[]{:S(2)}, u32[]{:S(2)}) collective-permute-start(bf16[512,256]{1,0:T(8,128)(2,1)S(1)} %slice.16), channel_id=1, source_target_pairs={{0,16},{1,17},{2,18},{3,19},{4,20},{5,21},{6,22},{7,23},{8,24},{9,... | collective-permute-start | bytes 786440 | tf_op jit(solution)/shard_map/ppermute | solution.py:349
  29.1 10.1 %copy-start.17 = (bf16[512,256]{1,0:T(8,128)(2,1)}, bf16[512,256]{1,0:T(8,128)(2,1)S(1)}, u32[]{:S(2)}) copy-start(bf16[512,256]{1,0:T(8,128)(2,1)S(1)} %collective-permute-done.10.refs_11_) | copy-start | bytes 786436
  29.1 9.5 %collective-permute-start.6 = (bf16[1024,256]{1,0:T(8,128)(2,1)S(1)}, bf16[1024,256]{1,0:T(8,128)(2,1)}, u32[]{:S(2)}, u32[]{:S(2)}) collective-permute-start(bf16[1024,256]{1,0:T(8,128)(2,1)S(1)} %collective-permute-done.1.refs_2_), channel_id=1, source_target_pairs={{0,8},{1,9},{2,10},{3,11},{4,12},{5,13},{6,14},{7,15},{8,0},{9,1},... | collective-permute-start | bytes 1572872 | tf_op jit(solution)/shard_map/ppermute | solution.py:349
  30.4 8.8 %copy-start.18 = (bf16[512,256]{1,0:T(8,128)(2,1)}, bf16[512,256]{1,0:T(8,128)(2,1)S(1)}, u32[]{:S(2)}) copy-start(bf16[512,256]{1,0:T(8,128)(2,1)S(1)} %collective-permute-done.9.refs_10_) | copy-start | bytes 786436
  30.4 8.8 %collective-permute-start.5 = (bf16[1024,256]{1,0:T(8,128)(2,1)S(1)}, bf16[1024,256]{1,0:T(8,128)(2,1)}, u32[]{:S(2)}, u32[]{:S(2)}) collective-permute-start(bf16[1024,256]{1,0:T(8,128)(2,1)S(1)} %collective-permute-done.refs_1_), channel_id=1, source_target_pairs={{0,8},{1,9},{2,10},{3,11},{4,12},{5,13},{6,14},{7,15},{8,0},{9,1},... | collective-permute-start | bytes 1572872 | tf_op jit(solution)/shard_map/ppermute | solution.py:349
  33.6 5.5 %copy-start.16 = (bf16[512,256]{1,0:T(8,128)(2,1)}, bf16[512,256]{1,0:T(8,128)(2,1)S(1)}, u32[]{:S(2)}) copy-start(bf16[512,256]{1,0:T(8,128)(2,1)S(1)} %collective-permute-done.3.refs_4_) | copy-start | bytes 786436
  33.6 4.9 %collective-permute-start.8 = (bf16[512,256]{1,0:T(8,128)(2,1)S(1)}, bf16[512,256]{1,0:T(8,128)(2,1)}, u32[]{:S(2)}, u32[]{:S(2)}) collective-permute-start(bf16[512,256]{1,0:T(8,128)(2,1)S(1)} %collective-permute-done.3.refs_4_), channel_id=1, source_target_pairs={{0,8},{1,9},{2,10},{3,11},{4,12},{5,13},{6,14},{7,15},{8,0},{9,1},... | collective-permute-start | bytes 786440 | tf_op jit(solution)/shard_map/ppermute | solution.py:349
  37.3 1.9 collective-permute-start.7
  56.9 24.9 %collective-permute-start.11 = (bf16[512,512]{1,0:T(8,128)(2,1)}, bf16[512,512]{1,0:T(8,128)(2,1)S(1)}, u32[]{:S(2)}, u32[]{:S(2)}) collective-permute-start(bf16[512,512]{1,0:T(8,128)(2,1)} %get-tuple-element.22), channel_id=1, source_target_pairs={{0,64},{1,65},{2,66},{3,67},{4,68},{5,69},{6,70},{7,71},{8,72},{9,... | collective-permute-start | bytes 1572872 | tf_op jit(solution)/shard_map/ppermute | solution.py:349
  58.3 26.1 %collective-permute-start.12 = (bf16[512,512]{1,0:T(8,128)(2,1)}, bf16[512,512]{1,0:T(8,128)(2,1)S(1)}, u32[]{:S(2)}, u32[]{:S(2)}) collective-permute-start(bf16[512,512]{1,0:T(8,128)(2,1)} %get-tuple-element.23), channel_id=1, source_target_pairs={{0,65},{1,64},{2,67},{3,66},{4,69},{5,68},{6,71},{7,70},{8,73},{9,... | collective-permute-start | bytes 1572872 | tf_op jit(solution)/shard_map/ppermute | solution.py:349
  59.6 41.0 %copy-start.14 = (s32[128,8]{0,1:T(8,128)S(1)}, s32[128,8]{0,1:T(8,128)}, u32[]{:S(2)}) copy-start(s32[128,8]{0,1:T(8,128)} %param.21) | copy-start | bytes 12292
  59.6 41.7 %copy-start.15 = (f32[128,8]{0,1:T(8,128)S(1)}, f32[128,8]{0,1:T(8,128)}, u32[]{:S(2)}) copy-start(f32[128,8]{0,1:T(8,128)} %param.22) | copy-start | bytes 12292
  59.6 53.2 %copy-start.8 = (bf16[128,2048]{1,0:T(8,128)(2,1)S(1)}, bf16[128,2048]{1,0:T(8,128)(2,1)}, u32[]{:S(2)}) copy-start(bf16[128,2048]{1,0:T(8,128)(2,1)} %stream_ref.1) | copy-start | bytes 1572868
  68.0 32.5 %copy-start.13 = (bf16[2048]{0:T(1024)(128)(2,1)S(1)}, bf16[2048]{0:T(1024)(128)(2,1)}, u32[]{:S(2)}) copy-start(bf16[2048]{0:T(1024)(128)(2,1)} %param.17) | copy-start | bytes 12292
  84.4 1.2 copy-start.6
  85.6 1.2 copy-start.7
  96.8 16.0 %collective-permute-start.13 = (bf16[1024,2048]{1,0:T(8,128)(2,1)}, bf16[1024,2048]{1,0:T(8,128)(2,1)}, u32[]{:S(2)}, u32[]{:S(2)}) collective-permute-start(bf16[1024,2048]{1,0:T(8,128)(2,1)} %all-gather.2.cloned.1.call-done.near_ref), channel_id=1, source_target_pairs={{0,8},{1,9},{2,10},{3,11},{4,12},{5,13},{6,14},{7,15},{8,0},{9,1},... | collective-permute-start | bytes 12582920 | tf_op jit(solution)/shard_map/ppermute | solution.py:349
  96.8 16.0 %all-to-all-start = ((bf16[8,128,256]{2,1,0:T(8,128)(2,1)}), bf16[8,128,256]{2,1,0:T(8,128)(2,1)S(1)}, u32[]{:S(2)}, u32[]{:S(2)}) async-start(bf16[8,128,256]{2,1,0:T(8,128)(2,1)} %bitcast.7), calls=%async_computation | async-start | bytes 1048576 | tf_op jit(solution)/shard_map/all_to_all | solution.py:425
  112.8 2.2 copy-start.2
  120.9 64.2 %copy-start.3 = (bf16[1,2048,768]{2,1,0:T(8,128)(2,1)S(1)}, bf16[1,2048,768]{2,1,0:T(8,128)(2,1)}, u32[]{:S(2)}) copy-start(bf16[1,2048,768]{2,1,0:T(8,128)(2,1)} %gate_ref.1) | copy-start | bytes 9437188
  120.9 64.2 %copy-start.4 = (bf16[1,2048,768]{2,1,0:T(8,128)(2,1)S(1)}, bf16[1,2048,768]{2,1,0:T(8,128)(2,1)}, u32[]{:S(2)}) copy-start(bf16[1,2048,768]{2,1,0:T(8,128)(2,1)} %up_ref.1) | copy-start | bytes 9437188
  120.9 64.2 %copy-start.5 = (bf16[1,768,2048]{2,1,0:T(8,128)(2,1)S(1)}, bf16[1,768,2048]{2,1,0:T(8,128)(2,1)}, u32[]{:S(2)}) copy-start(bf16[1,768,2048]{2,1,0:T(8,128)(2,1)} %down_ref.1) | copy-start | bytes 9437188
  198.0 2.2 copy-start.1
  200.2 5.9 %copy-start.12 = (f32[128,8]{1,0:T(8,128)S(1)}, f32[128,8]{1,0:T(8,128)}, u32[]{:S(2)}) copy-start(f32[128,8]{1,0:T(8,128)} %get-tuple-element.19) | copy-start | bytes 12292
  200.2 64.2 %all-to-all-start.2 = ((bf16[128,9,16,128]{3,2,1,0:T(8,128)(2,1)}), bf16[128,9,16,128]{3,2,1,0:T(8,128)(2,1)}, u32[]{:S(2)}, u32[]{:S(2)}) async-start(bf16[128,9,16,128]{3,2,1,0:T(8,128)(2,1)} %bitcast.12), calls=%async_computation.2 | async-start | bytes 9437184 | tf_op jit(solution)/shard_map/all_to_all | solution.py:443
Sparse Core Ops, SparseCore 0:
  9.7 87.0 all-gather.1

commit v3 on v2

--- a/solution.py
+++ b/solution.py
@@ -25,12 +25,16 @@
 
 def attend_part(final, meta_ref, lengths_ref, *refs):
     pieces = refs[:10]
+    count_q = 1 if final else 2
+    q_refs, out_refs = refs[10 : 10 + count_q], refs[10 + count_q : 12 + count_q]
+    kv_s, q_s, m_s, acc_s, v_s, start_s, sems = refs[12 + count_q :]
+    ctx = meta_ref[0]
+    half, z, core = ctx // HALF, (ctx // 2) & 3, ctx & 1
+    low = half * HALF
     if final:
-        q_ref, out_ref, lse_ref, kv_s, q_s, m_s, acc_s, v_s, sems = refs[10:]
+        base, active = ctx * SHARD, jnp.int32(1)
     else:
-        q_refs, out_refs = refs[10:12], refs[12:14]
-        kv_s, q_s, m_s, acc_s, v_s, sems = refs[14:]
-    base, low, active, z, core = (meta_ref[i] for i in range(5))
+        base, active = (ctx + HALF) * SHARD, 1 - half
     prompt = lengths_ref[0]
     scale = math.log2(math.e) / math.sqrt(HD)
 
@@ -69,12 +73,16 @@
     @pl.when(active > 0)
     def _():
         v_s[:, HD:] = jnp.ones((SHARD, HD), jnp.bfloat16)
+        pos = first + lax.broadcasted_iota(jnp.int32, (TQ, LANES), 0)
+        starts = jnp.zeros_like(pos)
+        end = jnp.int32(0)
+        for i in range(SEGMENTS):
+            end = end + lengths_ref[i]
+            starts = jnp.where(pos >= end, end, starts)
+        start_s[...] = starts
         for head in range(2):
             hs = slice(head * HD, (head + 1) * HD)
-            if final:
-                q = q_ref[:, hs].astype(jnp.float32) * scale
-            else:
-                q = jnp.concatenate([ref[:, hs] for ref in q_refs], axis=0).astype(jnp.float32) * scale
+            q = jnp.concatenate([ref[:, hs] for ref in q_refs], axis=0).astype(jnp.float32) * scale
             rounded = q.astype(jnp.bfloat16)
             q_s[head * TQ : (head + 1) * TQ, :HD] = rounded
             q_s[head * TQ : (head + 1) * TQ, HD:] = (q - rounded.astype(jnp.float32)).astype(jnp.bfloat16)
@@ -106,11 +114,7 @@
                     ahead = score(r + 1)
                 if masked:
                     pos = first + (r * RC) % TQ + lax.broadcasted_iota(jnp.int32, (RC, 1), 0)
-                    starts = jnp.zeros_like(pos)
-                    end = jnp.int32(0)
-                    for i in range(SEGMENTS):
-                        end = end + lengths_ref[i]
-                        starts = jnp.where(pos >= end, end, starts)
+                    starts = start_s[pl.ds((r * RC) % TQ, RC)][:, :1]
                     kpos = lo + lax.broadcasted_iota(jnp.int32, (1, SHARD), 1)
                     seen = jnp.where(kpos < prompt, SHARD * 2 * HALF, kpos) >= starts
                     if final:
@@ -140,27 +144,20 @@
             total = acc_s[hs, HD:]
             o = acc_s[hs, :HD] / total
             lse = m_s[hs] + jnp.log2(total)
-            if final:
-                out_ref[:, head * HD : (head + 1) * HD] = o
-                lse_ref[:, head * HD : (head + 1) * HD] = lse
-            else:
-                a = lse.astype(jnp.bfloat16).astype(jnp.float32)
-                b = (lse - a).astype(jnp.bfloat16).astype(jnp.float32)
-                c = lse - a - b
-                lane = lax.broadcasted_iota(jnp.int32, (TQ, LANES), 1)
-                parts = jnp.where(lane == 0, a, jnp.where(lane == 1, b, c)).astype(jnp.bfloat16)
-                o = o.astype(jnp.bfloat16)
-                half = TQ // 2
-                for n in range(2):
-                    out_refs[n][:, head * HD : (head + 1) * HD] = o[n * half : (n + 1) * half]
-                    out_refs[n][:, (2 + head) * HD : (3 + head) * HD] = parts[n * half : (n + 1) * half]
+            a = lse.astype(jnp.bfloat16).astype(jnp.float32)
+            b = (lse - a).astype(jnp.bfloat16).astype(jnp.float32)
+            c = lse - a - b
+            lane = lax.broadcasted_iota(jnp.int32, (TQ, LANES), 1)
+            parts = jnp.where(lane == 0, a, jnp.where(lane == 1, b, c)).astype(jnp.bfloat16)
+            o = o.astype(jnp.bfloat16)
+            rows = TQ // 2
+            for n in range(2):
+                out_refs[n][:, head * HD : (head + 1) * HD] = o[n * rows : (n + 1) * rows]
+                out_refs[n][:, (2 + head) * HD : (3 + head) * HD] = parts[n * rows : (n + 1) * rows]
 
 
 def attend(final, meta, lengths, q, pieces, blocks):
-    if final:
-        shapes = tuple(jax.ShapeDtypeStruct((SHARD, 2 * HD), jnp.float32) for _ in range(2))
-    else:
-        shapes = tuple(jax.ShapeDtypeStruct((TQ // 2, 4 * HD), jnp.bfloat16) for _ in range(2))
+    shapes = tuple(jax.ShapeDtypeStruct((TQ // 2, 4 * HD), jnp.bfloat16) for _ in range(2))
     return pl.pallas_call(
         functools.partial(attend_part, final),
         out_shape=shapes,
@@ -172,6 +169,7 @@
             pltpu.VMEM((2 * TQ, HD), jnp.float32),
             pltpu.VMEM((2 * TQ, 2 * HD), jnp.float32),
             pltpu.VMEM((SHARD, 2 * HD), jnp.bfloat16),
+            pltpu.VMEM((TQ, LANES), jnp.int32),
             pltpu.SemaphoreType.DMA((10,)),
         ],
         compiler_params=pltpu.CompilerParams(vmem_limit_bytes=60 << 20),
@@ -182,33 +180,38 @@
     )(meta, lengths, *pieces, *q)
 
 
-def merge_kernel(meta_ref, first_ref, second_ref, own_ref, lse_ref, out_ref):
-    high = meta_ref[0] > 0
-    half = first_ref.shape[0]
-    for n, sent_ref in enumerate((first_ref, second_ref)):
-        rs = pl.ds(n * half, half)
+def merge_kernel(meta_ref, *refs):
+    sent_refs, own_refs, out_ref = refs[:2], refs[2:4], refs[4]
+    high = meta_ref[0] >= HALF
+    half = out_ref.shape[0] // 2
+    for n in range(2):
+        sent_ref, own_ref = sent_refs[n], own_refs[n]
         for head in range(2):
-            hs = pl.ds(head * HD, HD)
-            parts = sent_ref[:, (2 + head) * HD : (3 + head) * HD].astype(jnp.float32)
-            sent = parts[:, 0:1] + parts[:, 1:2] + parts[:, 2:3]
-            sent = jnp.where(high, sent, NEVER)
-            here = lse_ref[rs, hs]
+            hs = slice(head * HD, (head + 1) * HD)
+
+            def log_sum(ref):
+                parts = ref[:, (2 + head) * HD : (3 + head) * HD].astype(jnp.float32)
+                return parts[:, 0:1] + parts[:, 1:2] + parts[:, 2:3]
+
+            sent, here = jnp.where(high, log_sum(sent_ref), NEVER), log_sum(own_ref)
             top = jnp.maximum(sent, here)
-            w_sent = jnp.exp2(sent - top)
-            w_here = jnp.exp2(here - top)
-            o = w_sent * sent_ref[:, hs].astype(jnp.float32) + w_here * own_ref[rs, hs]
-            out_ref[rs, hs] = (o / (w_sent + w_here)).astype(jnp.bfloat16)
-
-
-def merge(meta, first, second, own, lse):
+            w_sent, w_here = jnp.exp2(sent - top), jnp.exp2(here - top)
+            share = w_sent / (w_sent + w_here)
+            a, b = sent_ref[:, hs].astype(jnp.float32), own_ref[:, hs].astype(jnp.float32)
+            o = share * a + (1.0 - share) * b
+            out_ref[n * half : (n + 1) * half, hs] = o.astype(jnp.bfloat16)
+
+
+def merge(meta, sent, own):
+    half = own[0].shape[0]
     return pl.pallas_call(
         merge_kernel,
-        out_shape=jax.ShapeDtypeStruct(own.shape, jnp.bfloat16),
-        in_specs=[SM, VM, VM, VM, VM],
+        out_shape=jax.ShapeDtypeStruct((2 * half, 2 * HD), jnp.bfloat16),
+        in_specs=[SM] + [VM] * 4,
         out_specs=VM,
-        compiler_params=pltpu.CompilerParams(vmem_limit_bytes=32 << 20),
+        compiler_params=pltpu.CompilerParams(vmem_limit_bytes=16 << 20),
         name="merge",
-    )(meta, first, second, own, lse)
+    )(meta, *sent, *own)
 
 
 def slots_kernel(capacity, ids_ref, weights_ref, place_ref, shares_ref):
@@ -240,7 +243,7 @@
 ):
     rows, width = stream_ref.shape
     parts = width // LANES
-    upper = meta_ref[0] > 0
+    upper = (meta_ref[0] & 1) > 0
     near, far = [], []
     for e in range(attended_ref.shape[0]):
         a, b = attended_ref[e, :, :LANES], attended_ref[e, :, LANES:]
@@ -261,7 +264,7 @@
         for k in range(8):
             out_ref[place_ref[t * 8 + k]] = row
         return 0
-    lax.fori_loop(0, rows, one, 0, unroll=4)
+    lax.fori_loop(0, rows, one, 0, unroll=8)
 
 def pack(meta, place, attended, near, far, stream, gain, slots_count):
     rows, width = stream.shape
@@ -319,7 +322,7 @@
             acc = acc + shares_ref[t * 8 + k] * back_ref[place_ref[t * 8 + k]].astype(jnp.float32)
         total[t] = acc.astype(jnp.bfloat16)
         return 0
-    lax.fori_loop(0, rows, one, 0, unroll=2)
+    lax.fori_loop(0, rows, one, 0, unroll=8)
     out_ref[...] = total[...].reshape(rows, parts * lanes)
 
 def combine(place, shares, residual, back):
@@ -391,12 +394,13 @@
     expert_count = ctx_count * exp_count
     tok_rows, top_count = expert_ids.shape
     capacity = max(2, tok_rows * top_count * 9 // (expert_count * 8))
-    x_lo, z, core = ctx_index // 8, ctx_index // 2 % 4, ctx_index % 2
+    core = ctx_index % 2
     y = exp_index // 2
     own = jnp.concatenate(
         [lax.dynamic_slice_in_dim(keys, y * HD, HD, 1), lax.dynamic_slice_in_dim(values, y * HD, HD, 1)],
         axis=1,
     )
+    own, out_proj = lax.optimization_barrier((own, out_proj))
     middle = rows_ctx // 2
     up, down = along_z(own, 1), along_z(own, -1)
     q_sent = (down_x(queries[:middle], -1), down_x(queries[middle:], 1))
@@ -411,25 +415,22 @@
     place = place.reshape(-1)
     shares = shares.reshape(-1)
 
-    low = x_lo * HALF
-    one = jnp.int32(1)
-    meta_sent = jnp.stack([(ctx_index + HALF) * rows_ctx, low, one - x_lo, z, core])
-    meta_own = jnp.stack([ctx_index * rows_ctx, low, one, z, core])
-    sent = attend(False, meta_sent, segment_lengths, q_sent, pieces, 4)
-    meta_own, first, second = lax.optimization_barrier((meta_own, *sent))
+    here = ctx_index.reshape(1)
+    sent = attend(False, here, segment_lengths, q_sent, pieces, 4)
+    here, first, second = lax.optimization_barrier((here, *sent))
     first, second = back_x(first, 1), back_x(second, -1)
-    partial, lse = attend(True, meta_own, segment_lengths, (queries,), pieces, 5)
-    attended = merge(x_lo.reshape(1), first, second, partial, lse)
-    w_near, attended = lax.optimization_barrier((w_near, attended))
-    w_far = other_core(w_near)
+    own_parts = attend(True, here, segment_lengths, (queries,), pieces, 5)
+    attended = merge(here, (first, second), own_parts)
+    w_ready, _ = lax.optimization_barrier((w_near, attended))
+    w_far = other_core(w_ready)
     spread = lax.all_to_all(
         attended.reshape(exp_count, tok_rows, 2 * HD), "exp", split_axis=0, concat_axis=0, tiled=True
     )
     residual, outgoing = pack(
-        core.reshape(1),
+        here,
         place,
         spread,
-        w_near,
+        w_ready,
         w_far,
         stream,
         norm_gain.reshape(1, -1),

time: 276 us -> 276 us (level)
  waiting for transfers between devices: 107 us -> 111 us
  Pallas kernels: 53.9 us -> 50.1 us
    ppermute x14, waiting for transfers between devices: 32.4 us -> 36.7 us  [permute(): return lax.ppermute(x, ('ctx', 'exp'), pairs)]
    pallas_call x2, Pallas kernels: 26.1 us -> 22 us  [attend(): pl.pallas_call(functools.partial(attend_part, final), out_shape=shapes, i...]
    unnamed x40 -> x50, local copies, waits for them, and re-layouts: 9.52 us -> 9.61 us
  transfers between devices with their start and end apart: 17 -> 17, of which waited for: 10 -> 10; matrix products, arithmetic and copies ran while one was open for 2% -> 1% of each run, Pallas kernels for 11% -> 10%
where the time goes in v3:
time: 276 us
  waiting for transfers between devices  111 us (40%)
  blocking collectives  64.2 us (23%)
  Pallas kernels  50.1 us (18%)
  starting transfers between devices  23.4 us (8%)
  local copies, waits for them, and re-layouts  13.8 us (5%)
  between operations  13.7 us (5%)
    all_to_all x1, blocking collectives, on_device(): lax.all_to_all(outgoing.reshape(shape), ('ctx', 'exp'), split_axis=0, con...  64.2 us
    all_to_all x1, waiting for transfers between devices, on_device(): lax.all_to_all(results.reshape(shape), ('ctx', 'exp'), split_axis=0, conc...  58.2 us
    ppermute x14, waiting for transfers between devices, permute(): return lax.ppermute(x, ('ctx', 'exp'), pairs)  36.7 us
    pallas_call x2, Pallas kernels, attend(): pl.pallas_call(functools.partial(attend_part, final), out_shape=shapes, i...  22 us
    ppermute x14, starting transfers between devices, permute(): return lax.ppermute(x, ('ctx', 'exp'), pairs)  13.7 us
    pallas_call x1, Pallas kernels, experts(): pl.pallas_call(experts_kernel, out_shape=jax.ShapeDtypeStruct(x.shape, jn...  12.9 us
    unnamed x50, local copies, waits for them, and re-layouts  9.61 us
    all_gather x1, waiting for transfers between devices, on_device(): w_near = lax.all_gather(mine, 'exp', axis=0, tiled=True)  7.98 us
  transfers between devices with their start and end apart: 17, of which 10 were waited for; matrix products, arithmetic and copies ran while one was open for 1% of the time, Pallas kernels for 10%

profile of v3, /device:TPU:0, one launch (start us, length us, event | category | flops | bytes accessed | tf_op | source)
XLA Modules:
  0.0 275.8 jit_solution(3128954399493055572)
XLA Ops:
  6.5 1.2 constant_dynamic-slice_fusion.1
  7.7 0.1 pad_maximum_fusion.refs_0_
  7.8 0.0 copy-start.9
  7.8 0.1 copy-done
  7.9 0.9 constant_dynamic-slice_fusion
  8.8 0.0 all-gather.2.cloned.1.call-update
  8.8 4.2 %collective-permute-start.1 = (bf16[1024,256]{1,0:T(8,128)(2,1)S(1)}, bf16[1024,256]{1,0:T(8,128)(2,1)S(1)}, u32[]{:S(2)}, u32[]{:S(2)}) collective-permute-start(bf16[1024,256]{1,0:T(8,128)(2,1)S(1)} %pad_maximum_fusion.refs_0_), channel_id=1, source_target_pairs={{0,48},{1,49},{2,50},{3,51},{4,52},{5,53},{6,54},{7,55},{8,56},{9,... | collective-permute-start | bytes 1572872 | tf_op jit(solution)/shard_map/ppermute | solution.py:352
  13.0 0.0 collective-permute-start
  13.0 1.1 fusion
  14.1 1.3 collective-permute-start.10
  15.4 1.3 collective-permute-start.9
  16.7 0.1 collective-permute-start.4
  16.8 7.4 %collective-permute-done.1.refs_2_ = bf16[1024,256]{1,0:T(8,128)(2,1)S(1)} collective-permute-done((bf16[1024,256]{1,0:T(8,128)(2,1)S(1)}, bf16[1024,256]{1,0:T(8,128)(2,1)S(1)}, u32[]{:S(2)}, u32[]{:S(2)}) %collective-permute-start.1) | collective-permute-done | bytes 524320 | tf_op jit(solution)/shard_map/ppermute | solution.py:352
  24.2 3.8 %collective-permute-start.3 = (bf16[512,256]{1,0:T(8,128)(2,1)S(1)}, bf16[512,256]{1,0:T(8,128)(2,1)S(1)}, u32[]{:S(2)}, u32[]{:S(2)}) collective-permute-start(bf16[512,256]{1,0:T(8,128)(2,1)S(1)} %slice.17), channel_id=1, source_target_pairs={{0,48},{1,49},{2,50},{3,51},{4,52},{5,53},{6,54},{7,55},{8,56},{9,... | collective-permute-start | bytes 786440 | tf_op jit(solution)/shard_map/ppermute | solution.py:352
  28.0 0.0 collective-permute-done.refs_1_
  28.0 0.1 collective-permute-start.2
  28.1 0.0 collective-permute-done.10.refs_11_
  28.1 0.1 collective-permute-start.6
  28.2 1.6 collective-permute-done.9.refs_10_
  29.8 0.0 collective-permute-start.5
  29.8 2.9 %collective-permute-done.3.refs_4_ = bf16[512,256]{1,0:T(8,128)(2,1)S(1)} collective-permute-done((bf16[512,256]{1,0:T(8,128)(2,1)S(1)}, bf16[512,256]{1,0:T(8,128)(2,1)S(1)}, u32[]{:S(2)}, u32[]{:S(2)}) %collective-permute-start.3) | collective-permute-done | bytes 262176 | tf_op jit(solution)/shard_map/ppermute | solution.py:352
  32.8 0.0 collective-permute-start.8
  32.8 3.5 %collective-permute-done.2.refs_3_ = bf16[512,256]{1,0:T(8,128)(2,1)S(1)} collective-permute-done((bf16[512,256]{1,0:T(8,128)(2,1)S(1)}, bf16[512,256]{1,0:T(8,128)(2,1)S(1)}, u32[]{:S(2)}, u32[]{:S(2)}) %collective-permute-start.2) | collective-permute-done | bytes 262176 | tf_op jit(solution)/shard_map/ppermute | solution.py:352
  36.3 0.0 collective-permute-start.7
  36.3 0.0 collective-permute-done.4.refs_5_
  36.3 0.0 collective-permute-done.8.refs_9_
  36.3 0.0 collective-permute-done.6.refs_7_
  36.3 1.5 collective-permute-done.7.refs_8_
  37.8 0.7 copy-done.23
  38.5 0.8 copy-done.18
  39.4 14.3 %attend_sent.1 = (bf16[512,512]{1,0:T(8,128)(2,1)}, bf16[512,512]{1,0:T(8,128)(2,1)}) custom-call(s32[1]{0:T(128)} %bitcast.meta_ref, s32[17]{0:T(128)} %lengths_ref.3, bf16[1024,256]{1,0:T(8,128)(2,1)} %copy-done.9, bf16[1024,256]{1,0:T(8,128)(2,1)} %copy-done.11, bf16[1024,256]{1,0:T(8,128)(2,1)} %copy-done.10, bf16[512,256]{1,0:T(8,128)(2,1)} %copy-done.21, ...), custom_call_target="tpu_custom_call" | custom-call | flops 17179869184 | bytes 8388608 | tf_op jit(solution)/shard_map/attend_sent/pallas_call | solution.py:161
  53.7 0.0 copy-start.13
  53.7 0.0 copy-start.14
  53.7 0.0 copy-start.15
  53.7 1.5 collective-permute-start.11
  55.2 1.5 collective-permute-start.12
  56.7 7.7 %attend_own.1 = (bf16[512,512]{1,0:T(8,128)(2,1)}, bf16[512,512]{1,0:T(8,128)(2,1)}) custom-call(s32[1]{0:T(128)} %bitcast.meta_ref, s32[17]{0:T(128)} %lengths_ref.3, bf16[1024,256]{1,0:T(8,128)(2,1)} %copy-done.9, bf16[1024,256]{1,0:T(8,128)(2,1)} %copy-done.11, bf16[1024,256]{1,0:T(8,128)(2,1)} %copy-done.10, bf16[512,256]{1,0:T(8,128)(2,1)} %copy-done.21, ...), custom_call_target="tpu_custom_call" | custom-call | flops 21474836480 | bytes 8388608 | tf_op jit(solution)/shard_map/attend_own/pallas_call | solution.py:161
  64.4 0.0 copy-start.6
  64.4 14.4 %collective-permute-done.11.refs_0_ = bf16[512,512]{1,0:T(8,128)(2,1)S(1)} collective-permute-done((bf16[512,512]{1,0:T(8,128)(2,1)}, bf16[512,512]{1,0:T(8,128)(2,1)S(1)}, u32[]{:S(2)}, u32[]{:S(2)}) %collective-permute-start.11) | collective-permute-done | bytes 524320 | tf_op jit(solution)/shard_map/ppermute | solution.py:352
  78.8 5.3 %collective-permute-done.12.refs_1_ = bf16[512,512]{1,0:T(8,128)(2,1)S(1)} collective-permute-done((bf16[512,512]{1,0:T(8,128)(2,1)}, bf16[512,512]{1,0:T(8,128)(2,1)S(1)}, u32[]{:S(2)}, u32[]{:S(2)}) %collective-permute-start.12) | collective-permute-done | bytes 524320 | tf_op jit(solution)/shard_map/ppermute | solution.py:352
  84.1 1.0 copy-done.7
  85.2 1.0 copy-done.8
  86.2 2.4 merge.1
  88.6 8.0 %all-gather.2.cloned.1.call-done.near_ref = bf16[1024,2048]{1,0:T(8,128)(2,1)} async-done(((bf16[128,2048]{1,0:T(8,128)(2,1)}), bf16[1024,2048]{1,0:T(8,128)(2,1)}) %all-gather.2.cloned.1.call-update) | async-done | bytes 4194320 | tf_op jit(solution)/shard_map/all_gather | solution.py:412
  96.6 0.0 collective-permute-start.13
  96.6 3.7 %all-to-all-start = ((bf16[8,128,256]{2,1,0:T(8,128)(2,1)}), bf16[8,128,256]{2,1,0:T(8,128)(2,1)S(1)}, u32[]{:S(2)}, u32[]{:S(2)}) async-start(bf16[8,128,256]{2,1,0:T(8,128)(2,1)} %bitcast.1), calls=%async_computation | async-start | bytes 1048576 | tf_op jit(solution)/shard_map/all_to_all | solution.py:426
  100.3 0.7 copy.15.ids_ref
  101.0 0.7 copy.16.weights_ref
  101.8 2.1 slots.1
  103.9 0.9 reshape.27.place_ref
  104.8 7.7 %all-to-all-done.attended_ref = bf16[8,128,256]{2,1,0:T(8,128)(2,1)S(1)} async-done(((bf16[8,128,256]{2,1,0:T(8,128)(2,1)}), bf16[8,128,256]{2,1,0:T(8,128)(2,1)S(1)}, u32[]{:S(2)}, u32[]{:S(2)}) %all-to-all-start) | async-done | bytes 524320 | tf_op jit(solution)/shard_map/all_to_all | solution.py:426
  112.5 0.0 collective-permute-done.13.far_ref
  112.5 2.2 copy-done.2
  114.7 5.9 %pack.1 = (f32[128,16,128]{2,1,0:T(8,128)S(1)}, bf16[1152,16,128]{2,1,0:T(8,128)(2,1)S(1)}) custom-call(s32[1]{0:T(128)} %bitcast.meta_ref, s32[1024]{0:T(1024)S(1)} %reshape.27.place_ref, bf16[8,128,256]{2,1,0:T(8,128)(2,1)S(1)} %all-to-all-done.attended_ref, bf16[1024,2048]{1,0:T(8,128)(2,1)S(1)} %copy-done.2, ...), custom_call_target="tpu_custom_call" | custom-call | tf_op jit(solution)/shard_map/pack/pallas_call | solution.py:272
  120.6 0.0 copy-start.3
  120.6 0.0 copy-start.4
  120.6 0.0 copy-start.5
  120.6 64.2 %all_to_all.15 = bf16[128,9,16,128]{3,2,1,0:T(8,128)(2,1)} all-to-all(bf16[128,9,16,128]{3,2,1,0:T(8,128)(2,1)S(1)} %bitcast.7), channel_id=1, replica_groups=mesh['ctx'=16,'exp'=8] {'ctx','exp'}, dimensions={0} | all-to-all | bytes 9437184 | tf_op jit(solution)/shard_map/all_to_all | solution.py:440
  184.8 12.9 %experts.1 = bf16[1152,16,128]{2,1,0:T(8,128)(2,1)S(1)} custom-call(bf16[1152,16,128]{2,1,0:T(8,128)(2,1)} %bitcast.8, bf16[1,2048,768]{2,1,0:T(8,128)(2,1)S(1)} %copy-done.3, bf16[1,2048,768]{2,1,0:T(8,128)(2,1)S(1)} %copy-done.4, bf16[1,768,2048]{2,1,0:T(8,128)(2,1)S(1)} %copy-done.5), custom_call_target="tpu_custom_call" | custom-call | tf_op jit(solution)/shard_map/experts/pallas_call | solution.py:301
  197.8 2.2 copy-done.1
  199.9 5.9 %all-to-all-start.2 = ((bf16[128,9,16,128]{3,2,1,0:T(8,128)(2,1)}), bf16[128,9,16,128]{3,2,1,0:T(8,128)(2,1)}, u32[]{:S(2)}, u32[]{:S(2)}) async-start(bf16[128,9,16,128]{3,2,1,0:T(8,128)(2,1)} %bitcast.6), calls=%async_computation.2 | async-start | bytes 9437184 | tf_op jit(solution)/shard_map/all_to_all | solution.py:444
  205.9 0.1 reshape.28.shares_ref
  206.0 58.2 %all-to-all-done.2 = bf16[128,9,16,128]{3,2,1,0:T(8,128)(2,1)} async-done(((bf16[128,9,16,128]{3,2,1,0:T(8,128)(2,1)}), bf16[128,9,16,128]{3,2,1,0:T(8,128)(2,1)}, u32[]{:S(2)}, u32[]{:S(2)}) %all-to-all-start.2) | async-done | bytes 4718624 | tf_op jit(solution)/shard_map/all_to_all | solution.py:444
  264.1 4.8 %combine.1 = bf16[128,2048]{1,0:T(8,128)(2,1)} custom-call(s32[1024]{0:T(1024)S(1)} %reshape.27.place_ref, f32[1024]{0:T(1024)S(1)} %reshape.28.shares_ref, f32[128,16,128]{2,1,0:T(8,128)S(1)} %get-tuple-element.31.residual_ref, bf16[1152,16,128]{2,1,0:T(8,128)(2,1)} %bitcast.5.back_ref), custom_call_target="tpu_custom_call" | custom-call | tf_op jit(solution)/shard_map/combine/pallas_call | solution.py:330
  (38 shorter events, 0.1 us)
Async XLA Ops:
  6.5 1.4 copy-start
  6.5 90.0 %all-gather.2.cloned.1.call-start = ((), (), s32[]{:S(2)}) async-start(), calls=%async_computation.3 | async-start | bytes 4718592 | tf_op jit(solution)/shard_map/all_gather | solution.py:412
  7.8 31.5 %copy-start.9 = (bf16[1024,256]{1,0:T(8,128)(2,1)}, bf16[1024,256]{1,0:T(8,128)(2,1)S(1)}, u32[]{:S(2)}) copy-start(bf16[1024,256]{1,0:T(8,128)(2,1)S(1)} %pad_maximum_fusion.refs_0_) | copy-start | bytes 1572868
  8.8 15.4 %collective-permute-start.1 = (bf16[1024,256]{1,0:T(8,128)(2,1)S(1)}, bf16[1024,256]{1,0:T(8,128)(2,1)S(1)}, u32[]{:S(2)}, u32[]{:S(2)}) collective-permute-start(bf16[1024,256]{1,0:T(8,128)(2,1)S(1)} %pad_maximum_fusion.refs_0_), channel_id=1, source_target_pairs={{0,48},{1,49},{2,50},{3,51},{4,52},{5,53},{6,54},{7,55},{8,56},{9,... | collective-permute-start | bytes 1572872 | tf_op jit(solution)/shard_map/ppermute | solution.py:352
  13.0 15.0 %collective-permute-start = (bf16[1024,256]{1,0:T(8,128)(2,1)S(1)}, bf16[1024,256]{1,0:T(8,128)(2,1)S(1)}, u32[]{:S(2)}, u32[]{:S(2)}) collective-permute-start(bf16[1024,256]{1,0:T(8,128)(2,1)S(1)} %pad_maximum_fusion.refs_0_), channel_id=1, source_target_pairs={{0,16},{1,17},{2,18},{3,19},{4,20},{5,21},{6,22},{7,23},{8,24},{9,... | collective-permute-start | bytes 1572872 | tf_op jit(solution)/shard_map/ppermute | solution.py:352
  14.1 14.0 %collective-permute-start.10 = (bf16[512,256]{1,0:T(8,128)(2,1)S(1)}, bf16[512,256]{1,0:T(8,128)(2,1)}, u32[]{:S(2)}, u32[]{:S(2)}) collective-permute-start(bf16[512,256]{1,0:T(8,128)(2,1)S(1)} %get-tuple-element.33), channel_id=1, source_target_pairs={{64,1},{65,0},{66,3},{67,2},{68,5},{69,4},{70,7},{71,6},{72,9},{73... | collective-permute-start | bytes 786440 | tf_op jit(solution)/shard_map/ppermute | solution.py:352
  15.4 14.4 %collective-permute-start.9 = (bf16[512,256]{1,0:T(8,128)(2,1)S(1)}, bf16[512,256]{1,0:T(8,128)(2,1)S(1)}, u32[]{:S(2)}, u32[]{:S(2)}) collective-permute-start(bf16[512,256]{1,0:T(8,128)(2,1)S(1)} %get-tuple-element.34), channel_id=1, source_target_pairs={{64,0},{65,1},{66,2},{67,3},{68,4},{69,5},{70,6},{71,7},{72,8},{73... | collective-permute-start | bytes 786440 | tf_op jit(solution)/shard_map/ppermute | solution.py:352
  16.7 19.6 %collective-permute-start.4 = (bf16[1024,256]{1,0:T(8,128)(2,1)S(1)}, bf16[1024,256]{1,0:T(8,128)(2,1)S(1)}, u32[]{:S(2)}, u32[]{:S(2)}) collective-permute-start(bf16[1024,256]{1,0:T(8,128)(2,1)S(1)} %pad_maximum_fusion.refs_0_), channel_id=1, source_target_pairs={{0,8},{1,9},{2,10},{3,11},{4,12},{5,13},{6,14},{7,15},{8,0},{9,1},... | collective-permute-start | bytes 1572872 | tf_op jit(solution)/shard_map/ppermute | solution.py:352
  24.2 15.1 %copy-start.10 = (bf16[1024,256]{1,0:T(8,128)(2,1)}, bf16[1024,256]{1,0:T(8,128)(2,1)S(1)}, u32[]{:S(2)}) copy-start(bf16[1024,256]{1,0:T(8,128)(2,1)S(1)} %collective-permute-done.1.refs_2_) | copy-start | bytes 1572868
  24.2 8.6 %collective-permute-start.3 = (bf16[512,256]{1,0:T(8,128)(2,1)S(1)}, bf16[512,256]{1,0:T(8,128)(2,1)S(1)}, u32[]{:S(2)}, u32[]{:S(2)}) collective-permute-start(bf16[512,256]{1,0:T(8,128)(2,1)S(1)} %slice.17), channel_id=1, source_target_pairs={{0,48},{1,49},{2,50},{3,51},{4,52},{5,53},{6,54},{7,55},{8,56},{9,... | collective-permute-start | bytes 786440 | tf_op jit(solution)/shard_map/ppermute | solution.py:352
  28.0 11.4 %copy-start.11 = (bf16[1024,256]{1,0:T(8,128)(2,1)}, bf16[1024,256]{1,0:T(8,128)(2,1)S(1)}, u32[]{:S(2)}) copy-start(bf16[1024,256]{1,0:T(8,128)(2,1)S(1)} %collective-permute-done.refs_1_) | copy-start | bytes 1572868
  28.0 8.3 %collective-permute-start.2 = (bf16[512,256]{1,0:T(8,128)(2,1)S(1)}, bf16[512,256]{1,0:T(8,128)(2,1)S(1)}, u32[]{:S(2)}, u32[]{:S(2)}) collective-permute-start(bf16[512,256]{1,0:T(8,128)(2,1)S(1)} %slice.16), channel_id=1, source_target_pairs={{0,16},{1,17},{2,18},{3,19},{4,20},{5,21},{6,22},{7,23},{8,24},{9,... | collective-permute-start | bytes 786440 | tf_op jit(solution)/shard_map/ppermute | solution.py:352
  28.1 8.2 %collective-permute-start.6 = (bf16[1024,256]{1,0:T(8,128)(2,1)S(1)}, bf16[1024,256]{1,0:T(8,128)(2,1)S(1)}, u32[]{:S(2)}, u32[]{:S(2)}) collective-permute-start(bf16[1024,256]{1,0:T(8,128)(2,1)S(1)} %collective-permute-done.1.refs_2_), channel_id=1, source_target_pairs={{0,8},{1,9},{2,10},{3,11},{4,12},{5,13},{6,14},{7,15},{8,0},{9,1},... | collective-permute-start | bytes 1572872 | tf_op jit(solution)/shard_map/ppermute | solution.py:352
  29.8 8.0 %copy-start.20 = (bf16[512,256]{1,0:T(8,128)(2,1)}, bf16[512,256]{1,0:T(8,128)(2,1)S(1)}, u32[]{:S(2)}) copy-start(bf16[512,256]{1,0:T(8,128)(2,1)S(1)} %collective-permute-done.9.refs_10_) | copy-start | bytes 786436
  29.8 8.0 %collective-permute-start.5 = (bf16[1024,256]{1,0:T(8,128)(2,1)S(1)}, bf16[1024,256]{1,0:T(8,128)(2,1)S(1)}, u32[]{:S(2)}, u32[]{:S(2)}) collective-permute-start(bf16[1024,256]{1,0:T(8,128)(2,1)S(1)} %collective-permute-done.refs_1_), channel_id=1, source_target_pairs={{0,8},{1,9},{2,10},{3,11},{4,12},{5,13},{6,14},{7,15},{8,0},{9,1},... | collective-permute-start | bytes 1572872 | tf_op jit(solution)/shard_map/ppermute | solution.py:352
  32.8 6.6 %copy-start.19 = (bf16[512,256]{1,0:T(8,128)(2,1)}, bf16[512,256]{1,0:T(8,128)(2,1)S(1)}, u32[]{:S(2)}) copy-start(bf16[512,256]{1,0:T(8,128)(2,1)S(1)} %collective-permute-done.3.refs_4_) | copy-start | bytes 786436
  32.8 3.5 %collective-permute-start.8 = (bf16[512,256]{1,0:T(8,128)(2,1)S(1)}, bf16[512,256]{1,0:T(8,128)(2,1)S(1)}, u32[]{:S(2)}, u32[]{:S(2)}) collective-permute-start(bf16[512,256]{1,0:T(8,128)(2,1)S(1)} %collective-permute-done.3.refs_4_), channel_id=1, source_target_pairs={{0,8},{1,9},{2,10},{3,11},{4,12},{5,13},{6,14},{7,15},{8,0},{9,1},... | collective-permute-start | bytes 786440 | tf_op jit(solution)/shard_map/ppermute | solution.py:352
  36.3 1.6 copy-start.21
  36.3 1.5 collective-permute-start.7
  36.3 3.0 %copy-start.16 = (bf16[1024,256]{1,0:T(8,128)(2,1)}, bf16[1024,256]{1,0:T(8,128)(2,1)S(1)}, u32[]{:S(2)}) copy-start(bf16[1024,256]{1,0:T(8,128)(2,1)S(1)} %collective-permute-done.4.refs_5_) | copy-start | bytes 1572868
  36.3 1.5 copy-start.22
  36.3 3.0 %copy-start.17 = (bf16[1024,256]{1,0:T(8,128)(2,1)}, bf16[1024,256]{1,0:T(8,128)(2,1)S(1)}, u32[]{:S(2)}) copy-start(bf16[1024,256]{1,0:T(8,128)(2,1)S(1)} %collective-permute-done.6.refs_7_) | copy-start | bytes 1572868
  37.8 0.7 copy-start.23
  38.5 0.8 copy-start.18
  53.7 46.6 %copy-start.13 = (bf16[2048]{0:T(1024)(128)(2,1)S(1)}, bf16[2048]{0:T(1024)(128)(2,1)}, u32[]{:S(2)}) copy-start(bf16[2048]{0:T(1024)(128)(2,1)} %param.17) | copy-start | bytes 12292
  53.7 46.6 %copy-start.14 = (s32[128,8]{0,1:T(8,128)S(1)}, s32[128,8]{0,1:T(8,128)}, u32[]{:S(2)}) copy-start(s32[128,8]{0,1:T(8,128)} %param.21) | copy-start | bytes 12292
  53.7 47.3 %copy-start.15 = (f32[128,8]{0,1:T(8,128)S(1)}, f32[128,8]{0,1:T(8,128)}, u32[]{:S(2)}) copy-start(f32[128,8]{0,1:T(8,128)} %param.22) | copy-start | bytes 12292
  53.7 25.1 %collective-permute-start.11 = (bf16[512,512]{1,0:T(8,128)(2,1)}, bf16[512,512]{1,0:T(8,128)(2,1)S(1)}, u32[]{:S(2)}, u32[]{:S(2)}) collective-permute-start(bf16[512,512]{1,0:T(8,128)(2,1)} %get-tuple-element.25), channel_id=1, source_target_pairs={{0,64},{1,65},{2,66},{3,67},{4,68},{5,69},{6,70},{7,71},{8,72},{9,... | collective-permute-start | bytes 1572872 | tf_op jit(solution)/shard_map/ppermute | solution.py:352
  55.2 28.9 %collective-permute-start.12 = (bf16[512,512]{1,0:T(8,128)(2,1)}, bf16[512,512]{1,0:T(8,128)(2,1)S(1)}, u32[]{:S(2)}, u32[]{:S(2)}) collective-permute-start(bf16[512,512]{1,0:T(8,128)(2,1)} %get-tuple-element.26), channel_id=1, source_target_pairs={{0,65},{1,64},{2,67},{3,66},{4,69},{5,68},{6,71},{7,70},{8,73},{9,... | collective-permute-start | bytes 1572872 | tf_op jit(solution)/shard_map/ppermute | solution.py:352
  64.4 48.2 %copy-start.6 = (bf16[128,2048]{1,0:T(8,128)(2,1)S(1)}, bf16[128,2048]{1,0:T(8,128)(2,1)}, u32[]{:S(2)}) copy-start(bf16[128,2048]{1,0:T(8,128)(2,1)} %stream_ref.1) | copy-start | bytes 1572868
  84.1 1.0 copy-start.7
  85.2 1.0 copy-start.8
  96.6 16.0 %collective-permute-start.13 = (bf16[1024,2048]{1,0:T(8,128)(2,1)}, bf16[1024,2048]{1,0:T(8,128)(2,1)}, u32[]{:S(2)}, u32[]{:S(2)}) collective-permute-start(bf16[1024,2048]{1,0:T(8,128)(2,1)} %all-gather.2.cloned.1.call-done.near_ref), channel_id=1, source_target_pairs={{0,8},{1,9},{2,10},{3,11},{4,12},{5,13},{6,14},{7,15},{8,0},{9,1},... | collective-permute-start | bytes 12582920 | tf_op jit(solution)/shard_map/ppermute | solution.py:352
  96.6 16.0 %all-to-all-start = ((bf16[8,128,256]{2,1,0:T(8,128)(2,1)}), bf16[8,128,256]{2,1,0:T(8,128)(2,1)S(1)}, u32[]{:S(2)}, u32[]{:S(2)}) async-start(bf16[8,128,256]{2,1,0:T(8,128)(2,1)} %bitcast.1), calls=%async_computation | async-start | bytes 1048576 | tf_op jit(solution)/shard_map/all_to_all | solution.py:426
  112.5 2.2 copy-start.2
  120.6 64.2 %copy-start.3 = (bf16[1,2048,768]{2,1,0:T(8,128)(2,1)S(1)}, bf16[1,2048,768]{2,1,0:T(8,128)(2,1)}, u32[]{:S(2)}) copy-start(bf16[1,2048,768]{2,1,0:T(8,128)(2,1)} %gate_ref.1) | copy-start | bytes 9437188
  120.6 64.2 %copy-start.4 = (bf16[1,2048,768]{2,1,0:T(8,128)(2,1)S(1)}, bf16[1,2048,768]{2,1,0:T(8,128)(2,1)}, u32[]{:S(2)}) copy-start(bf16[1,2048,768]{2,1,0:T(8,128)(2,1)} %up_ref.1) | copy-start | bytes 9437188
  120.6 64.2 %copy-start.5 = (bf16[1,768,2048]{2,1,0:T(8,128)(2,1)S(1)}, bf16[1,768,2048]{2,1,0:T(8,128)(2,1)}, u32[]{:S(2)}) copy-start(bf16[1,768,2048]{2,1,0:T(8,128)(2,1)} %down_ref.1) | copy-start | bytes 9437188
  197.8 2.2 copy-start.1
  199.9 5.9 %copy-start.12 = (f32[128,8]{1,0:T(8,128)S(1)}, f32[128,8]{1,0:T(8,128)}, u32[]{:S(2)}) copy-start(f32[128,8]{1,0:T(8,128)} %get-tuple-element.20) | copy-start | bytes 12292
  199.9 64.2 %all-to-all-start.2 = ((bf16[128,9,16,128]{3,2,1,0:T(8,128)(2,1)}), bf16[128,9,16,128]{3,2,1,0:T(8,128)(2,1)}, u32[]{:S(2)}, u32[]{:S(2)}) async-start(bf16[128,9,16,128]{3,2,1,0:T(8,128)(2,1)} %bitcast.6), calls=%async_computation.2 | async-start | bytes 9437184 | tf_op jit(solution)/shard_map/all_to_all | solution.py:444
Sparse Core Ops, SparseCore 0:
  9.7 86.7 all-gather.1

commit v4 on v3

--- a/solution.py
+++ b/solution.py
@@ -139,6 +139,7 @@
             return 0
 
         lax.fori_loop(0, count, step, 0)
+        rows, terms = TQ // 2, []
         for head in range(2):
             hs = pl.ds(head * TQ, TQ)
             total = acc_s[hs, HD:]
@@ -146,18 +147,21 @@
             lse = m_s[hs] + jnp.log2(total)
             a = lse.astype(jnp.bfloat16).astype(jnp.float32)
             b = (lse - a).astype(jnp.bfloat16).astype(jnp.float32)
-            c = lse - a - b
-            lane = lax.broadcasted_iota(jnp.int32, (TQ, LANES), 1)
-            parts = jnp.where(lane == 0, a, jnp.where(lane == 1, b, c)).astype(jnp.bfloat16)
+            terms += [a, b, lse - a - b]
             o = o.astype(jnp.bfloat16)
-            rows = TQ // 2
             for n in range(2):
                 out_refs[n][:, head * HD : (head + 1) * HD] = o[n * rows : (n + 1) * rows]
-                out_refs[n][:, (2 + head) * HD : (3 + head) * HD] = parts[n * rows : (n + 1) * rows]
+        lane = lax.broadcasted_iota(jnp.int32, (TQ, LANES), 1)
+        parts = terms[-1]
+        for n in range(len(terms) - 1):
+            parts = jnp.where(lane == n, terms[n], parts)
+        parts = parts.astype(jnp.bfloat16)
+        for n in range(2):
+            out_refs[n][:, 2 * HD :] = parts[n * rows : (n + 1) * rows]
 
 
 def attend(final, meta, lengths, q, pieces, blocks):
-    shapes = tuple(jax.ShapeDtypeStruct((TQ // 2, 4 * HD), jnp.bfloat16) for _ in range(2))
+    shapes = tuple(jax.ShapeDtypeStruct((TQ // 2, 2 * HD + LANES), jnp.bfloat16) for _ in range(2))
     return pl.pallas_call(
         functools.partial(attend_part, final),
         out_shape=shapes,
@@ -172,7 +176,7 @@
             pltpu.VMEM((TQ, LANES), jnp.int32),
             pltpu.SemaphoreType.DMA((10,)),
         ],
-        compiler_params=pltpu.CompilerParams(vmem_limit_bytes=60 << 20),
+        compiler_params=pltpu.CompilerParams(vmem_limit_bytes=57 << 20),
         cost_estimate=pl.CostEstimate(
             flops=blocks * 32 * HD * SHARD * SHARD, bytes_accessed=8 << 20, transcendentals=blocks * 2 * SHARD * SHARD
         ),
@@ -190,8 +194,9 @@
             hs = slice(head * HD, (head + 1) * HD)
 
             def log_sum(ref):
-                parts = ref[:, (2 + head) * HD : (3 + head) * HD].astype(jnp.float32)
-                return parts[:, 0:1] + parts[:, 1:2] + parts[:, 2:3]
+                parts = ref[:, 2 * HD :].astype(jnp.float32)
+                at = 3 * head
+                return parts[:, at : at + 1] + parts[:, at + 1 : at + 2] + parts[:, at + 2 : at + 3]
 
             sent, here = jnp.where(high, log_sum(sent_ref), NEVER), log_sum(own_ref)
             top = jnp.maximum(sent, here)

time: 276 us -> 273 us (0.989)
  Pallas kernels: 50.1 us -> 46.2 us
    pallas_call x2, Pallas kernels: 22 us -> 18.2 us  [attend(): pl.pallas_call(functools.partial(attend_part, final), out_shape=shapes, i...]
    unnamed x50 -> x52, local copies, waits for them, and re-layouts: 9.61 us -> 8.81 us
  transfers between devices with their start and end apart: 17 -> 17, of which waited for: 10 -> 9; matrix products, arithmetic and copies ran while one was open for 1% -> 1% of each run, Pallas kernels for 10% -> 8%
where the time goes in v4:
time: 273 us; the launch traced here: 272 us
  waiting for transfers between devices  111 us (41%)
  blocking collectives  64 us (23%)
  Pallas kernels  46.2 us (17%)
  starting transfers between devices  23.8 us (9%)
  between operations  13.8 us (5%)
  local copies, waits for them, and re-layouts  12.9 us (5%)
    all_to_all x1, blocking collectives, on_device(): lax.all_to_all(outgoing.reshape(shape), ('ctx', 'exp'), split_axis=0, con...  64 us
    all_to_all x1, waiting for transfers between devices, on_device(): lax.all_to_all(results.reshape(shape), ('ctx', 'exp'), split_axis=0, conc...  58.2 us
    ppermute x14, waiting for transfers between devices, permute(): return lax.ppermute(x, ('ctx', 'exp'), pairs)  37.2 us
    pallas_call x2, Pallas kernels, attend(): pl.pallas_call(functools.partial(attend_part, final), out_shape=shapes, i...  18.2 us
    ppermute x14, starting transfers between devices, permute(): return lax.ppermute(x, ('ctx', 'exp'), pairs)  14.2 us
    pallas_call x1, Pallas kernels, experts(): pl.pallas_call(experts_kernel, out_shape=jax.ShapeDtypeStruct(x.shape, jn...  12.9 us
    unnamed x52, local copies, waits for them, and re-layouts  8.81 us
    all_gather x1, waiting for transfers between devices, on_device(): w_near = lax.all_gather(mine, 'exp', axis=0, tiled=True)  8.04 us
  transfers between devices with their start and end apart: 17, of which 9 were waited for; matrix products, arithmetic and copies ran while one was open for 1% of the time, Pallas kernels for 8%

profile of v4, /device:TPU:0, one launch (start us, length us, event | category | flops | bytes accessed | tf_op | source)
XLA Modules:
  0.0 272.0 jit_solution(14689100475946553426)
XLA Ops:
  6.5 1.2 constant_dynamic-slice_fusion.1
  7.7 0.1 pad_maximum_fusion.refs_0_
  7.8 0.0 copy-start.9
  7.8 0.1 copy-done
  7.9 0.8 constant_dynamic-slice_fusion
  8.8 0.0 all-gather.2.cloned.1.call-update
  8.8 4.2 %collective-permute-start.1 = (bf16[1024,256]{1,0:T(8,128)(2,1)S(1)}, bf16[1024,256]{1,0:T(8,128)(2,1)S(1)}, u32[]{:S(2)}, u32[]{:S(2)}) collective-permute-start(bf16[1024,256]{1,0:T(8,128)(2,1)S(1)} %pad_maximum_fusion.refs_0_), channel_id=1, source_target_pairs={{0,48},{1,49},{2,50},{3,51},{4,52},{5,53},{6,54},{7,55},{8,56},{9,... | collective-permute-start | bytes 1572872 | tf_op jit(solution)/shard_map/ppermute | solution.py:357
  13.0 0.0 collective-permute-start
  13.0 1.1 fusion
  14.1 1.3 collective-permute-start.10
  15.4 1.3 collective-permute-start.9
  16.7 0.1 collective-permute-start.4
  16.8 7.4 %collective-permute-done.1.refs_2_ = bf16[1024,256]{1,0:T(8,128)(2,1)S(1)} collective-permute-done((bf16[1024,256]{1,0:T(8,128)(2,1)S(1)}, bf16[1024,256]{1,0:T(8,128)(2,1)S(1)}, u32[]{:S(2)}, u32[]{:S(2)}) %collective-permute-start.1) | collective-permute-done | bytes 524320 | tf_op jit(solution)/shard_map/ppermute | solution.py:357
  24.2 3.8 %collective-permute-start.3 = (bf16[512,256]{1,0:T(8,128)(2,1)S(1)}, bf16[512,256]{1,0:T(8,128)(2,1)S(1)}, u32[]{:S(2)}, u32[]{:S(2)}) collective-permute-start(bf16[512,256]{1,0:T(8,128)(2,1)S(1)} %slice.17), channel_id=1, source_target_pairs={{0,48},{1,49},{2,50},{3,51},{4,52},{5,53},{6,54},{7,55},{8,56},{9,... | collective-permute-start | bytes 786440 | tf_op jit(solution)/shard_map/ppermute | solution.py:357
  28.0 0.0 collective-permute-done.refs_1_
  28.0 0.1 collective-permute-start.2
  28.1 0.0 collective-permute-done.10.refs_11_
  28.1 0.1 collective-permute-start.6
  28.2 0.0 collective-permute-done.9.refs_10_
  28.2 0.5 collective-permute-start.5
  28.7 4.0 %collective-permute-done.3.refs_4_ = bf16[512,256]{1,0:T(8,128)(2,1)S(1)} collective-permute-done((bf16[512,256]{1,0:T(8,128)(2,1)S(1)}, bf16[512,256]{1,0:T(8,128)(2,1)S(1)}, u32[]{:S(2)}, u32[]{:S(2)}) %collective-permute-start.3) | collective-permute-done | bytes 262176 | tf_op jit(solution)/shard_map/ppermute | solution.py:357
  32.7 0.0 collective-permute-start.8
  32.7 3.5 %collective-permute-done.2.refs_3_ = bf16[512,256]{1,0:T(8,128)(2,1)S(1)} collective-permute-done((bf16[512,256]{1,0:T(8,128)(2,1)S(1)}, bf16[512,256]{1,0:T(8,128)(2,1)S(1)}, u32[]{:S(2)}, u32[]{:S(2)}) %collective-permute-start.2) | collective-permute-done | bytes 262176 | tf_op jit(solution)/shard_map/ppermute | solution.py:357
  36.2 0.0 collective-permute-start.7
  36.2 0.0 collective-permute-done.4.refs_5_
  36.2 0.0 collective-permute-done.8.refs_9_
  36.2 0.0 collective-permute-done.6.refs_7_
  36.2 1.5 collective-permute-done.7.refs_8_
  37.7 0.0 collective-permute-done.5.refs_6_
  37.8 0.6 copy-done.24
  38.4 0.2 copy-done.18
  38.6 10.5 %attend_sent.1 = (bf16[512,384]{1,0:T(8,128)(2,1)}, bf16[512,384]{1,0:T(8,128)(2,1)}) custom-call(s32[1]{0:T(128)} %bitcast.meta_ref, s32[17]{0:T(128)} %lengths_ref.3, bf16[1024,256]{1,0:T(8,128)(2,1)} %copy-done.9, bf16[1024,256]{1,0:T(8,128)(2,1)} %copy-done.11, bf16[1024,256]{1,0:T(8,128)(2,1)} %copy-done.10, bf16[512,256]{1,0:T(8,128)(2,1)} %copy-done.22, ...), custom_call_target="tpu_custom_call" | custom-call | flops 17179869184 | bytes 8388608 | tf_op jit(solution)/shard_map/attend_sent/pallas_call | solution.py:165
  49.1 0.0 copy-start.13
  49.1 0.0 copy-start.14
  49.1 0.0 copy-start.15
  49.1 0.0 copy-start.6
  49.1 1.6 collective-permute-start.11
  50.8 1.3 collective-permute-start.12
  52.1 7.7 %attend_own.1 = (bf16[512,384]{1,0:T(8,128)(2,1)}, bf16[512,384]{1,0:T(8,128)(2,1)}) custom-call(s32[1]{0:T(128)} %bitcast.meta_ref, s32[17]{0:T(128)} %lengths_ref.3, bf16[1024,256]{1,0:T(8,128)(2,1)} %copy-done.9, bf16[1024,256]{1,0:T(8,128)(2,1)} %copy-done.11, bf16[1024,256]{1,0:T(8,128)(2,1)} %copy-done.10, bf16[512,256]{1,0:T(8,128)(2,1)} %copy-done.22, ...), custom_call_target="tpu_custom_call" | custom-call | flops 21474836480 | bytes 8388608 | tf_op jit(solution)/shard_map/attend_own/pallas_call | solution.py:165
  59.8 8.9 %collective-permute-done.11.refs_0_ = bf16[512,384]{1,0:T(8,128)(2,1)S(1)} collective-permute-done((bf16[512,384]{1,0:T(8,128)(2,1)}, bf16[512,384]{1,0:T(8,128)(2,1)S(1)}, u32[]{:S(2)}, u32[]{:S(2)}) %collective-permute-start.11) | collective-permute-done | bytes 393248 | tf_op jit(solution)/shard_map/ppermute | solution.py:357
  68.7 11.9 %collective-permute-done.12.refs_1_ = bf16[512,384]{1,0:T(8,128)(2,1)S(1)} collective-permute-done((bf16[512,384]{1,0:T(8,128)(2,1)}, bf16[512,384]{1,0:T(8,128)(2,1)S(1)}, u32[]{:S(2)}, u32[]{:S(2)}) %collective-permute-start.12) | collective-permute-done | bytes 393248 | tf_op jit(solution)/shard_map/ppermute | solution.py:357
  80.6 1.0 copy-done.7
  81.6 1.0 copy-done.8
  82.6 2.4 merge.1
  85.0 8.0 %all-gather.2.cloned.1.call-done.near_ref = bf16[1024,2048]{1,0:T(8,128)(2,1)} async-done(((bf16[128,2048]{1,0:T(8,128)(2,1)}), bf16[1024,2048]{1,0:T(8,128)(2,1)}) %all-gather.2.cloned.1.call-update) | async-done | bytes 4194320 | tf_op jit(solution)/shard_map/all_gather | solution.py:417
  93.0 3.7 %all-to-all-start = ((bf16[8,128,256]{2,1,0:T(8,128)(2,1)}), bf16[8,128,256]{2,1,0:T(8,128)(2,1)S(1)}, u32[]{:S(2)}, u32[]{:S(2)}) async-start(bf16[8,128,256]{2,1,0:T(8,128)(2,1)} %bitcast.1), calls=%async_computation | async-start | bytes 1048576 | tf_op jit(solution)/shard_map/all_to_all | solution.py:431
  96.8 0.7 copy.15.ids_ref
  97.5 0.7 copy.16.weights_ref
  98.2 2.1 slots.1
  100.3 0.9 reshape.27.place_ref
  101.2 7.8 %all-to-all-done.attended_ref = bf16[8,128,256]{2,1,0:T(8,128)(2,1)S(1)} async-done(((bf16[8,128,256]{2,1,0:T(8,128)(2,1)}), bf16[8,128,256]{2,1,0:T(8,128)(2,1)S(1)}, u32[]{:S(2)}, u32[]{:S(2)}) %all-to-all-start) | async-done | bytes 524320 | tf_op jit(solution)/shard_map/all_to_all | solution.py:431
  109.0 0.0 collective-permute-done.13.far_ref
  109.0 2.2 copy-done.2
  111.2 5.8 %pack.1 = (f32[128,16,128]{2,1,0:T(8,128)S(1)}, bf16[1152,16,128]{2,1,0:T(8,128)(2,1)S(1)}) custom-call(s32[1]{0:T(128)} %bitcast.meta_ref, s32[1024]{0:T(1024)S(1)} %reshape.27.place_ref, bf16[8,128,256]{2,1,0:T(8,128)(2,1)S(1)} %all-to-all-done.attended_ref, bf16[1024,2048]{1,0:T(8,128)(2,1)S(1)} %copy-done.2, ...), custom_call_target="tpu_custom_call" | custom-call | tf_op jit(solution)/shard_map/pack/pallas_call | solution.py:277
  117.0 0.0 copy-start.3
  117.0 0.0 copy-start.4
  117.0 0.0 copy-start.5
  117.1 64.0 %all_to_all.15 = bf16[128,9,16,128]{3,2,1,0:T(8,128)(2,1)} all-to-all(bf16[128,9,16,128]{3,2,1,0:T(8,128)(2,1)S(1)} %bitcast.7), channel_id=1, replica_groups=mesh['ctx'=16,'exp'=8] {'ctx','exp'}, dimensions={0} | all-to-all | bytes 9437184 | tf_op jit(solution)/shard_map/all_to_all | solution.py:445
  181.1 12.9 %experts.1 = bf16[1152,16,128]{2,1,0:T(8,128)(2,1)S(1)} custom-call(bf16[1152,16,128]{2,1,0:T(8,128)(2,1)} %bitcast.8, bf16[1,2048,768]{2,1,0:T(8,128)(2,1)S(1)} %copy-done.3, bf16[1,2048,768]{2,1,0:T(8,128)(2,1)S(1)} %copy-done.4, bf16[1,768,2048]{2,1,0:T(8,128)(2,1)S(1)} %copy-done.5), custom_call_target="tpu_custom_call" | custom-call | tf_op jit(solution)/shard_map/experts/pallas_call | solution.py:306
  194.0 2.2 copy-done.1
  196.2 5.9 %all-to-all-start.2 = ((bf16[128,9,16,128]{3,2,1,0:T(8,128)(2,1)}), bf16[128,9,16,128]{3,2,1,0:T(8,128)(2,1)}, u32[]{:S(2)}, u32[]{:S(2)}) async-start(bf16[128,9,16,128]{3,2,1,0:T(8,128)(2,1)} %bitcast.6), calls=%async_computation.2 | async-start | bytes 9437184 | tf_op jit(solution)/shard_map/all_to_all | solution.py:449
  202.1 0.1 reshape.28.shares_ref
  202.2 58.2 %all-to-all-done.2 = bf16[128,9,16,128]{3,2,1,0:T(8,128)(2,1)} async-done(((bf16[128,9,16,128]{3,2,1,0:T(8,128)(2,1)}), bf16[128,9,16,128]{3,2,1,0:T(8,128)(2,1)}, u32[]{:S(2)}, u32[]{:S(2)}) %all-to-all-start.2) | async-done | bytes 4718624 | tf_op jit(solution)/shard_map/all_to_all | solution.py:449
  260.4 4.8 %combine.1 = bf16[128,2048]{1,0:T(8,128)(2,1)} custom-call(s32[1024]{0:T(1024)S(1)} %reshape.27.place_ref, f32[1024]{0:T(1024)S(1)} %reshape.28.shares_ref, f32[128,16,128]{2,1,0:T(8,128)S(1)} %get-tuple-element.31.residual_ref, bf16[1152,16,128]{2,1,0:T(8,128)(2,1)} %bitcast.5.back_ref), custom_call_target="tpu_custom_call" | custom-call | tf_op jit(solution)/shard_map/combine/pallas_call | solution.py:335
  (40 shorter events, 0.1 us)
Async XLA Ops:
  6.5 1.4 copy-start
  6.5 86.5 %all-gather.2.cloned.1.call-start = ((), (), s32[]{:S(2)}) async-start(), calls=%async_computation.3 | async-start | bytes 4718592 | tf_op jit(solution)/shard_map/all_gather | solution.py:417
  7.8 29.9 %copy-start.9 = (bf16[1024,256]{1,0:T(8,128)(2,1)}, bf16[1024,256]{1,0:T(8,128)(2,1)S(1)}, u32[]{:S(2)}) copy-start(bf16[1024,256]{1,0:T(8,128)(2,1)S(1)} %pad_maximum_fusion.refs_0_) | copy-start | bytes 1572868
  8.8 15.4 %collective-permute-start.1 = (bf16[1024,256]{1,0:T(8,128)(2,1)S(1)}, bf16[1024,256]{1,0:T(8,128)(2,1)S(1)}, u32[]{:S(2)}, u32[]{:S(2)}) collective-permute-start(bf16[1024,256]{1,0:T(8,128)(2,1)S(1)} %pad_maximum_fusion.refs_0_), channel_id=1, source_target_pairs={{0,48},{1,49},{2,50},{3,51},{4,52},{5,53},{6,54},{7,55},{8,56},{9,... | collective-permute-start | bytes 1572872 | tf_op jit(solution)/shard_map/ppermute | solution.py:357
  13.0 15.0 %collective-permute-start = (bf16[1024,256]{1,0:T(8,128)(2,1)S(1)}, bf16[1024,256]{1,0:T(8,128)(2,1)S(1)}, u32[]{:S(2)}, u32[]{:S(2)}) collective-permute-start(bf16[1024,256]{1,0:T(8,128)(2,1)S(1)} %pad_maximum_fusion.refs_0_), channel_id=1, source_target_pairs={{0,16},{1,17},{2,18},{3,19},{4,20},{5,21},{6,22},{7,23},{8,24},{9,... | collective-permute-start | bytes 1572872 | tf_op jit(solution)/shard_map/ppermute | solution.py:357
  14.1 14.0 %collective-permute-start.10 = (bf16[512,256]{1,0:T(8,128)(2,1)S(1)}, bf16[512,256]{1,0:T(8,128)(2,1)S(1)}, u32[]{:S(2)}, u32[]{:S(2)}) collective-permute-start(bf16[512,256]{1,0:T(8,128)(2,1)S(1)} %get-tuple-element.33), channel_id=1, source_target_pairs={{64,1},{65,0},{66,3},{67,2},{68,5},{69,4},{70,7},{71,6},{72,9},{73... | collective-permute-start | bytes 786440 | tf_op jit(solution)/shard_map/ppermute | solution.py:357
  15.4 12.8 %collective-permute-start.9 = (bf16[512,256]{1,0:T(8,128)(2,1)S(1)}, bf16[512,256]{1,0:T(8,128)(2,1)S(1)}, u32[]{:S(2)}, u32[]{:S(2)}) collective-permute-start(bf16[512,256]{1,0:T(8,128)(2,1)S(1)} %get-tuple-element.34), channel_id=1, source_target_pairs={{64,0},{65,1},{66,2},{67,3},{68,4},{69,5},{70,6},{71,7},{72,8},{73... | collective-permute-start | bytes 786440 | tf_op jit(solution)/shard_map/ppermute | solution.py:357
  16.7 19.5 %collective-permute-start.4 = (bf16[1024,256]{1,0:T(8,128)(2,1)S(1)}, bf16[1024,256]{1,0:T(8,128)(2,1)S(1)}, u32[]{:S(2)}, u32[]{:S(2)}) collective-permute-start(bf16[1024,256]{1,0:T(8,128)(2,1)S(1)} %pad_maximum_fusion.refs_0_), channel_id=1, source_target_pairs={{0,8},{1,9},{2,10},{3,11},{4,12},{5,13},{6,14},{7,15},{8,0},{9,1},... | collective-permute-start | bytes 1572872 | tf_op jit(solution)/shard_map/ppermute | solution.py:357
  24.2 13.5 %copy-start.10 = (bf16[1024,256]{1,0:T(8,128)(2,1)}, bf16[1024,256]{1,0:T(8,128)(2,1)S(1)}, u32[]{:S(2)}) copy-start(bf16[1024,256]{1,0:T(8,128)(2,1)S(1)} %collective-permute-done.1.refs_2_) | copy-start | bytes 1572868
  24.2 8.5 %collective-permute-start.3 = (bf16[512,256]{1,0:T(8,128)(2,1)S(1)}, bf16[512,256]{1,0:T(8,128)(2,1)S(1)}, u32[]{:S(2)}, u32[]{:S(2)}) collective-permute-start(bf16[512,256]{1,0:T(8,128)(2,1)S(1)} %slice.17), channel_id=1, source_target_pairs={{0,48},{1,49},{2,50},{3,51},{4,52},{5,53},{6,54},{7,55},{8,56},{9,... | collective-permute-start | bytes 786440 | tf_op jit(solution)/shard_map/ppermute | solution.py:357
  28.0 9.8 %copy-start.11 = (bf16[1024,256]{1,0:T(8,128)(2,1)}, bf16[1024,256]{1,0:T(8,128)(2,1)S(1)}, u32[]{:S(2)}) copy-start(bf16[1024,256]{1,0:T(8,128)(2,1)S(1)} %collective-permute-done.refs_1_) | copy-start | bytes 1572868
  28.0 8.2 %collective-permute-start.2 = (bf16[512,256]{1,0:T(8,128)(2,1)S(1)}, bf16[512,256]{1,0:T(8,128)(2,1)S(1)}, u32[]{:S(2)}, u32[]{:S(2)}) collective-permute-start(bf16[512,256]{1,0:T(8,128)(2,1)S(1)} %slice.16), channel_id=1, source_target_pairs={{0,16},{1,17},{2,18},{3,19},{4,20},{5,21},{6,22},{7,23},{8,24},{9,... | collective-permute-start | bytes 786440 | tf_op jit(solution)/shard_map/ppermute | solution.py:357
  28.1 9.7 %copy-start.20 = (bf16[512,256]{1,0:T(8,128)(2,1)}, bf16[512,256]{1,0:T(8,128)(2,1)S(1)}, u32[]{:S(2)}) copy-start(bf16[512,256]{1,0:T(8,128)(2,1)S(1)} %collective-permute-done.10.refs_11_) | copy-start | bytes 786436
  28.1 8.1 %collective-permute-start.6 = (bf16[1024,256]{1,0:T(8,128)(2,1)S(1)}, bf16[1024,256]{1,0:T(8,128)(2,1)S(1)}, u32[]{:S(2)}, u32[]{:S(2)}) collective-permute-start(bf16[1024,256]{1,0:T(8,128)(2,1)S(1)} %collective-permute-done.1.refs_2_), channel_id=1, source_target_pairs={{0,8},{1,9},{2,10},{3,11},{4,12},{5,13},{6,14},{7,15},{8,0},{9,1},... | collective-permute-start | bytes 1572872 | tf_op jit(solution)/shard_map/ppermute | solution.py:357
  28.2 9.6 %copy-start.21 = (bf16[512,256]{1,0:T(8,128)(2,1)}, bf16[512,256]{1,0:T(8,128)(2,1)S(1)}, u32[]{:S(2)}) copy-start(bf16[512,256]{1,0:T(8,128)(2,1)S(1)} %collective-permute-done.9.refs_10_) | copy-start | bytes 786436
  28.2 9.5 %collective-permute-start.5 = (bf16[1024,256]{1,0:T(8,128)(2,1)S(1)}, bf16[1024,256]{1,0:T(8,128)(2,1)S(1)}, u32[]{:S(2)}, u32[]{:S(2)}) collective-permute-start(bf16[1024,256]{1,0:T(8,128)(2,1)S(1)} %collective-permute-done.refs_1_), channel_id=1, source_target_pairs={{0,8},{1,9},{2,10},{3,11},{4,12},{5,13},{6,14},{7,15},{8,0},{9,1},... | collective-permute-start | bytes 1572872 | tf_op jit(solution)/shard_map/ppermute | solution.py:357
  32.7 5.1 %copy-start.19 = (bf16[512,256]{1,0:T(8,128)(2,1)}, bf16[512,256]{1,0:T(8,128)(2,1)S(1)}, u32[]{:S(2)}) copy-start(bf16[512,256]{1,0:T(8,128)(2,1)S(1)} %collective-permute-done.3.refs_4_) | copy-start | bytes 786436
  32.7 3.5 %collective-permute-start.8 = (bf16[512,256]{1,0:T(8,128)(2,1)S(1)}, bf16[512,256]{1,0:T(8,128)(2,1)S(1)}, u32[]{:S(2)}, u32[]{:S(2)}) collective-permute-start(bf16[512,256]{1,0:T(8,128)(2,1)S(1)} %collective-permute-done.3.refs_4_), channel_id=1, source_target_pairs={{0,8},{1,9},{2,10},{3,11},{4,12},{5,13},{6,14},{7,15},{8,0},{9,1},... | collective-permute-start | bytes 786440 | tf_op jit(solution)/shard_map/ppermute | solution.py:357
  36.2 1.6 copy-start.22
  36.2 1.5 collective-permute-start.7
  36.2 1.6 copy-start.16
  36.2 1.6 copy-start.23
  36.2 1.6 copy-start.17
  37.7 0.7 copy-start.24
  37.7 0.9 copy-start.18
  49.1 47.7 %copy-start.13 = (bf16[2048]{0:T(1024)(128)(2,1)S(1)}, bf16[2048]{0:T(1024)(128)(2,1)}, u32[]{:S(2)}) copy-start(bf16[2048]{0:T(1024)(128)(2,1)} %param.17) | copy-start | bytes 12292
  49.1 47.7 %copy-start.14 = (s32[128,8]{0,1:T(8,128)S(1)}, s32[128,8]{0,1:T(8,128)}, u32[]{:S(2)}) copy-start(s32[128,8]{0,1:T(8,128)} %param.21) | copy-start | bytes 12292
  49.1 48.4 %copy-start.15 = (f32[128,8]{0,1:T(8,128)S(1)}, f32[128,8]{0,1:T(8,128)}, u32[]{:S(2)}) copy-start(f32[128,8]{0,1:T(8,128)} %param.22) | copy-start | bytes 12292
  49.1 59.9 %copy-start.6 = (bf16[128,2048]{1,0:T(8,128)(2,1)S(1)}, bf16[128,2048]{1,0:T(8,128)(2,1)}, u32[]{:S(2)}) copy-start(bf16[128,2048]{1,0:T(8,128)(2,1)} %stream_ref.1) | copy-start | bytes 1572868
  49.1 19.6 %collective-permute-start.11 = (bf16[512,384]{1,0:T(8,128)(2,1)}, bf16[512,384]{1,0:T(8,128)(2,1)S(1)}, u32[]{:S(2)}, u32[]{:S(2)}) collective-permute-start(bf16[512,384]{1,0:T(8,128)(2,1)} %get-tuple-element.25), channel_id=1, source_target_pairs={{0,64},{1,65},{2,66},{3,67},{4,68},{5,69},{6,70},{7,71},{8,72},{9,... | collective-permute-start | bytes 1179656 | tf_op jit(solution)/shard_map/ppermute | solution.py:357
  50.8 29.8 %collective-permute-start.12 = (bf16[512,384]{1,0:T(8,128)(2,1)}, bf16[512,384]{1,0:T(8,128)(2,1)S(1)}, u32[]{:S(2)}, u32[]{:S(2)}) collective-permute-start(bf16[512,384]{1,0:T(8,128)(2,1)} %get-tuple-element.26), channel_id=1, source_target_pairs={{0,65},{1,64},{2,67},{3,66},{4,69},{5,68},{6,71},{7,70},{8,73},{9,... | collective-permute-start | bytes 1179656 | tf_op jit(solution)/shard_map/ppermute | solution.py:357
  80.6 1.0 copy-start.7
  81.6 1.0 copy-start.8
  93.0 16.0 %collective-permute-start.13 = (bf16[1024,2048]{1,0:T(8,128)(2,1)}, bf16[1024,2048]{1,0:T(8,128)(2,1)}, u32[]{:S(2)}, u32[]{:S(2)}) collective-permute-start(bf16[1024,2048]{1,0:T(8,128)(2,1)} %all-gather.2.cloned.1.call-done.near_ref), channel_id=1, source_target_pairs={{0,8},{1,9},{2,10},{3,11},{4,12},{5,13},{6,14},{7,15},{8,0},{9,1},... | collective-permute-start | bytes 12582920 | tf_op jit(solution)/shard_map/ppermute | solution.py:357
  93.0 16.0 %all-to-all-start = ((bf16[8,128,256]{2,1,0:T(8,128)(2,1)}), bf16[8,128,256]{2,1,0:T(8,128)(2,1)S(1)}, u32[]{:S(2)}, u32[]{:S(2)}) async-start(bf16[8,128,256]{2,1,0:T(8,128)(2,1)} %bitcast.1), calls=%async_computation | async-start | bytes 1048576 | tf_op jit(solution)/shard_map/all_to_all | solution.py:431
  109.0 2.2 copy-start.2
  117.0 64.0 %copy-start.3 = (bf16[1,2048,768]{2,1,0:T(8,128)(2,1)S(1)}, bf16[1,2048,768]{2,1,0:T(8,128)(2,1)}, u32[]{:S(2)}) copy-start(bf16[1,2048,768]{2,1,0:T(8,128)(2,1)} %gate_ref.1) | copy-start | bytes 9437188
  117.0 64.0 %copy-start.4 = (bf16[1,2048,768]{2,1,0:T(8,128)(2,1)S(1)}, bf16[1,2048,768]{2,1,0:T(8,128)(2,1)}, u32[]{:S(2)}) copy-start(bf16[1,2048,768]{2,1,0:T(8,128)(2,1)} %up_ref.1) | copy-start | bytes 9437188
  117.0 64.0 %copy-start.5 = (bf16[1,768,2048]{2,1,0:T(8,128)(2,1)S(1)}, bf16[1,768,2048]{2,1,0:T(8,128)(2,1)}, u32[]{:S(2)}) copy-start(bf16[1,768,2048]{2,1,0:T(8,128)(2,1)} %down_ref.1) | copy-start | bytes 9437188
  194.0 2.2 copy-start.1
  196.2 5.9 %copy-start.12 = (f32[128,8]{1,0:T(8,128)S(1)}, f32[128,8]{1,0:T(8,128)}, u32[]{:S(2)}) copy-start(f32[128,8]{1,0:T(8,128)} %get-tuple-element.20) | copy-start | bytes 12292
  196.2 64.2 %all-to-all-start.2 = ((bf16[128,9,16,128]{3,2,1,0:T(8,128)(2,1)}), bf16[128,9,16,128]{3,2,1,0:T(8,128)(2,1)}, u32[]{:S(2)}, u32[]{:S(2)}) async-start(bf16[128,9,16,128]{3,2,1,0:T(8,128)(2,1)} %bitcast.6), calls=%async_computation.2 | async-start | bytes 9437184 | tf_op jit(solution)/shard_map/all_to_all | solution.py:449
Sparse Core Ops, SparseCore 0:
  9.7 83.2 all-gather.1

commit v5 on v4

--- a/solution.py
+++ b/solution.py
@@ -283,7 +283,7 @@
         in_specs=[SM, SM] + [VM] * 5,
         out_specs=(VM, VM),
         scratch_shapes=[pltpu.VMEM((rows, parts, LANES), jnp.bfloat16)],
-        compiler_params=pltpu.CompilerParams(vmem_limit_bytes=32 << 20),
+        compiler_params=pltpu.CompilerParams(vmem_limit_bytes=54 << 20),
         name="pack",
     )(meta, place, attended, near, far, stream, gain)
 

time: 273 us -> 277 us (1.015)
  waiting for transfers between devices: 111 us -> 82.1 us
  Pallas kernels: 46.2 us -> 69.3 us
  starting transfers between devices: 23.8 us -> 34.9 us
    ppermute x14, waiting for transfers between devices: 37.2 us -> 16.4 us  [permute(): return lax.ppermute(x, ('ctx', 'exp'), pairs)]
    pallas_call x2, Pallas kernels: 18.2 us -> 37.2 us  [attend(): pl.pallas_call(functools.partial(attend_part, final), out_shape=shapes, i...]
    ppermute x14, starting transfers between devices: 14.2 us -> 22.1 us  [permute(): return lax.ppermute(x, ('ctx', 'exp'), pairs)]
    all_gather x1, waiting for transfers between devices: 8.04 us -> 1.4 us  [on_device(): w_near = lax.all_gather(mine, 'exp', axis=0, tiled=True)]
    pallas_call x1, Pallas kernels: 5.81 us -> 9.93 us  [pack(): pl.pallas_call(pack_kernel, out_shape=(jax.ShapeDtypeStruct((rows, parts,...]
    all_to_all x1, starting transfers between devices: 3.72 us -> 6.94 us  [on_device(): lax.all_to_all(attended.reshape(exp_count, tok_rows, 2 * HD), 'exp', spli...]
    unnamed x52 -> x54, local copies, waits for them, and re-layouts: 8.81 us -> 7.4 us
  transfers between devices with their start and end apart: 17 -> 17, of which waited for: 9 -> 7; matrix products, arithmetic and copies ran while one was open for 1% -> 2% of each run, Pallas kernels for 8% -> 15%
where the time goes in v5:
time: 277 us; the launch traced here: 278 us
  waiting for transfers between devices  82.1 us (30%)
  Pallas kernels  69.3 us (25%)
  blocking collectives  64.6 us (23%)
  starting transfers between devices  34.9 us (13%)
  between operations  13.8 us (5%)
  local copies, waits for them, and re-layouts  12.7 us (5%)
    all_to_all x1, blocking collectives, on_device(): lax.all_to_all(outgoing.reshape(shape), ('ctx', 'exp'), split_axis=0, con...  64.6 us
    all_to_all x1, waiting for transfers between devices, on_device(): lax.all_to_all(results.reshape(shape), ('ctx', 'exp'), split_axis=0, conc...  58.2 us
    pallas_call x2, Pallas kernels, attend(): pl.pallas_call(functools.partial(attend_part, final), out_shape=shapes, i...  37.2 us
    ppermute x14, starting transfers between devices, permute(): return lax.ppermute(x, ('ctx', 'exp'), pairs)  22.1 us
    ppermute x14, waiting for transfers between devices, permute(): return lax.ppermute(x, ('ctx', 'exp'), pairs)  16.4 us
    pallas_call x1, Pallas kernels, experts(): pl.pallas_call(experts_kernel, out_shape=jax.ShapeDtypeStruct(x.shape, jn...  12.9 us
    pallas_call x1, Pallas kernels, pack(): pl.pallas_call(pack_kernel, out_shape=(jax.ShapeDtypeStruct((rows, parts,...  9.93 us
    unnamed x54, local copies, waits for them, and re-layouts  7.4 us
  transfers between devices with their start and end apart: 17, of which 7 were waited for; matrix products, arithmetic and copies ran while one was open for 2% of the time, Pallas kernels for 15%

profile of v5, /device:TPU:0, one launch (start us, length us, event | category | flops | bytes accessed | tf_op | source)
XLA Modules:
  0.0 277.5 jit_solution(12698767435865983461)
XLA Ops:
  6.5 0.0 all-gather.2.cloned.1.call-start
  6.5 1.2 constant_dynamic-slice_fusion.1
  7.7 0.1 pad_maximum_fusion.refs_0_
  7.8 0.0 copy-start.10
  7.8 0.1 copy-done
  7.9 0.8 constant_dynamic-slice_fusion
  8.8 0.0 all-gather.2.cloned.1.call-update
  8.8 4.2 %collective-permute-start.1 = (bf16[1024,256]{1,0:T(8,128)(2,1)S(1)}, bf16[1024,256]{1,0:T(8,128)(2,1)S(1)}, u32[]{:S(2)}, u32[]{:S(2)}) collective-permute-start(bf16[1024,256]{1,0:T(8,128)(2,1)S(1)} %pad_maximum_fusion.refs_0_), channel_id=1, source_target_pairs={{0,48},{1,49},{2,50},{3,51},{4,52},{5,53},{6,54},{7,55},{8,56},{9,... | collective-permute-start | bytes 1572872 | tf_op jit(solution)/shard_map/ppermute | solution.py:357
  13.0 0.0 collective-permute-start
  13.0 1.1 fusion
  14.1 1.3 collective-permute-start.10
  15.4 1.3 collective-permute-start.9
  16.7 0.1 collective-permute-start.4
  16.8 7.4 %collective-permute-done.1.refs_2_ = bf16[1024,256]{1,0:T(8,128)(2,1)S(1)} collective-permute-done((bf16[1024,256]{1,0:T(8,128)(2,1)S(1)}, bf16[1024,256]{1,0:T(8,128)(2,1)S(1)}, u32[]{:S(2)}, u32[]{:S(2)}) %collective-permute-start.1) | collective-permute-done | bytes 524320 | tf_op jit(solution)/shard_map/ppermute | solution.py:357
  24.2 3.8 %collective-permute-start.3 = (bf16[512,256]{1,0:T(8,128)(2,1)S(1)}, bf16[512,256]{1,0:T(8,128)(2,1)S(1)}, u32[]{:S(2)}, u32[]{:S(2)}) collective-permute-start(bf16[512,256]{1,0:T(8,128)(2,1)S(1)} %slice.17), channel_id=1, source_target_pairs={{0,48},{1,49},{2,50},{3,51},{4,52},{5,53},{6,54},{7,55},{8,56},{9,... | collective-permute-start | bytes 786440 | tf_op jit(solution)/shard_map/ppermute | solution.py:357
  28.0 0.0 collective-permute-done.refs_1_
  28.0 0.1 collective-permute-start.2
  28.1 0.0 collective-permute-done.10.refs_11_
  28.1 0.1 collective-permute-start.6
  28.2 0.0 collective-permute-done.9.refs_10_
  28.2 0.5 collective-permute-start.5
  28.7 4.0 %collective-permute-done.3.refs_4_ = bf16[512,256]{1,0:T(8,128)(2,1)S(1)} collective-permute-done((bf16[512,256]{1,0:T(8,128)(2,1)S(1)}, bf16[512,256]{1,0:T(8,128)(2,1)S(1)}, u32[]{:S(2)}, u32[]{:S(2)}) %collective-permute-start.3) | collective-permute-done | bytes 262176 | tf_op jit(solution)/shard_map/ppermute | solution.py:357
  32.7 0.0 collective-permute-start.8
  32.7 3.5 %collective-permute-done.2.refs_3_ = bf16[512,256]{1,0:T(8,128)(2,1)S(1)} collective-permute-done((bf16[512,256]{1,0:T(8,128)(2,1)S(1)}, bf16[512,256]{1,0:T(8,128)(2,1)S(1)}, u32[]{:S(2)}, u32[]{:S(2)}) %collective-permute-start.2) | collective-permute-done | bytes 262176 | tf_op jit(solution)/shard_map/ppermute | solution.py:357
  36.2 0.0 collective-permute-start.7
  36.2 0.0 collective-permute-done.4.refs_5_
  36.2 0.0 collective-permute-done.8.refs_9_
  36.2 0.0 copy-start.24
  36.2 0.0 collective-permute-done.6.refs_7_
  36.2 1.5 collective-permute-done.7.refs_8_
  37.7 0.0 collective-permute-done.5.refs_6_
  37.8 0.6 copy-done.25
  38.4 0.2 copy-done.19
  38.6 29.5 %attend_sent.1 = (bf16[512,384]{1,0:T(8,128)(2,1)}, bf16[512,384]{1,0:T(8,128)(2,1)}) custom-call(s32[1]{0:T(128)} %bitcast.meta_ref, s32[17]{0:T(128)} %lengths_ref.3, bf16[1024,256]{1,0:T(8,128)(2,1)} %copy-done.10, bf16[1024,256]{1,0:T(8,128)(2,1)} %copy-done.12, bf16[1024,256]{1,0:T(8,128)(2,1)} %copy-done.11, bf16[512,256]{1,0:T(8,128)(2,1)} %copy-done.23, ...), custom_call_target="tpu_custom_call" | custom-call | flops 17179869184 | bytes 8388608 | tf_op jit(solution)/shard_map/attend_sent/pallas_call | solution.py:165
  68.1 0.0 copy-start.14
  68.1 0.0 copy-start.15
  68.1 0.0 copy-start.16
  68.1 1.6 collective-permute-start.11
  69.8 1.3 collective-permute-start.12
  71.1 7.7 %attend_own.1 = (bf16[512,384]{1,0:T(8,128)(2,1)}, bf16[512,384]{1,0:T(8,128)(2,1)}) custom-call(s32[1]{0:T(128)} %bitcast.meta_ref, s32[17]{0:T(128)} %lengths_ref.3, bf16[1024,256]{1,0:T(8,128)(2,1)} %copy-done.10, bf16[1024,256]{1,0:T(8,128)(2,1)} %copy-done.12, bf16[1024,256]{1,0:T(8,128)(2,1)} %copy-done.11, bf16[512,256]{1,0:T(8,128)(2,1)} %copy-done.23, ...), custom_call_target="tpu_custom_call" | custom-call | flops 21474836480 | bytes 8388608 | tf_op jit(solution)/shard_map/attend_own/pallas_call | solution.py:165
  78.8 0.0 collective-permute-done.11.refs_0_
  78.8 0.0 collective-permute-done.12.refs_1_
  78.8 1.0 copy-done.6
  79.8 1.0 copy-done.7
  80.8 2.4 merge.1
  83.2 1.4 all-gather.2.cloned.1.call-done.near_ref
  84.6 7.8 %collective-permute-start.13 = (bf16[1024,2048]{1,0:T(8,128)(2,1)}, bf16[1024,2048]{1,0:T(8,128)(2,1)}, u32[]{:S(2)}, u32[]{:S(2)}) collective-permute-start(bf16[1024,2048]{1,0:T(8,128)(2,1)} %all-gather.2.cloned.1.call-done.near_ref), channel_id=1, source_target_pairs={{0,8},{1,9},{2,10},{3,11},{4,12},{5,13},{6,14},{7,15},{8,0},{9,1},... | collective-permute-start | bytes 12582920 | tf_op jit(solution)/shard_map/ppermute | solution.py:357
  92.4 6.9 %all-to-all-start = ((bf16[8,128,256]{2,1,0:T(8,128)(2,1)}), bf16[8,128,256]{2,1,0:T(8,128)(2,1)S(1)}, u32[]{:S(2)}, u32[]{:S(2)}) async-start(bf16[8,128,256]{2,1,0:T(8,128)(2,1)} %bitcast.1), calls=%async_computation | async-start | bytes 1048576 | tf_op jit(solution)/shard_map/all_to_all | solution.py:431
  99.4 0.6 reshape.31.gain_ref
  100.0 0.7 copy.15.ids_ref
  100.7 0.7 copy.16.weights_ref
  101.4 2.1 slots.1
  103.5 1.5 reshape.27.place_ref
  105.0 6.1 %all-to-all-done.attended_ref = bf16[8,128,256]{2,1,0:T(8,128)(2,1)S(1)} async-done(((bf16[8,128,256]{2,1,0:T(8,128)(2,1)}), bf16[8,128,256]{2,1,0:T(8,128)(2,1)S(1)}, u32[]{:S(2)}, u32[]{:S(2)}) %all-to-all-start) | async-done | bytes 524320 | tf_op jit(solution)/shard_map/all_to_all | solution.py:431
  111.1 0.0 collective-permute-done.13.far_ref
  111.1 0.8 copy-done.9
  111.9 9.9 %pack.1 = (f32[128,16,128]{2,1,0:T(8,128)}, bf16[1152,16,128]{2,1,0:T(8,128)(2,1)}) custom-call(s32[1]{0:T(128)} %bitcast.meta_ref, s32[1024]{0:T(1024)} %reshape.27.place_ref, bf16[8,128,256]{2,1,0:T(8,128)(2,1)} %copy-done.9, bf16[1024,2048]{1,0:T(8,128)(2,1)} %all-gather.2.cloned.1.call-done.near_ref, bf16[1024,2048]{1,0:T(8,128)(2,1)} %collective-permute-done.13.far_ref, ...), custom_call_target="tpu_custom_call" | custom-call | tf_op jit(solution)/shard_map/pack/pallas_call | solution.py:277
  121.9 64.6 %all_to_all.15 = bf16[128,9,16,128]{3,2,1,0:T(8,128)(2,1)} all-to-all(bf16[128,9,16,128]{3,2,1,0:T(8,128)(2,1)} %bitcast.8), channel_id=1, replica_groups=mesh['ctx'=16,'exp'=8] {'ctx','exp'}, dimensions={0} | all-to-all | bytes 9437184 | tf_op jit(solution)/shard_map/all_to_all | solution.py:445
  186.5 12.9 %experts.1 = bf16[1152,16,128]{2,1,0:T(8,128)(2,1)S(1)} custom-call(bf16[1152,16,128]{2,1,0:T(8,128)(2,1)} %bitcast.7, bf16[1,2048,768]{2,1,0:T(8,128)(2,1)S(1)} %copy-done.2, bf16[1,2048,768]{2,1,0:T(8,128)(2,1)S(1)} %copy-done.3, bf16[1,768,2048]{2,1,0:T(8,128)(2,1)S(1)} %copy-done.4), custom_call_target="tpu_custom_call" | custom-call | tf_op jit(solution)/shard_map/experts/pallas_call | solution.py:306
  199.5 2.2 copy-done.1
  201.6 5.9 %all-to-all-start.2 = ((bf16[128,9,16,128]{3,2,1,0:T(8,128)(2,1)}), bf16[128,9,16,128]{3,2,1,0:T(8,128)(2,1)}, u32[]{:S(2)}, u32[]{:S(2)}) async-start(bf16[128,9,16,128]{3,2,1,0:T(8,128)(2,1)} %bitcast.6), calls=%async_computation.2 | async-start | bytes 9437184 | tf_op jit(solution)/shard_map/all_to_all | solution.py:449
  207.6 0.1 reshape.28.shares_ref
  207.7 58.2 %all-to-all-done.2 = bf16[128,9,16,128]{3,2,1,0:T(8,128)(2,1)} async-done(((bf16[128,9,16,128]{3,2,1,0:T(8,128)(2,1)}), bf16[128,9,16,128]{3,2,1,0:T(8,128)(2,1)}, u32[]{:S(2)}, u32[]{:S(2)}) %all-to-all-start.2) | async-done | bytes 4718624 | tf_op jit(solution)/shard_map/all_to_all | solution.py:449
  265.9 4.8 %combine.1 = bf16[128,2048]{1,0:T(8,128)(2,1)} custom-call(s32[1024]{0:T(1024)S(1)} %copy-done.8, f32[1024]{0:T(1024)S(1)} %reshape.28.shares_ref, f32[128,16,128]{2,1,0:T(8,128)S(1)} %copy-done.5, bf16[1152,16,128]{2,1,0:T(8,128)(2,1)} %bitcast.5.back_ref), custom_call_target="tpu_custom_call" | custom-call | tf_op jit(solution)/shard_map/combine/pallas_call | solution.py:335
  (42 shorter events, 0.1 us)
Async XLA Ops:
  6.5 1.4 copy-start
  6.5 78.1 %all-gather.2.cloned.1.call-start = ((), (), s32[]{:S(2)}) async-start(), calls=%async_computation.3 | async-start | bytes 4718592 | tf_op jit(solution)/shard_map/all_gather | solution.py:417
  7.8 29.9 %copy-start.10 = (bf16[1024,256]{1,0:T(8,128)(2,1)}, bf16[1024,256]{1,0:T(8,128)(2,1)S(1)}, u32[]{:S(2)}) copy-start(bf16[1024,256]{1,0:T(8,128)(2,1)S(1)} %pad_maximum_fusion.refs_0_) | copy-start | bytes 1572868
  8.8 15.4 %collective-permute-start.1 = (bf16[1024,256]{1,0:T(8,128)(2,1)S(1)}, bf16[1024,256]{1,0:T(8,128)(2,1)S(1)}, u32[]{:S(2)}, u32[]{:S(2)}) collective-permute-start(bf16[1024,256]{1,0:T(8,128)(2,1)S(1)} %pad_maximum_fusion.refs_0_), channel_id=1, source_target_pairs={{0,48},{1,49},{2,50},{3,51},{4,52},{5,53},{6,54},{7,55},{8,56},{9,... | collective-permute-start | bytes 1572872 | tf_op jit(solution)/shard_map/ppermute | solution.py:357
  13.0 15.0 %collective-permute-start = (bf16[1024,256]{1,0:T(8,128)(2,1)S(1)}, bf16[1024,256]{1,0:T(8,128)(2,1)S(1)}, u32[]{:S(2)}, u32[]{:S(2)}) collective-permute-start(bf16[1024,256]{1,0:T(8,128)(2,1)S(1)} %pad_maximum_fusion.refs_0_), channel_id=1, source_target_pairs={{0,16},{1,17},{2,18},{3,19},{4,20},{5,21},{6,22},{7,23},{8,24},{9,... | collective-permute-start | bytes 1572872 | tf_op jit(solution)/shard_map/ppermute | solution.py:357
  14.1 14.0 %collective-permute-start.10 = (bf16[512,256]{1,0:T(8,128)(2,1)S(1)}, bf16[512,256]{1,0:T(8,128)(2,1)S(1)}, u32[]{:S(2)}, u32[]{:S(2)}) collective-permute-start(bf16[512,256]{1,0:T(8,128)(2,1)S(1)} %get-tuple-element.33), channel_id=1, source_target_pairs={{64,1},{65,0},{66,3},{67,2},{68,5},{69,4},{70,7},{71,6},{72,9},{73... | collective-permute-start | bytes 786440 | tf_op jit(solution)/shard_map/ppermute | solution.py:357
  15.4 12.8 %collective-permute-start.9 = (bf16[512,256]{1,0:T(8,128)(2,1)S(1)}, bf16[512,256]{1,0:T(8,128)(2,1)S(1)}, u32[]{:S(2)}, u32[]{:S(2)}) collective-permute-start(bf16[512,256]{1,0:T(8,128)(2,1)S(1)} %get-tuple-element.34), channel_id=1, source_target_pairs={{64,0},{65,1},{66,2},{67,3},{68,4},{69,5},{70,6},{71,7},{72,8},{73... | collective-permute-start | bytes 786440 | tf_op jit(solution)/shard_map/ppermute | solution.py:357
  16.7 19.5 %collective-permute-start.4 = (bf16[1024,256]{1,0:T(8,128)(2,1)S(1)}, bf16[1024,256]{1,0:T(8,128)(2,1)S(1)}, u32[]{:S(2)}, u32[]{:S(2)}) collective-permute-start(bf16[1024,256]{1,0:T(8,128)(2,1)S(1)} %pad_maximum_fusion.refs_0_), channel_id=1, source_target_pairs={{0,8},{1,9},{2,10},{3,11},{4,12},{5,13},{6,14},{7,15},{8,0},{9,1},... | collective-permute-start | bytes 1572872 | tf_op jit(solution)/shard_map/ppermute | solution.py:357
  24.2 13.5 %copy-start.11 = (bf16[1024,256]{1,0:T(8,128)(2,1)}, bf16[1024,256]{1,0:T(8,128)(2,1)S(1)}, u32[]{:S(2)}) copy-start(bf16[1024,256]{1,0:T(8,128)(2,1)S(1)} %collective-permute-done.1.refs_2_) | copy-start | bytes 1572868
  24.2 8.5 %collective-permute-start.3 = (bf16[512,256]{1,0:T(8,128)(2,1)S(1)}, bf16[512,256]{1,0:T(8,128)(2,1)S(1)}, u32[]{:S(2)}, u32[]{:S(2)}) collective-permute-start(bf16[512,256]{1,0:T(8,128)(2,1)S(1)} %slice.17), channel_id=1, source_target_pairs={{0,48},{1,49},{2,50},{3,51},{4,52},{5,53},{6,54},{7,55},{8,56},{9,... | collective-permute-start | bytes 786440 | tf_op jit(solution)/shard_map/ppermute | solution.py:357
  28.0 9.8 %copy-start.12 = (bf16[1024,256]{1,0:T(8,128)(2,1)}, bf16[1024,256]{1,0:T(8,128)(2,1)S(1)}, u32[]{:S(2)}) copy-start(bf16[1024,256]{1,0:T(8,128)(2,1)S(1)} %collective-permute-done.refs_1_) | copy-start | bytes 1572868
  28.0 8.2 %collective-permute-start.2 = (bf16[512,256]{1,0:T(8,128)(2,1)S(1)}, bf16[512,256]{1,0:T(8,128)(2,1)S(1)}, u32[]{:S(2)}, u32[]{:S(2)}) collective-permute-start(bf16[512,256]{1,0:T(8,128)(2,1)S(1)} %slice.16), channel_id=1, source_target_pairs={{0,16},{1,17},{2,18},{3,19},{4,20},{5,21},{6,22},{7,23},{8,24},{9,... | collective-permute-start | bytes 786440 | tf_op jit(solution)/shard_map/ppermute | solution.py:357
  28.1 9.7 %copy-start.21 = (bf16[512,256]{1,0:T(8,128)(2,1)}, bf16[512,256]{1,0:T(8,128)(2,1)S(1)}, u32[]{:S(2)}) copy-start(bf16[512,256]{1,0:T(8,128)(2,1)S(1)} %collective-permute-done.10.refs_11_) | copy-start | bytes 786436
  28.1 8.1 %collective-permute-start.6 = (bf16[1024,256]{1,0:T(8,128)(2,1)S(1)}, bf16[1024,256]{1,0:T(8,128)(2,1)S(1)}, u32[]{:S(2)}, u32[]{:S(2)}) collective-permute-start(bf16[1024,256]{1,0:T(8,128)(2,1)S(1)} %collective-permute-done.1.refs_2_), channel_id=1, source_target_pairs={{0,8},{1,9},{2,10},{3,11},{4,12},{5,13},{6,14},{7,15},{8,0},{9,1},... | collective-permute-start | bytes 1572872 | tf_op jit(solution)/shard_map/ppermute | solution.py:357
  28.2 9.6 %copy-start.22 = (bf16[512,256]{1,0:T(8,128)(2,1)}, bf16[512,256]{1,0:T(8,128)(2,1)S(1)}, u32[]{:S(2)}) copy-start(bf16[512,256]{1,0:T(8,128)(2,1)S(1)} %collective-permute-done.9.refs_10_) | copy-start | bytes 786436
  28.2 9.5 %collective-permute-start.5 = (bf16[1024,256]{1,0:T(8,128)(2,1)S(1)}, bf16[1024,256]{1,0:T(8,128)(2,1)S(1)}, u32[]{:S(2)}, u32[]{:S(2)}) collective-permute-start(bf16[1024,256]{1,0:T(8,128)(2,1)S(1)} %collective-permute-done.refs_1_), channel_id=1, source_target_pairs={{0,8},{1,9},{2,10},{3,11},{4,12},{5,13},{6,14},{7,15},{8,0},{9,1},... | collective-permute-start | bytes 1572872 | tf_op jit(solution)/shard_map/ppermute | solution.py:357
  32.7 5.1 %copy-start.20 = (bf16[512,256]{1,0:T(8,128)(2,1)}, bf16[512,256]{1,0:T(8,128)(2,1)S(1)}, u32[]{:S(2)}) copy-start(bf16[512,256]{1,0:T(8,128)(2,1)S(1)} %collective-permute-done.3.refs_4_) | copy-start | bytes 786436
  32.7 3.5 %collective-permute-start.8 = (bf16[512,256]{1,0:T(8,128)(2,1)S(1)}, bf16[512,256]{1,0:T(8,128)(2,1)S(1)}, u32[]{:S(2)}, u32[]{:S(2)}) collective-permute-start(bf16[512,256]{1,0:T(8,128)(2,1)S(1)} %collective-permute-done.3.refs_4_), channel_id=1, source_target_pairs={{0,8},{1,9},{2,10},{3,11},{4,12},{5,13},{6,14},{7,15},{8,0},{9,1},... | collective-permute-start | bytes 786440 | tf_op jit(solution)/shard_map/ppermute | solution.py:357
  36.2 1.6 copy-start.23
  36.2 1.5 collective-permute-start.7
  36.2 1.6 copy-start.17
  36.2 1.6 copy-start.24
  36.2 1.6 copy-start.18
  37.7 0.7 copy-start.25
  37.7 0.9 copy-start.19
  68.1 31.3 %copy-start.14 = (bf16[2048]{0:T(1024)(128)(2,1)S(1)}, bf16[2048]{0:T(1024)(128)(2,1)}, u32[]{:S(2)}) copy-start(bf16[2048]{0:T(1024)(128)(2,1)} %param.17) | copy-start | bytes 12292
  68.1 31.9 %copy-start.15 = (s32[128,8]{0,1:T(8,128)S(1)}, s32[128,8]{0,1:T(8,128)}, u32[]{:S(2)}) copy-start(s32[128,8]{0,1:T(8,128)} %param.21) | copy-start | bytes 12292
  68.1 32.6 %copy-start.16 = (f32[128,8]{0,1:T(8,128)S(1)}, f32[128,8]{0,1:T(8,128)}, u32[]{:S(2)}) copy-start(f32[128,8]{0,1:T(8,128)} %param.22) | copy-start | bytes 12292
  68.1 10.7 %collective-permute-start.11 = (bf16[512,384]{1,0:T(8,128)(2,1)}, bf16[512,384]{1,0:T(8,128)(2,1)S(1)}, u32[]{:S(2)}, u32[]{:S(2)}) collective-permute-start(bf16[512,384]{1,0:T(8,128)(2,1)} %get-tuple-element.25), channel_id=1, source_target_pairs={{0,64},{1,65},{2,66},{3,67},{4,68},{5,69},{6,70},{7,71},{8,72},{9,... | collective-permute-start | bytes 1179656 | tf_op jit(solution)/shard_map/ppermute | solution.py:357
  69.8 9.0 %collective-permute-start.12 = (bf16[512,384]{1,0:T(8,128)(2,1)}, bf16[512,384]{1,0:T(8,128)(2,1)S(1)}, u32[]{:S(2)}, u32[]{:S(2)}) collective-permute-start(bf16[512,384]{1,0:T(8,128)(2,1)} %get-tuple-element.26), channel_id=1, source_target_pairs={{0,65},{1,64},{2,67},{3,66},{4,69},{5,68},{6,71},{7,70},{8,73},{9,... | collective-permute-start | bytes 1179656 | tf_op jit(solution)/shard_map/ppermute | solution.py:357
  78.8 1.0 copy-start.6
  79.8 1.0 copy-start.7
  84.6 26.5 %collective-permute-start.13 = (bf16[1024,2048]{1,0:T(8,128)(2,1)}, bf16[1024,2048]{1,0:T(8,128)(2,1)}, u32[]{:S(2)}, u32[]{:S(2)}) collective-permute-start(bf16[1024,2048]{1,0:T(8,128)(2,1)} %all-gather.2.cloned.1.call-done.near_ref), channel_id=1, source_target_pairs={{0,8},{1,9},{2,10},{3,11},{4,12},{5,13},{6,14},{7,15},{8,0},{9,1},... | collective-permute-start | bytes 12582920 | tf_op jit(solution)/shard_map/ppermute | solution.py:357
  92.4 18.7 %all-to-all-start = ((bf16[8,128,256]{2,1,0:T(8,128)(2,1)}), bf16[8,128,256]{2,1,0:T(8,128)(2,1)S(1)}, u32[]{:S(2)}, u32[]{:S(2)}) async-start(bf16[8,128,256]{2,1,0:T(8,128)(2,1)} %bitcast.1), calls=%async_computation | async-start | bytes 1048576 | tf_op jit(solution)/shard_map/all_to_all | solution.py:431
  111.1 0.8 copy-start.9
  121.9 64.7 %copy-start.2 = (bf16[1,2048,768]{2,1,0:T(8,128)(2,1)S(1)}, bf16[1,2048,768]{2,1,0:T(8,128)(2,1)}, u32[]{:S(2)}) copy-start(bf16[1,2048,768]{2,1,0:T(8,128)(2,1)} %gate_ref.1) | copy-start | bytes 9437188
  121.9 64.7 %copy-start.3 = (bf16[1,2048,768]{2,1,0:T(8,128)(2,1)S(1)}, bf16[1,2048,768]{2,1,0:T(8,128)(2,1)}, u32[]{:S(2)}) copy-start(bf16[1,2048,768]{2,1,0:T(8,128)(2,1)} %up_ref.1) | copy-start | bytes 9437188
  121.9 64.7 %copy-start.4 = (bf16[1,768,2048]{2,1,0:T(8,128)(2,1)S(1)}, bf16[1,768,2048]{2,1,0:T(8,128)(2,1)}, u32[]{:S(2)}) copy-start(bf16[1,768,2048]{2,1,0:T(8,128)(2,1)} %down_ref.1) | copy-start | bytes 9437188
  199.5 2.2 copy-start.1
  201.6 5.9 %copy-start.13 = (f32[128,8]{1,0:T(8,128)S(1)}, f32[128,8]{1,0:T(8,128)}, u32[]{:S(2)}) copy-start(f32[128,8]{1,0:T(8,128)} %get-tuple-element.20) | copy-start | bytes 12292
  201.6 64.2 %copy-start.5 = (f32[128,16,128]{2,1,0:T(8,128)S(1)}, f32[128,16,128]{2,1,0:T(8,128)}, u32[]{:S(2)}) copy-start(f32[128,16,128]{2,1,0:T(8,128)} %get-tuple-element.31.residual_ref) | copy-start | bytes 3145732
  201.6 64.2 %copy-start.8 = (s32[1024]{0:T(1024)S(1)}, s32[1024]{0:T(1024)}, u32[]{:S(2)}) copy-start(s32[1024]{0:T(1024)} %reshape.27.place_ref) | copy-start | bytes 12292
  201.6 64.2 %all-to-all-start.2 = ((bf16[128,9,16,128]{3,2,1,0:T(8,128)(2,1)}), bf16[128,9,16,128]{3,2,1,0:T(8,128)(2,1)}, u32[]{:S(2)}, u32[]{:S(2)}) async-start(bf16[128,9,16,128]{3,2,1,0:T(8,128)(2,1)} %bitcast.6), calls=%async_computation.2 | async-start | bytes 9437184 | tf_op jit(solution)/shard_map/all_to_all | solution.py:449
Sparse Core Ops, SparseCore 0:
  9.7 74.8 all-gather.1
